TPU v7x, 32 devices: a whole 2x2x4 slice. The times are simulated.
32 devices in a mesh: dp: 16 (over z, y, x), tensor: 2 (over core).
Axes of the slice: x: 2, y: 2, z: 4, core: 2. Of those that a mesh axis runs over, the one named last changes fastest.
Arguments:
- hidden_in: bfloat16 [32768, 768], P('dp'), may hold values from -6 to 6
- grad_out: bfloat16 [32768, 768], P('dp'), may hold values from -6 to 6
- lengths: int32 [128], P('dp'), may hold values from 16 to 256, as said below
- key_mask: int32 [128, 256], P('dp'), may hold values 0 or 1
- triple_weight: bfloat16 [3, 768, 768], P(None, None, 'tensor'), may hold values from -0.21875 to 0.21875
- outward_weight: bfloat16 [768, 768], P('tensor'), may hold values from -1.25 to 1.25
- expand_weight: bfloat16 [768, 3072], P(None, 'tensor'), may hold values from -0.21875 to 0.21875
- contract_weight: bfloat16 [3072, 768], P('tensor'), may hold values from -0.109375 to 0.109375
- triple_master: float32 [3, 768, 768], P(None, 'dp', 'tensor'), may hold values from -0.21875 to 0.21875
- triple_first: float32 [3, 768, 768], P(None, 'dp', 'tensor'), may hold values from -512 to 512
- triple_second: float32 [3, 768, 768], P(None, 'dp', 'tensor'), may hold values from 8192 to 32768
- outward_master: float32 [768, 768], P('tensor', 'dp'), may hold values from -1.25 to 1.25
- outward_first: float32 [768, 768], P('tensor', 'dp'), may hold values from -160 to 160
- outward_second: float32 [768, 768], P('tensor', 'dp'), may hold values from 737.28 to 2949.12
- expand_master: float32 [768, 3072], P('dp', 'tensor'), may hold values from -0.21875 to 0.21875
- expand_first: float32 [768, 3072], P('dp', 'tensor'), may hold values from -256 to 256
- expand_second: float32 [768, 3072], P('dp', 'tensor'), may hold values from 2048 to 8192
- contract_master: float32 [3072, 768], P('tensor', 'dp'), may hold values from -0.109375 to 0.109375
- contract_first: float32 [3072, 768], P('tensor', 'dp'), may hold values from -512 to 512
- contract_second: float32 [3072, 768], P('tensor', 'dp'), may hold values from 8192 to 32768
- pair_bias: float32 [2, 768], P(None, 'tensor'), may hold values from -3 to 3
- pair_first: float32 [2, 768], P(None, 'tensor'), may hold values from -512 to 512
- pair_second: float32 [2, 768], P(None, 'tensor'), may hold values from 8192 to 32768
- expand_bias: float32 [3072], P('tensor'), may hold values from -3 to 3
- expand_bias_first: float32 [3072], P('tensor'), may hold values from -256 to 256
- expand_bias_second: float32 [3072], P('tensor'), may hold values from 2048 to 8192
- norm_vectors: float32 [6, 768], replicated, may hold values from -0.9 to 1.45
- vectors_first: float32 [6, 768], replicated, may hold values from -896 to 896
- vectors_second: float32 [6, 768], replicated, may hold values from 20971.52 to 83886.08
Outputs:
- layer_out: bfloat16 [32768, 768], P('dp')
- input_grad: float32 [32768, 768], P('dp')
- triple_master_new: float32 [3, 768, 768], P(None, 'dp', 'tensor')
- triple_first_new: float32 [3, 768, 768], P(None, 'dp', 'tensor')
- triple_second_new: float32 [3, 768, 768], P(None, 'dp', 'tensor')
- triple_copy: bfloat16 [3, 768, 768], P(None, None, 'tensor')
- outward_master_new: float32 [768, 768], P('tensor', 'dp')
- outward_first_new: float32 [768, 768], P('tensor', 'dp')
- outward_second_new: float32 [768, 768], P('tensor', 'dp')
- outward_copy: bfloat16 [768, 768], P('tensor')
- expand_master_new: float32 [768, 3072], P('dp', 'tensor')
- expand_first_new: float32 [768, 3072], P('dp', 'tensor')
- expand_second_new: float32 [768, 3072], P('dp', 'tensor')
- expand_copy: bfloat16 [768, 3072], P(None, 'tensor')
- contract_master_new: float32 [3072, 768], P('tensor', 'dp')
- contract_first_new: float32 [3072, 768], P('tensor', 'dp')
- contract_second_new: float32 [3072, 768], P('tensor', 'dp')
- contract_copy: bfloat16 [3072, 768], P('tensor')
- pair_bias_new: float32 [2, 768], P(None, 'tensor')
- pair_first_new: float32 [2, 768], P(None, 'tensor')
- pair_second_new: float32 [2, 768], P(None, 'tensor')
- expand_bias_new: float32 [3072], P('tensor')
- expand_bias_first_new: float32 [3072], P('tensor')
- expand_bias_second_new: float32 [3072], P('tensor')
- vectors_new: float32 [6, 768], replicated
- vectors_first_new: float32 [6, 768], replicated
- vectors_second_new: float32 [6, 768], replicated
Inputs may be any that keep to these rules, and one draw needn't show every extreme that they name: `lengths`: each sequence has at least 1 used slot, and some sequence of the batch uses all 256.
All inputs are finite; a program needn't handle non-finite values. No bound on the sum of `key_mask` on one device may be relied on, other than what follows from the above.
Results may differ from a plain program's by a relative error of at most 0.017.
The roundings to bfloat16 on the way count: a program that leaves them out, or rounds other values in their place, can miss the bound.
Values may be sent and summed in bfloat16 or wider, within the bound.
No kernel may reach another device: no remote copies, remote signals or barrier semaphores. Data moves between devices by JAX's collectives and lax.ppermute only.
A program may use at most 192 MiB of HBM per device.

v0:
```python
from functools import partial

import jax
import jax.numpy as jnp
from jax import lax
from jax.sharding import PartitionSpec as P

HEAD_DIM = 64
STEP = 7


MASK_FILL = -1e30
NORM_EPSILON = 1e-05
FIRST_DECAY = 0.5
SECOND_DECAY = 0.5
LEARN_RATE = 0.1
WEIGHT_DECAY = 0.01
EPSILON = 1e-08


def norm_rows(inputs):
    row_mean = jnp.mean(inputs, axis=-1, keepdims=True)
    centred = inputs - row_mean
    spread = jnp.mean(centred * centred, axis=-1, keepdims=True)
    inverse = lax.rsqrt(spread + NORM_EPSILON)
    return (centred * inverse, inverse[:, 0])


def norm_back(upstream, normed, inverse, gain_row):
    scaled = upstream * gain_row
    first_mean = jnp.mean(scaled, axis=-1, keepdims=True)
    cross_mean = jnp.mean(scaled * normed, axis=-1, keepdims=True)
    return inverse[:, None] * (scaled - first_mean - normed * cross_mean)


def adamw_step(master, first_moment, second_moment, gradient, decay_rate):
    first_new = FIRST_DECAY * first_moment + (1.0 - FIRST_DECAY) * gradient
    second_new = SECOND_DECAY * second_moment + (1.0 - SECOND_DECAY) * gradient * gradient
    first_fixed = first_new / (1.0 - FIRST_DECAY**STEP)
    second_fixed = second_new / (1.0 - SECOND_DECAY**STEP)
    direction = first_fixed / (jnp.sqrt(second_fixed) + EPSILON)
    master_new = master - LEARN_RATE * (direction + decay_rate * master)
    return (master_new, first_new, second_new)


def local(
    hidden_in,
    grad_out,
    lengths,
    key_mask,
    triple_weight,
    outward_weight,
    expand_weight,
    contract_weight,
    triple_master,
    triple_first,
    triple_second,
    outward_master,
    outward_first,
    outward_second,
    expand_master,
    expand_first,
    expand_second,
    contract_master,
    contract_first,
    contract_second,
    pair_bias,
    pair_first,
    pair_second,
    expand_bias,
    expand_bias_first,
    expand_bias_second,
    norm_vectors,
    vectors_first,
    vectors_second,
):
    seqs_here = lengths.shape[0]
    seq_len = key_mask.shape[1]
    tokens_here = hidden_in.shape[0]
    local_width = triple_weight.shape[2]
    local_heads = local_width // HEAD_DIM
    score_scale = HEAD_DIM ** (-0.5)
    split_shape = (seqs_here, seq_len, local_heads, HEAD_DIM)
    positions = lax.broadcasted_iota(jnp.int32, (seqs_here, seq_len), 1)
    valid_keys = (positions < lengths[:, None]) & ((key_mask == 1) | (positions == 0))
    key_valid = valid_keys[:, None, None, :]
    projected = jnp.einsum(
        "td,jdc->jtc", hidden_in, triple_weight, preferred_element_type=jnp.float32
    )
    offsets = jnp.stack([pair_bias[0], jnp.zeros_like(pair_bias[0]), pair_bias[1]])
    projected_low = (projected + offsets[:, None, :]).astype(jnp.bfloat16)
    queries = projected_low[0].reshape(split_shape)
    key_rows = projected_low[1].reshape(split_shape)
    values = projected_low[2].reshape(split_shape)
    scores = (
        jnp.einsum("sqhd,skhd->shqk", queries, key_rows, preferred_element_type=jnp.float32)
        * score_scale
    )
    masked = jnp.where(key_valid, scores, MASK_FILL)
    row_top = jnp.max(masked, axis=-1, keepdims=True)
    exp_terms = jnp.where(key_valid, jnp.exp(masked - row_top), 0.0)
    totals = jnp.sum(exp_terms, axis=-1, keepdims=True)
    log_total = row_top + jnp.log(totals)
    weights_low = (exp_terms / totals).astype(jnp.bfloat16)
    context = jnp.einsum("shqk,skhd->sqhd", weights_low, values, preferred_element_type=jnp.float32)
    context = context.astype(jnp.bfloat16).reshape(tokens_here, local_width)
    attn_part = jnp.dot(context, outward_weight, preferred_element_type=jnp.float32)
    residual_one = hidden_in.astype(jnp.float32) + norm_vectors[0]
    attn_total = lax.psum(attn_part.astype(jnp.bfloat16), "tensor").astype(jnp.float32)
    normed_one, inverse_one = norm_rows(residual_one + attn_total)
    hidden_one = normed_one * norm_vectors[2] + norm_vectors[3]
    hidden_low = hidden_one.astype(jnp.bfloat16)
    widened = jnp.dot(hidden_low, expand_weight, preferred_element_type=jnp.float32) + expand_bias
    active_low = jax.nn.gelu(widened, approximate=False).astype(jnp.bfloat16)
    ffn_part = jnp.dot(active_low, contract_weight, preferred_element_type=jnp.float32)
    residual_two = hidden_one + norm_vectors[1]
    ffn_total = lax.psum(ffn_part.astype(jnp.bfloat16), "tensor").astype(jnp.float32)
    normed_two, inverse_two = norm_rows(residual_two + ffn_total)
    layer_out = (normed_two * norm_vectors[4] + norm_vectors[5]).astype(jnp.bfloat16)
    upstream = grad_out.astype(jnp.float32)
    gain_two_grad = jnp.sum(upstream * normed_two, axis=0)
    shift_two_grad = jnp.sum(upstream, axis=0)
    pre_two_grad = norm_back(upstream, normed_two, inverse_two, norm_vectors[4])
    bias_two_grad = jnp.sum(pre_two_grad, axis=0)
    branch_grad = pre_two_grad.astype(jnp.bfloat16)
    contract_grad = jnp.einsum(
        "tf,td->fd", active_low, branch_grad, preferred_element_type=jnp.float32
    )
    active_grad = jnp.einsum(
        "td,fd->tf", branch_grad, contract_weight, preferred_element_type=jnp.float32
    )
    gelu_value, gelu_back = jax.vjp(partial(jax.nn.gelu, approximate=False), widened)
    widened_grad = gelu_back(active_grad)[0].astype(jnp.bfloat16)
    expand_bias_grad = jnp.sum(widened_grad, axis=0, dtype=jnp.float32)
    expand_grad = jnp.einsum(
        "td,tf->df", hidden_low, widened_grad, preferred_element_type=jnp.float32
    )
    hidden_part = jnp.einsum(
        "tf,df->td", widened_grad, expand_weight, preferred_element_type=jnp.float32
    )
    hidden_grad = pre_two_grad + lax.psum(hidden_part.astype(jnp.bfloat16), "tensor").astype(
        jnp.float32
    )
    gain_one_grad = jnp.sum(hidden_grad * normed_one, axis=0)
    shift_one_grad = jnp.sum(hidden_grad, axis=0)
    pre_one_grad = norm_back(hidden_grad, normed_one, inverse_one, norm_vectors[2])
    bias_one_grad = jnp.sum(pre_one_grad, axis=0)
    attention_grad = pre_one_grad.astype(jnp.bfloat16)
    outward_grad = jnp.einsum(
        "tc,td->cd", context, attention_grad, preferred_element_type=jnp.float32
    )
    context_grad = jnp.einsum(
        "td,cd->tc", attention_grad, outward_weight, preferred_element_type=jnp.float32
    )
    context_grad = context_grad.astype(jnp.bfloat16).reshape(split_shape)
    recomputed = (
        jnp.einsum("sqhd,skhd->shqk", queries, key_rows, preferred_element_type=jnp.float32)
        * score_scale
    )
    attention = jnp.where(key_valid, jnp.exp(recomputed - log_total), 0.0)
    attention_low = attention.astype(jnp.bfloat16)
    probs_grad = jnp.einsum(
        "sqhd,skhd->shqk", context_grad, values, preferred_element_type=jnp.float32
    )
    values_grad = jnp.einsum(
        "shqk,sqhd->skhd", attention_low, context_grad, preferred_element_type=jnp.float32
    )
    row_dot = jnp.sum(probs_grad * attention, axis=-1, keepdims=True)
    score_grad = (attention * (probs_grad - row_dot)).astype(jnp.bfloat16)
    queries_grad = (
        jnp.einsum("shqk,skhd->sqhd", score_grad, key_rows, preferred_element_type=jnp.float32)
        * score_scale
    )
    keys_grad = (
        jnp.einsum("shqk,sqhd->skhd", score_grad, queries, preferred_element_type=jnp.float32)
        * score_scale
    )
    projected_grad = (
        jnp.stack([queries_grad, keys_grad, values_grad])
        .reshape(3, tokens_here, local_width)
        .astype(jnp.bfloat16)
    )
    pair_grad = jnp.stack(
        [
            jnp.sum(projected_grad[0], axis=0, dtype=jnp.float32),
            jnp.sum(projected_grad[2], axis=0, dtype=jnp.float32),
        ]
    )
    triple_grad = jnp.einsum(
        "td,jtc->jdc", hidden_in, projected_grad, preferred_element_type=jnp.float32
    )
    input_part = jnp.einsum(
        "jtc,jdc->td", projected_grad, triple_weight, preferred_element_type=jnp.float32
    )
    input_grad = pre_one_grad + lax.psum(input_part.astype(jnp.bfloat16), "tensor").astype(
        jnp.float32
    )
    vector_grad = jnp.stack(
        [bias_one_grad, bias_two_grad, gain_one_grad, shift_one_grad, gain_two_grad, shift_two_grad]
    )
    triple_share, outward_share, expand_share, contract_share = (
        lax.psum_scatter(triple_grad, "dp", scatter_dimension=1, tiled=True),
        lax.psum_scatter(outward_grad, "dp", scatter_dimension=1, tiled=True),
        lax.psum_scatter(expand_grad, "dp", scatter_dimension=0, tiled=True),
        lax.psum_scatter(contract_grad, "dp", scatter_dimension=1, tiled=True),
    )
    pair_total, widen_total, vector_total = lax.psum(
        (pair_grad, expand_bias_grad, vector_grad), "dp"
    )
    triple_new = adamw_step(triple_master, triple_first, triple_second, triple_share, WEIGHT_DECAY)
    outward_new = adamw_step(
        outward_master, outward_first, outward_second, outward_share, WEIGHT_DECAY
    )
    expand_new = adamw_step(expand_master, expand_first, expand_second, expand_share, WEIGHT_DECAY)
    contract_new = adamw_step(
        contract_master, contract_first, contract_second, contract_share, WEIGHT_DECAY
    )
    pair_new = adamw_step(pair_bias, pair_first, pair_second, pair_total, 0.0)
    widen_new = adamw_step(expand_bias, expand_bias_first, expand_bias_second, widen_total, 0.0)
    vectors_new = adamw_step(norm_vectors, vectors_first, vectors_second, vector_total, 0.0)
    triple_copy, outward_copy, expand_copy, contract_copy = (
        lax.all_gather(triple_new[0].astype(jnp.bfloat16), "dp", axis=1, tiled=True),
        lax.all_gather(outward_new[0].astype(jnp.bfloat16), "dp", axis=1, tiled=True),
        lax.all_gather(expand_new[0].astype(jnp.bfloat16), "dp", axis=0, tiled=True),
        lax.all_gather(contract_new[0].astype(jnp.bfloat16), "dp", axis=1, tiled=True),
    )
    return (
        layer_out,
        input_grad,
        triple_new[0],
        triple_new[1],
        triple_new[2],
        triple_copy,
        outward_new[0],
        outward_new[1],
        outward_new[2],
        outward_copy,
        expand_new[0],
        expand_new[1],
        expand_new[2],
        expand_copy,
        contract_new[0],
        contract_new[1],
        contract_new[2],
        contract_copy,
        pair_new[0],
        pair_new[1],
        pair_new[2],
        widen_new[0],
        widen_new[1],
        widen_new[2],
        vectors_new[0],
        vectors_new[1],
        vectors_new[2],
    )


def solution(mesh):
    in_specs = (
        P("dp", None),
        P("dp", None),
        P("dp"),
        P("dp", None),
        P(None, None, "tensor"),
        P("tensor", None),
        P(None, "tensor"),
        P("tensor", None),
        P(None, "dp", "tensor"),
        P(None, "dp", "tensor"),
        P(None, "dp", "tensor"),
        P("tensor", "dp"),
        P("tensor", "dp"),
        P("tensor", "dp"),
        P("dp", "tensor"),
        P("dp", "tensor"),
        P("dp", "tensor"),
        P("tensor", "dp"),
        P("tensor", "dp"),
        P("tensor", "dp"),
        P(None, "tensor"),
        P(None, "tensor"),
        P(None, "tensor"),
        P("tensor"),
        P("tensor"),
        P("tensor"),
        P(),
        P(),
        P(),
    )
    out_specs = (
        P("dp", None),
        P("dp", None),
        P(None, "dp", "tensor"),
        P(None, "dp", "tensor"),
        P(None, "dp", "tensor"),
        P(None, None, "tensor"),
        P("tensor", "dp"),
        P("tensor", "dp"),
        P("tensor", "dp"),
        P("tensor", None),
        P("dp", "tensor"),
        P("dp", "tensor"),
        P("dp", "tensor"),
        P(None, "tensor"),
        P("tensor", "dp"),
        P("tensor", "dp"),
        P("tensor", "dp"),
        P("tensor", None),
        P(None, "tensor"),
        P(None, "tensor"),
        P(None, "tensor"),
        P("tensor"),
        P("tensor"),
        P("tensor"),
        P(),
        P(),
        P(),
    )
    return jax.shard_map(local, mesh=mesh, in_specs=in_specs, out_specs=out_specs, check_vma=False)
```

profile of v0, /device:TPU:0, one launch (start us, length us, event | category | flops | bytes accessed | tf_op | source)
XLA Modules:
  0.0 1131.6 jit_solution(4850098220106660398)
XLA Ops:
  8.3 6.7 fusion.24
  36.5 25.9 %all-reduce.8.cloned.1.call-done = bf16[2048,768]{1,0:T(8,128)(2,1)} async-done(((bf16[2048,768]{1,0:T(8,128)(2,1)}), bf16[2048,768]{1,0:T(8,128)(2,1)}) %all-reduce.8.cloned.1.call-update) | async-done | bytes 3145744 | tf_op jit(solution)/shard_map/psum | solution.py:109
  69.1 34.3 %multiply_convert_fusion.1 = (bf16[2048,1536]{1,0:T(8,128)(2,1)S(1)}, f32[2048,1536]{1,0:T(8,128)}, f32[2048,1536]{1,0:T(8,128)}) fusion(f32[1536]{0:T(1024)S(1)} %copy-done.29, bf16[768,1536]{1,0:T(8,128)(2,1)S(1)} %copy-done, f32[768]{0:T(1024)S(1)} %get-tuple-element.146, f32[768]{0:T(1024)S(1)} %get-tuple-element.147, f32[2048]{0:T(1024)S(1)} %add_rsqrt_fusion.1, ...), kind=kOutput, calls=%fused_computation.7 | convolution fusion | flops 5053612032 | bytes 40139776 | tf_op jit(solution)/shard_map/dot_general | solution.py:113
  112.4 24.5 %all-reduce.10.cloned.1.call-done = bf16[2048,768]{1,0:T(8,128)(2,1)} async-done(((bf16[2048,768]{1,0:T(8,128)(2,1)}), bf16[2048,768]{1,0:T(8,128)(2,1)}) %all-reduce.10.cloned.1.call-update) | async-done | bytes 3145744 | tf_op jit(solution)/shard_map/psum | solution.py:117
  152.4 20.4 %convert_reduce_fusion = (f32[1536]{0:T(1024)}, bf16[2048,1536]{1,0:T(8,128)(2,1)}) fusion(f32[2048,1536]{1,0:T(8,128)} %get-tuple-element.183, bf16[1536,768]{1,0:T(8,128)(2,1)} %param.36, f32[2048,768]{1,0:T(8,128)} %get-tuple-element.184, f32[2048,1536]{1,0:T(8,128)} %get-tuple-element.193, f32[1536]{0:T(1024)S(1)} %copy-done.29), kind=kOutput, calls=%fused_computation.2 | convolution fusion | flops 4886886912 | bytes 40120320 | tf_op jit(solution)/shard_map/td,fd->tf/dot_general | solution.py:129
  172.8 9.4 convolution_convert_fusion.1
  182.3 24.5 %all-reduce.12.cloned.1.call-done = bf16[2048,768]{1,0:T(8,128)(2,1)} async-done(((bf16[2048,768]{1,0:T(8,128)(2,1)}), bf16[2048,768]{1,0:T(8,128)(2,1)}) %all-reduce.12.cloned.1.call-update) | async-done | bytes 3145744 | tf_op jit(solution)/shard_map/psum | solution.py:141
  206.8 10.5 multiply_reduce_fusion.1
  239.8 10.4 multiply_reduce_fusion
  250.2 8.4 multiply_convert_fusion
  292.2 9.0 fusion.28
  307.5 10.6 fusion.38
  318.2 12.6 %fusion.57 = f32[768,1536]{1,0:T(8,128)} fusion(bf16[2048,1536]{1,0:T(8,128)(2,1)} %get-tuple-element.197, f32[768]{0:T(1024)S(1)} %get-tuple-element.146, f32[768]{0:T(1024)S(1)} %get-tuple-element.147, bf16[2048,768]{1,0:T(8,128)(2,1)} %all-reduce.8.cloned.1.call-done, bf16[2048,768]{1,0:T(8,128)(2,1)} %param.29, f32[2048]{0:T(1024)S(1)} %add_rsqrt_fusion.1, ...), kind=kOutput, calls=%fused_computation.96 | convolution fusion | flops 4845993984 | bytes 17327104 | tf_op jit(solution)/shard_map/td,tf->df/dot_general | solution.py:135
  337.4 9.0 bitcast_convert_fusion
  348.5 140.1 %all-reduce.16.cloned.1.call-done = f32[3,768,384]{2,0,1:T(4,128)} async-done(((f32[3,768,384]{2,0,1:T(4,128)}), f32[3,768,384]{2,0,1:T(4,128)}) %all-reduce.16.cloned.1.call-update) | async-done | bytes 3538960
  491.8 138.4 %reduce-scatter.8.cloned.1.call-done = f32[1536,48]{0,1:T(8,128)} async-done(((f32[1536,768]{0,1:T(8,128)}), f32[1536,48]{0,1:T(8,128)}) %reduce-scatter.8.cloned.1.call-update) | async-done | bytes 294928 | tf_op jit(solution)/shard_map/reduce_scatter | solution.py:205
  632.3 140.6 %reduce-scatter.6.cloned.1.call-done = f32[48,1536]{1,0:T(8,128)} async-done(((f32[768,1536]{1,0:T(8,128)}), f32[48,1536]{1,0:T(8,128)}) %reduce-scatter.6.cloned.1.call-update) | async-done | bytes 294928 | tf_op jit(solution)/shard_map/reduce_scatter | solution.py:204
  780.0 75.7 %all-reduce.1 = (f32[2,384]{1,0:T(2,128)S(1)}, f32[1536]{0:T(1024)S(1)}, f32[6,768]{1,0:T(8,128)S(1)}) all-reduce(f32[2,384]{1,0:T(2,128)S(1)} %pad_maximum_fusion.4, f32[1536]{0:T(1024)} %get-tuple-element.196, f32[6,768]{1,0:T(8,128)S(1)} %stack.59), channel_id=1, replica_groups=mesh['dp'=16,'tensor'=2] {'dp'}, use_global_device_ids=true, to_apply=%region_21.22 | all-reduce | flops 6912 | bytes 55296 | tf_op jit(solution)/shard_map/psum | solution.py:207
  859.9 41.4 %reduce-scatter.4.cloned.1.call-done = f32[384,48]{0,1:T(8,128)} async-done(((f32[384,768]{0,1:T(8,128)}), f32[384,48]{0,1:T(8,128)}) %reduce-scatter.4.cloned.1.call-update) | async-done | bytes 73744 | tf_op jit(solution)/shard_map/reduce_scatter | solution.py:203
  902.9 42.4 %all_gather.13 = bf16[384,768]{0,1:T(8,128)(2,1)S(1)} all-gather(bf16[384,48]{0,1:T(8,128)(2,1)S(1)} %get-tuple-element.172), channel_id=1, replica_groups=mesh['dp'=16,'tensor'=2] {'dp'}, dimensions={1}, use_global_device_ids=true | all-gather | bytes 626688 | tf_op jit(solution)/shard_map/all_gather | solution.py:223
  946.4 7.0 convert_add_fusion
  953.4 35.7 %all-gather.4.cloned.1.call-done = bf16[3,768,384]{2,1,0:T(8,128)(2,1)} async-done(((bf16[3,48,384]{2,1,0:T(8,128)(2,1)}), bf16[3,768,384]{2,1,0:T(8,128)(2,1)}) %all-gather.4.cloned.1.call-update) | async-done | bytes 1769488 | tf_op jit(solution)/shard_map/all_gather | solution.py:222
  989.1 64.7 %all-gather.8.cloned.1.call-done = bf16[1536,768]{0,1:T(8,128)(2,1)} async-done(((bf16[1536,48]{0,1:T(8,128)(2,1)}), bf16[1536,768]{0,1:T(8,128)(2,1)}) %all-gather.8.cloned.1.call-update) | async-done | bytes 2359312 | tf_op jit(solution)/shard_map/all_gather | solution.py:225
  1058.1 60.6 %all-gather.6.cloned.1.call-done = bf16[768,1536]{1,0:T(8,128)(2,1)} async-done(((bf16[48,1536]{1,0:T(8,128)(2,1)}), bf16[768,1536]{1,0:T(8,128)(2,1)}) %all-gather.6.cloned.1.call-update) | async-done | bytes 2359312 | tf_op jit(solution)/shard_map/all_gather | solution.py:224
  (172 shorter events, 153.2 us)
Async XLA Ops:
  7.2 61.9 %copy-start = (bf16[768,1536]{1,0:T(8,128)(2,1)S(1)}, bf16[768,1536]{1,0:T(8,128)(2,1)}, u32[]{:S(2)}) copy-start(bf16[768,1536]{1,0:T(8,128)(2,1)} %param.35) | copy-start | bytes 7077892
  7.2 55.2 %all-reduce.8.cloned.1.call-start = ((), (), s32[]{:S(2)}) async-start(), calls=%async_computation.3 | async-start | bytes 6291456 | tf_op jit(solution)/shard_map/psum | solution.py:109
  15.9 9.8 copy-start.13
  36.4 100.5 %all-reduce.10.cloned.1.call-start = ((), (), s32[]{:S(2)}) async-start(), calls=%async_computation.4 | async-start | bytes 6291456 | tf_op jit(solution)/shard_map/psum | solution.py:117
  69.1 36.9 %copy-start.32 = (bf16[1536,768]{1,0:T(8,128)(2,1)S(1)}, bf16[1536,768]{1,0:T(8,128)(2,1)}, u32[]{:S(2)}) copy-start(bf16[1536,768]{1,0:T(8,128)(2,1)} %param.36) | copy-start | bytes 7077892
  112.3 94.5 %all-reduce.12.cloned.1.call-start = ((), (), s32[]{:S(2)}) async-start(), calls=%async_computation.5 | async-start | bytes 6291456 | tf_op jit(solution)/shard_map/psum | solution.py:141
  182.2 306.3 %all-reduce.16.cloned.1.call-start = ((), (), s32[]{:S(2)}) async-start(), calls=%async_computation.13 | async-start | bytes 9437184
  206.8 10.5 copy-start.4
  206.8 10.5 copy-start.6
  206.8 10.5 copy-start.12
  233.7 16.5 %slice-start = ((s8[12582912]{0:T(1024)(128)(4,1)}), s8[4194304]{0:T(1024)(128)(4,1)S(1)}, s32[]{:S(2)}) async-start(s8[12582912]{0:T(1024)(128)(4,1)} %bitcast.79), calls=%async_computation.14 | async-start | bytes 8388608
  233.7 16.5 %slice-start.1 = ((s8[12582912]{0:T(1024)(128)(4,1)}), s8[4194304]{0:T(1024)(128)(4,1)S(1)}, s32[]{:S(2)}) async-start(s8[12582912]{0:T(1024)(128)(4,1)} %bitcast.79), calls=%async_computation.15 | async-start | bytes 8388608
  239.8 10.4 slice-start.2
  307.5 322.7 %reduce-scatter.8.cloned.1.call-start = ((), (), s32[]{:S(2)}) async-start(), calls=%async_computation.11 | async-start | bytes 5013504 | tf_op jit(solution)/shard_map/reduce_scatter | solution.py:205
  318.2 454.7 %reduce-scatter.6.cloned.1.call-start = ((), (), s32[]{:S(2)}) async-start(), calls=%async_computation.9 | async-start | bytes 5013504 | tf_op jit(solution)/shard_map/reduce_scatter | solution.py:204
  330.8 570.4 %reduce-scatter.4.cloned.1.call-start = ((), (), s32[]{:S(2)}) async-start(), calls=%async_computation.8 | async-start | bytes 1253376 | tf_op jit(solution)/shard_map/reduce_scatter | solution.py:203
  337.1 293.0 %copy-start.20 = (f32[1536,48]{0,1:T(8,128)S(1)}, f32[1536,48]{0,1:T(8,128)}, u32[]{:S(2)}) copy-start(f32[1536,48]{0,1:T(8,128)} %param.46) | copy-start | bytes 884740
  337.1 293.0 %copy-start.21 = (f32[1536,48]{0,1:T(8,128)S(1)}, f32[1536,48]{0,1:T(8,128)}, u32[]{:S(2)}) copy-start(f32[1536,48]{0,1:T(8,128)} %param.47) | copy-start | bytes 884740
  337.1 293.0 %copy-start.22 = (f32[1536,48]{0,1:T(8,128)S(1)}, f32[1536,48]{0,1:T(8,128)}, u32[]{:S(2)}) copy-start(f32[1536,48]{0,1:T(8,128)} %param.48) | copy-start | bytes 884740
  337.1 609.3 %all-reduce.14.cloned.1.call-start = ((), (), s32[]{:S(2)}) async-start(), calls=%async_computation.6 | async-start | bytes 6291456 | tf_op jit(solution)/shard_map/psum | solution.py:195
  346.4 426.4 %copy-start.23 = (f32[48,1536]{1,0:T(8,128)S(1)}, f32[48,1536]{1,0:T(8,128)}, u32[]{:S(2)}) copy-start(f32[48,1536]{1,0:T(8,128)} %param.43) | copy-start | bytes 884740
  346.5 642.6 %all-gather.4.cloned.1.call-start = ((), (), s32[]{:S(2)}) async-start(), calls=%async_computation.7 | async-start | bytes 1880064 | tf_op jit(solution)/shard_map/all_gather | solution.py:222
  491.7 562.1 %all-gather.8.cloned.1.call-start = ((), (), s32[]{:S(2)}) async-start(), calls=%async_computation.12 | async-start | bytes 2506752 | tf_op jit(solution)/shard_map/all_gather | solution.py:225
  632.2 486.5 %all-gather.6.cloned.1.call-start = ((), (), s32[]{:S(2)}) async-start(), calls=%async_computation.10 | async-start | bytes 2506752 | tf_op jit(solution)/shard_map/all_gather | solution.py:224
  (24 other events, 118.7 us)
Sparse Core Ops, SparseCore 0:
  36.5 25.9 all-reduce.7
  112.4 24.3 all-reduce.9
  182.4 24.3 all-reduce.11
  307.6 180.9 all-reduce.15
  493.6 136.5 reduce-scatter.7
  636.6 136.2 reduce-scatter.5
  777.6 123.5 reduce-scatter.3
  903.5 22.1 all-reduce.13
  928.8 60.2 all-gather.3
  992.7 61.0 all-gather.7
  1057.6 61.0 all-gather.5
where the time goes:
time: 1140 us; the launch traced here: 1130 us
  waiting for transfers between devices  697 us (61%)
  matrix products  161 us (14%)
  blocking collectives  118 us (10%)
  other arithmetic  72.8 us (6%)
  local copies, waits for them, and re-layouts  66.5 us (6%)
  between operations  15.4 us (1%)
    reduce_scatter x1, waiting for transfers between devices, local(): lax.psum_scatter(expand_grad, 'dp', scatter_dimension=0, tiled=True)  141 us
    unnamed x12, waiting for transfers between devices  140 us
    reduce_scatter x1, waiting for transfers between devices, local(): lax.psum_scatter(contract_grad, 'dp', scatter_dimension=1, tiled=True)  138 us
    psum x1, blocking collectives, local(): lax.psum((pair_grad, expand_bias_grad, vector_grad), 'dp')  75.7 us
    all_gather x1, waiting for transfers between devices, local(): lax.all_gather(contract_new[0].astype(jnp.bfloat16), 'dp', axis=1, tiled=...  64.7 us
    all_gather x1, waiting for transfers between devices, local(): lax.all_gather(expand_new[0].astype(jnp.bfloat16), 'dp', axis=0, tiled=True)  60.6 us
    all_gather x1, blocking collectives, local(): lax.all_gather(outward_new[0].astype(jnp.bfloat16), 'dp', axis=1, tiled=T...  42.4 us
    reduce_scatter x1, waiting for transfers between devices, local(): lax.psum_scatter(outward_grad, 'dp', scatter_dimension=1, tiled=True)  41.4 us
  transfers between devices with their start and end apart: 11, of which 10 were waited for; matrix products, arithmetic and copies ran while one was open for 6% of the time, Pallas kernels for 0%

commit v1 on v0

v1 whole, which is shorter than its diff:
```python
from functools import partial

import jax
import jax.numpy as jnp
from jax import lax
from jax.sharding import PartitionSpec as P

HEAD_DIM = 64
STEP = 7


MASK_FILL = -1e30
NORM_EPSILON = 1e-05
FIRST_DECAY = 0.5
SECOND_DECAY = 0.5
LEARN_RATE = 0.1
WEIGHT_DECAY = 0.01
EPSILON = 1e-08
LOW = jnp.bfloat16
WIDE = jnp.float32


def norm_rows(inputs):
    row_mean = jnp.mean(inputs, axis=-1, keepdims=True)
    centred = inputs - row_mean
    spread = jnp.mean(centred * centred, axis=-1, keepdims=True)
    inverse = lax.rsqrt(spread + NORM_EPSILON)
    return (centred * inverse, inverse[:, 0])


def norm_back(upstream, normed, inverse, gain_row):
    scaled = upstream * gain_row
    first_mean = jnp.mean(scaled, axis=-1, keepdims=True)
    cross_mean = jnp.mean(scaled * normed, axis=-1, keepdims=True)
    return inverse[:, None] * (scaled - first_mean - normed * cross_mean)


def adamw_step(master, first_moment, second_moment, gradient, decay_rate):
    first_new = FIRST_DECAY * first_moment + (1.0 - FIRST_DECAY) * gradient
    second_new = SECOND_DECAY * second_moment + (1.0 - SECOND_DECAY) * gradient * gradient
    first_fixed = first_new / (1.0 - FIRST_DECAY**STEP)
    second_fixed = second_new / (1.0 - SECOND_DECAY**STEP)
    direction = first_fixed / (jnp.sqrt(second_fixed) + EPSILON)
    master_new = master - LEARN_RATE * (direction + decay_rate * master)
    return (master_new, first_new, second_new)


def swap(value):
    return lax.ppermute(value, "tensor", [(0, 1), (1, 0)])


def across(value, bit, count):
    return lax.ppermute(value, "dp", [(i, i ^ (1 << bit)) for i in range(count)])


def bit_orders(count):
    bits = list(range(count.bit_length() - 1))
    return (bits, bits[1::-1] + bits[2:])


def scatter_rows(grad, order, rank, count):
    rows, width = grad.shape
    left = sorted(order, reverse=True)
    held = grad.reshape((2,) * len(left) + (rows // count, width))
    for bit in order:
        axis = left.index(bit)
        mine = (rank >> bit) & 1
        kept = lax.dynamic_index_in_dim(held, mine, axis, keepdims=False)
        sent = lax.dynamic_index_in_dim(held, 1 - mine, axis, keepdims=False)
        came = across(sent, bit, count)
        held = (kept.astype(WIDE) + came.astype(WIDE)).astype(LOW)
        left.remove(bit)
    return held


def gather_rows(shard, order, rank, count):
    rows, width = shard.shape
    have = []
    held = shard
    for bit in reversed(order):
        came = across(held, bit, count)
        have = sorted(have + [bit], reverse=True)
        axis = have.index(bit)
        low_side = ((rank >> bit) & 1) == 0
        held = jnp.stack(
            [jnp.where(low_side, held, came), jnp.where(low_side, came, held)], axis=axis
        )
    return held.reshape(count * rows, width)


def local(
    n_dp,
    hidden_in,
    grad_out,
    lengths,
    key_mask,
    triple_weight,
    outward_weight,
    expand_weight,
    contract_weight,
    triple_master,
    triple_first,
    triple_second,
    outward_master,
    outward_first,
    outward_second,
    expand_master,
    expand_first,
    expand_second,
    contract_master,
    contract_first,
    contract_second,
    pair_bias,
    pair_first,
    pair_second,
    expand_bias,
    expand_bias_first,
    expand_bias_second,
    norm_vectors,
    vectors_first,
    vectors_second,
):
    core = lax.axis_index("tensor")
    rank = lax.axis_index("dp")
    orders = bit_orders(n_dp)

    def own_half(value):
        size = value.shape[0] // 2
        return lax.dynamic_slice_in_dim(value, core * size, size, 0)

    def whole_tokens(value):
        other = swap(value)
        return jnp.where(
            core == 0, jnp.concatenate([value, other]), jnp.concatenate([other, value])
        )

    triple_all = jnp.concatenate([triple_weight, swap(triple_weight)], axis=2)
    outward_all = jnp.concatenate([outward_weight, swap(outward_weight)], axis=0)
    expand_all = jnp.concatenate([expand_weight, swap(expand_weight)], axis=1)
    contract_all = jnp.concatenate([contract_weight, swap(contract_weight)], axis=0)
    bias_bundle = jnp.concatenate([pair_bias[0], pair_bias[1], expand_bias])
    other_bundle = swap(bias_bundle)
    n_pair = pair_bias.shape[1]
    n_bias = expand_bias.shape[0]
    query_bias = jnp.concatenate([pair_bias[0], other_bundle[:n_pair]])
    value_bias = jnp.concatenate([pair_bias[1], other_bundle[n_pair : 2 * n_pair]])
    expand_bias_all = jnp.concatenate([expand_bias, other_bundle[2 * n_pair :]])

    hidden = own_half(hidden_in)
    upstream = own_half(grad_out).astype(WIDE)
    lengths = own_half(lengths)
    key_mask = own_half(key_mask)
    seqs_here = lengths.shape[0]
    seq_len = key_mask.shape[1]
    tokens_here = hidden.shape[0]
    width = triple_all.shape[2]
    heads = width // HEAD_DIM
    score_scale = HEAD_DIM ** (-0.5)
    split_shape = (seqs_here, seq_len, heads, HEAD_DIM)
    positions = lax.broadcasted_iota(jnp.int32, (seqs_here, seq_len), 1)
    valid_keys = (positions < lengths[:, None]) & ((key_mask == 1) | (positions == 0))
    key_valid = valid_keys[:, None, None, :]
    projected = jnp.einsum("td,jdc->jtc", hidden, triple_all, preferred_element_type=WIDE)
    offsets = jnp.stack([query_bias, jnp.zeros_like(query_bias), value_bias])
    projected_low = (projected + offsets[:, None, :]).astype(LOW)
    queries = projected_low[0].reshape(split_shape)
    key_rows = projected_low[1].reshape(split_shape)
    values = projected_low[2].reshape(split_shape)
    scores = (
        jnp.einsum("sqhd,skhd->shqk", queries, key_rows, preferred_element_type=WIDE) * score_scale
    )
    masked = jnp.where(key_valid, scores, MASK_FILL)
    row_top = jnp.max(masked, axis=-1, keepdims=True)
    exp_terms = jnp.where(key_valid, jnp.exp(masked - row_top), 0.0)
    totals = jnp.sum(exp_terms, axis=-1, keepdims=True)
    log_total = row_top + jnp.log(totals)
    weights_low = (exp_terms / totals).astype(LOW)
    context = jnp.einsum("shqk,skhd->sqhd", weights_low, values, preferred_element_type=WIDE)
    context = context.astype(LOW).reshape(tokens_here, width)
    attn_total = jnp.dot(context, outward_all, preferred_element_type=WIDE)
    residual_one = hidden.astype(WIDE) + norm_vectors[0]
    normed_one, inverse_one = norm_rows(residual_one + attn_total)
    hidden_one = normed_one * norm_vectors[2] + norm_vectors[3]
    hidden_low = hidden_one.astype(LOW)
    widened = jnp.dot(hidden_low, expand_all, preferred_element_type=WIDE) + expand_bias_all
    active_low = jax.nn.gelu(widened, approximate=False).astype(LOW)
    ffn_total = jnp.dot(active_low, contract_all, preferred_element_type=WIDE)
    residual_two = hidden_one + norm_vectors[1]
    normed_two, inverse_two = norm_rows(residual_two + ffn_total)
    layer_own = (normed_two * norm_vectors[4] + norm_vectors[5]).astype(LOW)
    layer_out = whole_tokens(layer_own)

    def to_owner(grad):
        half = grad.shape[1] // 2
        return (grad[:, :half] + swap(grad[:, half:].astype(LOW)).astype(WIDE)).astype(LOW)

    def to_shard(grad):
        half = grad.shape[1] // 2
        parts = [
            scatter_rows(grad[:, i * half : (i + 1) * half], orders[i], rank, n_dp)
            for i in range(2)
        ]
        return jnp.concatenate(parts, axis=1).astype(WIDE)

    def to_all(shard):
        half = shard.shape[1] // 2
        parts = [
            gather_rows(shard[:, i * half : (i + 1) * half], orders[i], rank, n_dp)
            for i in range(2)
        ]
        return jnp.concatenate(parts, axis=1)

    gain_two_grad = jnp.sum(upstream * normed_two, axis=0)
    shift_two_grad = jnp.sum(upstream, axis=0)
    pre_two_grad = norm_back(upstream, normed_two, inverse_two, norm_vectors[4])
    bias_two_grad = jnp.sum(pre_two_grad, axis=0)
    branch_grad = pre_two_grad.astype(LOW)
    contract_grad = jnp.einsum("td,tf->df", branch_grad, active_low, preferred_element_type=WIDE)
    contract_share = to_shard(to_owner(contract_grad))
    active_grad = jnp.einsum("td,fd->tf", branch_grad, contract_all, preferred_element_type=WIDE)
    _, gelu_back = jax.vjp(partial(jax.nn.gelu, approximate=False), widened)
    widened_grad = gelu_back(active_grad)[0].astype(LOW)
    expand_bias_grad = jnp.sum(widened_grad, axis=0, dtype=WIDE)
    expand_grad = jnp.einsum("td,tf->df", hidden_low, widened_grad, preferred_element_type=WIDE)
    expand_share = to_shard(to_owner(expand_grad))
    hidden_part = jnp.einsum("tf,df->td", widened_grad, expand_all, preferred_element_type=WIDE)
    hidden_grad = pre_two_grad + hidden_part
    gain_one_grad = jnp.sum(hidden_grad * normed_one, axis=0)
    shift_one_grad = jnp.sum(hidden_grad, axis=0)
    pre_one_grad = norm_back(hidden_grad, normed_one, inverse_one, norm_vectors[2])
    bias_one_grad = jnp.sum(pre_one_grad, axis=0)
    attention_grad = pre_one_grad.astype(LOW)
    outward_grad = jnp.einsum("td,tc->dc", attention_grad, context, preferred_element_type=WIDE)
    context_grad = jnp.einsum(
        "td,cd->tc", attention_grad, outward_all, preferred_element_type=WIDE
    )
    context_grad = context_grad.astype(LOW).reshape(split_shape)
    recomputed = (
        jnp.einsum("sqhd,skhd->shqk", queries, key_rows, preferred_element_type=WIDE) * score_scale
    )
    attention = jnp.where(key_valid, jnp.exp(recomputed - log_total), 0.0)
    attention_low = attention.astype(LOW)
    probs_grad = jnp.einsum("sqhd,skhd->shqk", context_grad, values, preferred_element_type=WIDE)
    values_grad = jnp.einsum(
        "shqk,sqhd->skhd", attention_low, context_grad, preferred_element_type=WIDE
    )
    row_dot = jnp.sum(probs_grad * attention, axis=-1, keepdims=True)
    score_grad = (attention * (probs_grad - row_dot)).astype(LOW)
    queries_grad = (
        jnp.einsum("shqk,skhd->sqhd", score_grad, key_rows, preferred_element_type=WIDE)
        * score_scale
    )
    keys_grad = (
        jnp.einsum("shqk,sqhd->skhd", score_grad, queries, preferred_element_type=WIDE)
        * score_scale
    )
    projected_grad = [
        g.astype(LOW).reshape(tokens_here, width) for g in (queries_grad, keys_grad, values_grad)
    ]
    pair_grad = jnp.stack(
        [
            jnp.sum(projected_grad[0], axis=0, dtype=WIDE),
            jnp.sum(projected_grad[2], axis=0, dtype=WIDE),
        ]
    )
    triple_grad = [
        jnp.einsum("td,tc->dc", hidden, g, preferred_element_type=WIDE) for g in projected_grad
    ]
    own = n_pair
    attn_grad = jnp.concatenate(
        [g[:, :own] for g in triple_grad]
        + [outward_grad[:, :own]]
        + [g[:, own:] for g in triple_grad]
        + [outward_grad[:, own:]],
        axis=1,
    )
    attn_share = to_shard(to_owner(attn_grad))
    input_part = sum(
        jnp.einsum("tc,dc->td", projected_grad[j], triple_all[j], preferred_element_type=WIDE)
        for j in range(3)
    )
    input_grad = whole_tokens((pre_one_grad + input_part).astype(LOW)).astype(WIDE)

    vector_grad = jnp.stack(
        [bias_one_grad, bias_two_grad, gain_one_grad, shift_one_grad, gain_two_grad, shift_two_grad]
    )
    own_side = jnp.concatenate([pair_grad[:, :own].reshape(-1), expand_bias_grad[:n_bias]])
    other_side = jnp.concatenate([pair_grad[:, own:].reshape(-1), expand_bias_grad[n_bias:]])
    vector_flat = vector_grad.reshape(-1)
    vector_sum = jnp.concatenate([vector_flat, own_side]) + swap(
        jnp.concatenate([vector_flat, other_side])
    )
    for bit in orders[0]:
        vector_sum = vector_sum + across(vector_sum, bit, n_dp)
    n_vec = vector_flat.shape[0]
    vector_total = vector_sum[:n_vec].reshape(norm_vectors.shape)
    pair_total = vector_sum[n_vec : n_vec + 2 * own].reshape(2, own)
    widen_total = vector_sum[n_vec + 2 * own :]

    contract_new = adamw_step(
        contract_master.T, contract_first.T, contract_second.T, contract_share, WEIGHT_DECAY
    )
    contract_copy = to_all(contract_new[0].astype(LOW)).T
    expand_new = adamw_step(expand_master, expand_first, expand_second, expand_share, WEIGHT_DECAY)
    expand_copy = to_all(expand_new[0].astype(LOW))
    triple_share = jnp.stack([attn_share[:, j * own : (j + 1) * own] for j in range(3)])
    triple_new = adamw_step(triple_master, triple_first, triple_second, triple_share, WEIGHT_DECAY)
    outward_new = adamw_step(
        outward_master.T, outward_first.T, outward_second.T, attn_share[:, 3 * own :], WEIGHT_DECAY
    )
    attn_copy = to_all(
        jnp.concatenate([triple_new[0][j] for j in range(3)] + [outward_new[0]], axis=1).astype(LOW)
    )
    triple_copy = jnp.stack([attn_copy[:, j * own : (j + 1) * own] for j in range(3)])
    outward_copy = attn_copy[:, 3 * own :].T
    pair_new = adamw_step(pair_bias, pair_first, pair_second, pair_total, 0.0)
    widen_new = adamw_step(expand_bias, expand_bias_first, expand_bias_second, widen_total, 0.0)
    vectors_new = adamw_step(norm_vectors, vectors_first, vectors_second, vector_total, 0.0)
    return (
        layer_out,
        input_grad,
        triple_new[0],
        triple_new[1],
        triple_new[2],
        triple_copy,
        outward_new[0].T,
        outward_new[1].T,
        outward_new[2].T,
        outward_copy,
        expand_new[0],
        expand_new[1],
        expand_new[2],
        expand_copy,
        contract_new[0].T,
        contract_new[1].T,
        contract_new[2].T,
        contract_copy,
        pair_new[0],
        pair_new[1],
        pair_new[2],
        widen_new[0],
        widen_new[1],
        widen_new[2],
        vectors_new[0],
        vectors_new[1],
        vectors_new[2],
    )


def solution(mesh):
    matrix_specs = (
        P(None, "dp", "tensor"),
        P("tensor", "dp"),
        P("dp", "tensor"),
        P("tensor", "dp"),
    )
    copy_specs = (P(None, None, "tensor"), P("tensor", None), P(None, "tensor"), P("tensor", None))
    vector_specs = (P(None, "tensor"),) * 3 + (P("tensor"),) * 3 + (P(),) * 3
    in_specs = (
        (P("dp", None), P("dp", None), P("dp"), P("dp", None))
        + copy_specs
        + tuple(spec for spec in matrix_specs for _ in range(3))
        + vector_specs
    )
    out_specs = (P("dp", None), P("dp", None))
    for spec, copied in zip(matrix_specs, copy_specs):
        out_specs += (spec,) * 3 + (copied,)
    out_specs += vector_specs
    return jax.shard_map(
        partial(local, mesh.shape["dp"]),
        mesh=mesh,
        in_specs=in_specs,
        out_specs=out_specs,
        check_vma=False,
    )
```

time: 1140 us -> 457 us (0.40)
  waiting for transfers between devices: 697 us -> 97 us
  blocking collectives: 118 us -> 0 us
  starting transfers between devices: 0.71 us -> 63 us
  matrix products: 161 us -> 143 us
  between operations: 15.4 us -> 3.11 us
  local copies, waits for them, and re-layouts: 66.5 us -> 78.6 us
    reduce_scatter x3 -> x0, waiting for transfers between devices: 320 us -> none  [the longest x1 141 us: local(): lax.psum_scatter(expand_grad, 'dp', scatter_dimension=0, tiled=True)]
    all_gather x3 -> x0, waiting for transfers between devices: 161 us -> none  [the longest x1 64.7 us: local(): lax.all_gather(contract_new[0].astype(jnp.bfloat16), 'dp', axis=1, tiled=...]
    unnamed x12 -> x0, waiting for transfers between devices: 140 us -> none
    ppermute x0 -> x63, waiting for transfers between devices: none -> 97 us  [the longest x52 97 us: across(): return lax.ppermute(value, 'dp', [(i, i ^ 1 << bit) for i in range(count)])]
    psum x1 -> x0, blocking collectives: 75.7 us -> none  [local(): lax.psum((pair_grad, expand_bias_grad, vector_grad), 'dp')]
    psum x4 -> x0, waiting for transfers between devices: 74.9 us -> none  [the longest x1 25.9 us: local(): lax.psum(attn_part.astype(jnp.bfloat16), 'tensor').astype(jnp.float32)]
    ppermute x0 -> x63, starting transfers between devices: none -> 63 us  [the longest x52 60.2 us: across(): return lax.ppermute(value, 'dp', [(i, i ^ 1 << bit) for i in range(count)])]
    all_gather x1 -> x0, blocking collectives: 42.4 us -> none  [local(): lax.all_gather(outward_new[0].astype(jnp.bfloat16), 'dp', axis=1, tiled=T...]
  transfers between devices with their start and end apart: 11 -> 63, of which waited for: 10 -> 29; matrix products, arithmetic and copies ran while one was open for 6% -> 37% of each run, Pallas kernels for 0% -> 0%
where the time goes in v1:
time: 457 us; the launch traced here: 450 us
  matrix products  143 us (31%)
  waiting for transfers between devices  97 us (21%)
  local copies, waits for them, and re-layouts  78.6 us (17%)
  other arithmetic  65.3 us (14%)
  starting transfers between devices  63 us (14%)
    ppermute x52, waiting for transfers between devices, across(): return lax.ppermute(value, 'dp', [(i, i ^ 1 << bit) for i in range(count)])  97 us
    ppermute x52, starting transfers between devices, across(): return lax.ppermute(value, 'dp', [(i, i ^ 1 << bit) for i in range(count)])  60.2 us
    dot_general x1, matrix products, local(): jnp.dot(hidden_low, expand_all, preferred_element_type=WIDE)  35.3 us
    unnamed x190, local copies, waits for them, and re-layouts  25.4 us
    dot_general x1, matrix products, local(): jnp.einsum('td,fd->tf', branch_grad, contract_all, preferred_element_type...  18.6 us
    dot_general x1, matrix products, local(): jnp.einsum('tf,df->td', widened_grad, expand_all, preferred_element_type=...  10.4 us
    dot_general x1, matrix products, local(): jnp.einsum('td,tf->df', branch_grad, active_low, preferred_element_type=W...  10.3 us
    dot_general x1, matrix products, local(): jnp.einsum('sqhd,skhd->shqk', context_grad, values, preferred_element_typ...  10.2 us
  transfers between devices with their start and end apart: 63, of which 29 were waited for; matrix products, arithmetic and copies ran while one was open for 37% of the time, Pallas kernels for 0%

profile of v1, /device:TPU:0, one launch (start us, length us, event | category | flops | bytes accessed | tf_op | source)
XLA Modules:
  0.0 449.7 jit_solution(5777933822931294159)
XLA Ops:
  20.8 6.1 %fusion.15 = bf16[3,1024,768]{1,2,0:T(8,128)(2,1)S(1)} fusion(f32[3,768]{1,0:T(4,128)S(1)} %pad_maximum_fusion.39, bf16[3,768,384]{1,2,0:T(8,128)(2,1)S(1)} %collective-permute-done, bf16[3,768,384]{1,2,0:T(8,128)(2,1)S(1)} %copy.86, bf16[2048,768]{1,0:T(8,128)(2,1)} %param.29, s32[]{:T(128)S(6)} %select_n.312), kind=kOutput, calls=%fused_computation.43 | convolution fusion | flops 3635675136 | bytes 9839620 | tf_op jit(solution)/shard_map/td,jdc->jtc/dot_general | solution.py:163
  38.7 4.1 fusion.6
  43.4 4.4 fusion.37
  55.4 35.3 %multiply_convert_fusion.1 = (bf16[1024,3072]{1,0:T(8,128)(2,1)S(1)}, f32[1024,3072]{1,0:T(8,128)}, f32[1024,3072]{1,0:T(8,128)}) fusion(f32[3072]{0:T(1024)S(1)} %copy-done.64, bf16[768,3072]{1,0:T(8,128)(2,1)S(1)} %constant_dynamic-update-slice_fusion.2, f32[1024,768]{1,0:T(8,128)S(1)} %get-tuple-element.217, f32[768]{0:T(1024)S(1)} %copy-done.57, ...), kind=kOutput, calls=%fused_computation.7 | convolution fusion | flops 5043388416 | bytes 39348224 | tf_op jit(solution)/shard_map/dot_general | solution.py:185
  90.9 3.6 constant_dynamic-update-slice_fusion.4
  94.5 5.5 %fusion.157 = (f32[1024]{0:T(1024)S(1)}, f32[1024,768]{1,0:T(8,128)S(1)}) fusion(bf16[1024,3072]{1,0:T(8,128)(2,1)S(1)} %get-tuple-element.122, bf16[3072,768]{1,0:T(8,128)(2,1)S(1)} %constant_dynamic-update-slice_fusion.4, f32[768]{0:T(1024)S(1)} %copy-done.68, f32[768]{0:T(1024)S(1)} %copy-done.57, f32[768]{0:T(1024)S(1)} %get-tuple-element.92, ...), kind=kOutput, calls=%fused_computation.413 | convolution fusion | flops 4837342208 | bytes 17323008 | tf_op jit(solution)/shard_map/dot_general | solution.py:187
  106.2 18.6 %convert_reduce_fusion = (f32[3072]{0:T(1024)S(1)}, bf16[1024,3072]{1,0:T(8,128)(2,1)}) fusion(f32[1024,3072]{1,0:T(8,128)} %get-tuple-element.123, bf16[3072,768]{1,0:T(8,128)(2,1)} %copy-done.34, f32[1024,768]{1,0:T(8,128)} %get-tuple-element.107, f32[1024,3072]{1,0:T(8,128)} %get-tuple-element.218, f32[3072]{0:T(1024)S(1)} %copy-done.64), kind=kOutput, calls=%fused_computation.2 | convolution fusion | flops 4886098944 | bytes 39346176 | tf_op jit(solution)/shard_map/td,fd->tf/dot_general | solution.py:220
  124.8 10.4 %multiply_reduce_fusion.1 = (f32[768]{0:T(1024)S(1)}, f32[1024]{0:T(1024)S(1)}, f32[1024]{0:T(1024)S(1)}, f32[768]{0:T(1024)S(1)}, f32[1024,768]{1,0:T(8,128)S(1)}) fusion(f32[1024,768]{1,0:T(8,128)S(1)} %get-tuple-element.217, f32[1024]{0:T(1024)S(1)} %add_rsqrt_fusion.1, f32[1024]{0:T(1024)S(1)} %broadcast_multiply_fusion.5, ...), kind=kOutput, calls=%fused_computation.65 | convolution fusion | flops 4839698432 | bytes 20472832 | tf_op jit(solution)/shard_map/tf,df->td/dot_general | solution.py:226
  135.3 8.4 %fusion.133 = f32[768,3072]{1,0:T(8,128)} fusion(bf16[1024,3072]{1,0:T(8,128)(2,1)S(1)} %copy-done.9, f32[1024,768]{1,0:T(8,128)S(1)} %get-tuple-element.217, f32[768]{0:T(1024)S(1)} %copy-done.57, f32[768]{0:T(1024)S(1)} %get-tuple-element.92, f32[1024]{0:T(1024)S(1)} %add_rsqrt_fusion.1, f32[1024]{0:T(1024)S(1)} %broadcast_multiply_fusion.5), kind=kOutput, calls=%fused_computation.398 | convolution fusion | flops 4835770368 | bytes 18888704 | tf_op jit(solution)/shard_map/td,tf->df/dot_general | solution.py:224
  143.7 10.3 %fusion.77 = f32[768,3072]{1,0:T(8,128)} fusion(bf16[1024,3072]{1,0:T(8,128)(2,1)} %copy-done.76, f32[1024,768]{1,0:T(8,128)S(1)} %copy-done.19), kind=kOutput, calls=%fused_computation.144 | convolution fusion | flops 4832624640 | bytes 18874368 | tf_op jit(solution)/shard_map/td,tf->df/dot_general | solution.py:218
  162.9 8.4 %convert_reduce_fusion.2 = (f32[12,64]{1,0:T(8,128)S(1)}, bf16[4,256,12,64]{1,3,2,0:T(8,128)(2,1)}) fusion(f32[4,12,256,256]{2,3,1,0:T(8,128)} %copy-done, f32[4,12,256]{2,1,0:T(8,128)S(1)} %copy-done.36, pred[4,256]{1,0:T(4,128)(4,1)S(1)} %copy-done.49, bf16[4,256,12,64]{1,0,3,2:T(4,128)(2,1)S(1)} %reshape.240), kind=kOutput, calls=%fused_computation.63 | convolution fusion | flops 417594624 | bytes 15781888 | tf_op jit(solution)/shard_map/shqk,sqhd->skhd/dot_general | solution.py:244
  171.3 10.2 %multiply_reduce_fusion = (f32[4,12,256]{2,1,0:T(8,128)S(1)}, f32[4,12,256,256]{2,3,1,0:T(8,128)}) fusion(f32[4,12,256,256]{2,3,1,0:T(8,128)} %copy-done, f32[4,12,256]{2,1,0:T(8,128)S(1)} %copy-done.36, pred[4,256]{1,0:T(4,128)(4,1)S(1)} %copy-done.49, bf16[4,256,12,64]{1,0,3,2:T(4,128)(2,1)S(1)} %copy-done.8, bf16[4,256,12,64]{1,0,3,2:T(4,128)(2,1)S(1)} %reshape.240), kind=kOutput, calls=%fused_computation.4 | convolution fusion | flops 418369536 | bytes 28410880 | tf_op jit(solution)/shard_map/sqhd,skhd->shqk/dot_general | solution.py:243
  181.6 8.4 %multiply_convert_fusion = bf16[4,12,256,256]{2,3,1,0:T(8,128)(2,1)S(1)} fusion(f32[4,12,256,256]{2,3,1,0:T(8,128)} %get-tuple-element.223, f32[4,12,256,256]{2,3,1,0:T(8,128)S(1)} %bitcast.395, f32[4,12,256]{2,1,0:T(8,128)S(1)} %get-tuple-element.222, f32[4,12,256]{2,1,0:T(8,128)S(1)} %copy-done.36, pred[4,256]{1,0:T(4,128)(4,1)S(1)} %copy-done.49), kind=kLoop, calls=%fused_computation.3 | loop fusion | flops 18874368 | bytes 31556608 | tf_op jit(solution)/shard_map/convert_element_type | solution.py:248
  198.9 4.0 slice.410
  236.3 4.1 slice.409
  242.8 3.6 maximum_select_fusion
  246.4 5.5 %fusion.27 = f32[2048,768]{1,0:T(8,128)} fusion(bf16[1024,768]{1,0:T(8,128)(2,1)} %collective-permute-done.6, bf16[1024,768]{1,0:T(8,128)(2,1)} %add_convert_fusion.2, pred[]{:T(512)S(6)} %eq.19), kind=kLoop, calls=%fused_computation.62 | loop fusion | flops 15728640 | bytes 9437185 | tf_op jit(solution)/shard_map/convert_element_type | solution.py:282
  281.0 7.5 %collective-permute-done.46 = bf16[2,2,2,48,768]{4,3,0,1,2:T(8,128)(2,1)} collective-permute-done((bf16[2,2,2,48,768]{4,3,0,1,2:T(8,128)(2,1)}, bf16[2,2,2,48,768]{4,3,0,1,2:T(8,128)(2,1)}, u32[]{:S(2)}, u32[]{:S(2)}) %collective-permute-start.46) | collective-permute-done | bytes 589856 | tf_op jit(solution)/shard_map/ppermute | solution.py:53
  293.6 9.1 %collective-permute-done.8 = bf16[2,2,2,48,768]{4,3,2,1,0:T(8,128)(2,1)} collective-permute-done((bf16[2,2,2,48,768]{4,3,2,1,0:T(8,128)(2,1)}, bf16[2,2,2,48,768]{4,3,2,1,0:T(8,128)(2,1)}, u32[]{:S(2)}, u32[]{:S(2)}) %collective-permute-start.8) | collective-permute-done | bytes 589856 | tf_op jit(solution)/shard_map/ppermute | solution.py:53
  311.8 3.4 collective-permute-done.47
  326.3 4.3 collective-permute-done.44
  391.9 4.4 collective-permute-done.56
  398.8 5.5 %collective-permute-done.23 = bf16[2,2,2,48,768]{4,3,0,1,2:T(8,128)(2,1)S(1)} collective-permute-done((bf16[2,2,2,48,768]{4,3,0,1,2:T(8,128)(2,1)S(1)}, bf16[2,2,2,48,768]{4,3,0,1,2:T(8,128)(2,1)S(1)}, u32[]{:S(2)}, u32[]{:S(2)}) %collective-permute-start.23) | collective-permute-done | bytes 589856 | tf_op jit(solution)/shard_map/ppermute | solution.py:53
  404.8 27.5 %collective-permute-done.19 = bf16[2,2,2,48,768]{4,3,0,1,2:T(8,128)(2,1)S(1)} collective-permute-done((bf16[2,2,2,48,768]{4,3,0,1,2:T(8,128)(2,1)S(1)}, bf16[2,2,2,48,768]{4,3,0,1,2:T(8,128)(2,1)S(1)}, u32[]{:S(2)}, u32[]{:S(2)}) %collective-permute-start.19) | collective-permute-done | bytes 589856 | tf_op jit(solution)/shard_map/ppermute | solution.py:53
  (536 shorter events, 234.0 us)
Async XLA Ops:
  6.5 46.6 %collective-permute-start.3 = (bf16[768,1536]{1,0:T(8,128)(2,1)}, bf16[768,1536]{1,0:T(8,128)(2,1)}, u32[]{:S(2)}, u32[]{:S(2)}) collective-permute-start(bf16[768,1536]{1,0:T(8,128)(2,1)} %param.35), channel_id=1, source_target_pairs={{0,1},{1,0},{2,3},{3,2},{4,5},{5,4},{6,7},{7,6},{8,9},{9,8},{10,11... | collective-permute-start | bytes 7077896 | tf_op jit(solution)/shard_map/ppermute | solution.py:49
  6.6 84.3 %collective-permute-start.4 = (bf16[1536,768]{1,0:T(8,128)(2,1)}, bf16[1536,768]{1,0:T(8,128)(2,1)}, u32[]{:S(2)}, u32[]{:S(2)}) collective-permute-start(bf16[1536,768]{1,0:T(8,128)(2,1)} %param.36), channel_id=1, source_target_pairs={{0,1},{1,0},{2,3},{3,2},{4,5},{5,4},{6,7},{7,6},{8,9},{9,8},{10,11... | collective-permute-start | bytes 7077896 | tf_op jit(solution)/shard_map/ppermute | solution.py:49
  198.8 44.1 %collective-permute-start.5 = (bf16[1024,768]{1,0:T(8,128)(2,1)S(1)}, bf16[1024,768]{1,0:T(8,128)(2,1)}, u32[]{:S(2)}, u32[]{:S(2)}) collective-permute-start(bf16[1024,768]{1,0:T(8,128)(2,1)S(1)} %get-tuple-element.127), channel_id=1, source_target_pairs={{0,1},{1,0},{2,3},{3,2},{4,5},{5,4},{6,7},{7,6},{8,9},{9,8},{10,11... | collective-permute-start | bytes 4718600 | tf_op jit(solution)/shard_map/ppermute | solution.py:49
  202.9 49.1 %collective-permute-start.24 = (bf16[768,1536]{1,0:T(8,128)(2,1)}, bf16[768,1536]{1,0:T(8,128)(2,1)}, u32[]{:S(2)}, u32[]{:S(2)}) collective-permute-start(bf16[768,1536]{1,0:T(8,128)(2,1)} %slice.410), channel_id=1, source_target_pairs={{0,1},{1,0},{2,3},{3,2},{4,5},{5,4},{6,7},{7,6},{8,9},{9,8},{10,11... | collective-permute-start | bytes 7077896 | tf_op jit(solution)/shard_map/ppermute | solution.py:49
  227.0 19.4 %collective-permute-start.6 = (bf16[1024,768]{1,0:T(8,128)(2,1)}, bf16[1024,768]{1,0:T(8,128)(2,1)}, u32[]{:S(2)}, u32[]{:S(2)}) collective-permute-start(bf16[1024,768]{1,0:T(8,128)(2,1)} %add_convert_fusion.2), channel_id=1, source_target_pairs={{0,1},{1,0},{2,3},{3,2},{4,5},{5,4},{6,7},{7,6},{8,9},{9,8},{10,11... | collective-permute-start | bytes 4718600 | tf_op jit(solution)/shard_map/ppermute | solution.py:49
  240.3 21.5 %collective-permute-start.41 = (bf16[768,1536]{1,0:T(8,128)(2,1)}, bf16[768,1536]{1,0:T(8,128)(2,1)}, u32[]{:S(2)}, u32[]{:S(2)}) collective-permute-start(bf16[768,1536]{1,0:T(8,128)(2,1)} %slice.409), channel_id=1, source_target_pairs={{0,1},{1,0},{2,3},{3,2},{4,5},{5,4},{6,7},{7,6},{8,9},{9,8},{10,11... | collective-permute-start | bytes 7077896 | tf_op jit(solution)/shard_map/ppermute | solution.py:49
  240.4 29.2 %collective-permute-start.7 = (bf16[768,1536]{0,1:T(8,128)(2,1)}, bf16[768,1536]{0,1:T(8,128)(2,1)}, u32[]{:S(2)}, u32[]{:S(2)}) collective-permute-start(bf16[768,1536]{0,1:T(8,128)(2,1)} %pad_maximum_fusion.2), channel_id=1, source_target_pairs={{0,1},{1,0},{2,3},{3,2},{4,5},{5,4},{6,7},{7,6},{8,9},{9,8},{10,11... | collective-permute-start | bytes 7077896 | tf_op jit(solution)/shard_map/ppermute | solution.py:49
  259.3 16.5 %collective-permute-start.29 = (bf16[2,2,2,48,768]{4,3,0,1,2:T(8,128)(2,1)}, bf16[2,2,2,48,768]{4,3,0,1,2:T(8,128)(2,1)}, u32[]{:S(2)}, u32[]{:S(2)}) collective-permute-start(bf16[2,2,2,48,768]{4,3,0,1,2:T(8,128)(2,1)} %bitcast.391), channel_id=1, source_target_pairs={{0,4},{2,6},{4,0},{6,2},{8,12},{10,14},{12,8},{14,10},{16,20},{18,... | collective-permute-start | bytes 1769480 | tf_op jit(solution)/shard_map/ppermute | solution.py:53
  260.8 17.8 %collective-permute-start.25 = (bf16[2,2,2,48,768]{4,3,0,1,2:T(8,128)(2,1)}, bf16[2,2,2,48,768]{4,3,0,1,2:T(8,128)(2,1)}, u32[]{:S(2)}, u32[]{:S(2)}) collective-permute-start(bf16[2,2,2,48,768]{4,3,0,1,2:T(8,128)(2,1)} %bitcast.392), channel_id=1, source_target_pairs={{0,2},{2,0},{4,6},{6,4},{8,10},{10,8},{12,14},{14,12},{16,18},{18,... | collective-permute-start | bytes 1769480 | tf_op jit(solution)/shard_map/ppermute | solution.py:53
  268.1 20.4 %collective-permute-start.46 = (bf16[2,2,2,48,768]{4,3,0,1,2:T(8,128)(2,1)}, bf16[2,2,2,48,768]{4,3,0,1,2:T(8,128)(2,1)}, u32[]{:S(2)}, u32[]{:S(2)}) collective-permute-start(bf16[2,2,2,48,768]{4,3,0,1,2:T(8,128)(2,1)} %bitcast.389), channel_id=1, source_target_pairs={{0,4},{2,6},{4,0},{6,2},{8,12},{10,14},{12,8},{14,10},{16,20},{18,... | collective-permute-start | bytes 1769480 | tf_op jit(solution)/shard_map/ppermute | solution.py:53
  268.6 22.6 %collective-permute-start.42 = (bf16[2,2,2,48,768]{4,3,0,1,2:T(8,128)(2,1)}, bf16[2,2,2,48,768]{4,3,0,1,2:T(8,128)(2,1)}, u32[]{:S(2)}, u32[]{:S(2)}) collective-permute-start(bf16[2,2,2,48,768]{4,3,0,1,2:T(8,128)(2,1)} %bitcast.390), channel_id=1, source_target_pairs={{0,2},{2,0},{4,6},{6,4},{8,10},{10,8},{12,14},{14,12},{16,18},{18,... | collective-permute-start | bytes 1769480 | tf_op jit(solution)/shard_map/ppermute | solution.py:53
  273.3 29.3 %collective-permute-start.8 = (bf16[2,2,2,48,768]{4,3,2,1,0:T(8,128)(2,1)}, bf16[2,2,2,48,768]{4,3,2,1,0:T(8,128)(2,1)}, u32[]{:S(2)}, u32[]{:S(2)}) collective-permute-start(bf16[2,2,2,48,768]{4,3,2,1,0:T(8,128)(2,1)} %dynamic-slice_bitcast_fusion), channel_id=1, source_target_pairs={{0,2},{2,0},{4,6},{6,4},{8,10},{10,8},{12,14},{14,12},{16,18},{18,... | collective-permute-start | bytes 1769480 | tf_op jit(solution)/shard_map/ppermute | solution.py:53
  275.8 28.6 %collective-permute-start.12 = (bf16[2,2,2,48,768]{4,3,0,1,2:T(8,128)(2,1)S(1)}, bf16[2,2,2,48,768]{4,3,0,1,2:T(8,128)(2,1)S(1)}, u32[]{:S(2)}, u32[]{:S(2)}) collective-permute-start(bf16[2,2,2,48,768]{4,3,0,1,2:T(8,128)(2,1)S(1)} %bitcast.429), channel_id=1, source_target_pairs={{0,4},{2,6},{4,0},{6,2},{8,12},{10,14},{12,8},{14,10},{16,20},{18,... | collective-permute-start | bytes 1769480 | tf_op jit(solution)/shard_map/ppermute | solution.py:53
  278.6 30.2 %collective-permute-start.30 = (bf16[2,2,48,768]{3,2,0,1:T(8,128)(2,1)S(1)}, bf16[2,2,48,768]{3,2,0,1:T(8,128)(2,1)S(1)}, u32[]{:S(2)}, u32[]{:S(2)}) collective-permute-start(bf16[2,2,48,768]{3,2,0,1:T(8,128)(2,1)S(1)} %dynamic-slice_bitcast_fusion.3), channel_id=1, source_target_pairs={{0,2},{2,0},{4,6},{6,4},{8,10},{10,8},{12,14},{14,12},{16,18},{18,... | collective-permute-start | bytes 884744 | tf_op jit(solution)/shard_map/ppermute | solution.py:53
  288.4 21.6 %collective-permute-start.26 = (bf16[2,2,48,768]{3,2,0,1:T(8,128)(2,1)S(1)}, bf16[2,2,48,768]{3,2,0,1:T(8,128)(2,1)S(1)}, u32[]{:S(2)}, u32[]{:S(2)}) collective-permute-start(bf16[2,2,48,768]{3,2,0,1:T(8,128)(2,1)S(1)} %dynamic-slice_bitcast_fusion.4), channel_id=1, source_target_pairs={{0,4},{2,6},{4,0},{6,2},{8,12},{10,14},{12,8},{14,10},{16,20},{18,... | collective-permute-start | bytes 884744 | tf_op jit(solution)/shard_map/ppermute | solution.py:53
  291.2 24.0 %collective-permute-start.47 = (bf16[2,2,48,768]{3,2,0,1:T(8,128)(2,1)S(1)}, bf16[2,2,48,768]{3,2,0,1:T(8,128)(2,1)S(1)}, u32[]{:S(2)}, u32[]{:S(2)}) collective-permute-start(bf16[2,2,48,768]{3,2,0,1:T(8,128)(2,1)S(1)} %dynamic-slice_bitcast_fusion.1), channel_id=1, source_target_pairs={{0,2},{2,0},{4,6},{6,4},{8,10},{10,8},{12,14},{14,12},{16,18},{18,... | collective-permute-start | bytes 884744 | tf_op jit(solution)/shard_map/ppermute | solution.py:53
  323.5 15.2 %collective-permute-start.28 = (bf16[48,768]{1,0:T(8,128)(2,1)S(1)}, bf16[48,768]{1,0:T(8,128)(2,1)S(1)}, u32[]{:S(2)}, u32[]{:S(2)}) collective-permute-start(bf16[48,768]{1,0:T(8,128)(2,1)S(1)} %dynamic-slice_bitcast_fusion.16), channel_id=1, source_target_pairs={{0,16},{2,18},{4,20},{6,22},{8,24},{10,26},{12,28},{14,30},{16,0},... | collective-permute-start | bytes 221192 | tf_op jit(solution)/shard_map/ppermute | solution.py:53
  381.1 15.2 %collective-permute-start.56 = (bf16[2,2,48,768]{3,2,0,1:T(8,128)(2,1)S(1)}, bf16[2,2,48,768]{3,2,0,1:T(8,128)(2,1)S(1)}, u32[]{:S(2)}, u32[]{:S(2)}) collective-permute-start(bf16[2,2,48,768]{3,2,0,1:T(8,128)(2,1)S(1)} %pad_maximum_fusion.24), channel_id=1, source_target_pairs={{0,2},{2,0},{4,6},{6,4},{8,10},{10,8},{12,14},{14,12},{16,18},{18,... | collective-permute-start | bytes 884744 | tf_op jit(solution)/shard_map/ppermute | solution.py:53
  384.5 49.5 %collective-permute-start.36 = (bf16[2,2,2,48,768]{4,3,0,1,2:T(8,128)(2,1)S(1)}, bf16[2,2,2,48,768]{4,3,0,1,2:T(8,128)(2,1)S(1)}, u32[]{:S(2)}, u32[]{:S(2)}) collective-permute-start(bf16[2,2,2,48,768]{4,3,0,1,2:T(8,128)(2,1)S(1)} %pad_maximum_fusion.15), channel_id=1, source_target_pairs={{0,2},{2,0},{4,6},{6,4},{8,10},{10,8},{12,14},{14,12},{16,18},{18,... | collective-permute-start | bytes 1769480 | tf_op jit(solution)/shard_map/ppermute | solution.py:53
  385.6 48.5 %collective-permute-start.53 = (bf16[2,2,2,48,768]{4,3,0,1,2:T(8,128)(2,1)S(1)}, bf16[2,2,2,48,768]{4,3,0,1,2:T(8,128)(2,1)S(1)}, u32[]{:S(2)}, u32[]{:S(2)}) collective-permute-start(bf16[2,2,2,48,768]{4,3,0,1,2:T(8,128)(2,1)S(1)} %pad_maximum_fusion.17), channel_id=1, source_target_pairs={{0,2},{2,0},{4,6},{6,4},{8,10},{10,8},{12,14},{14,12},{16,18},{18,... | collective-permute-start | bytes 1769480 | tf_op jit(solution)/shard_map/ppermute | solution.py:53
  388.0 16.3 %collective-permute-start.23 = (bf16[2,2,2,48,768]{4,3,0,1,2:T(8,128)(2,1)S(1)}, bf16[2,2,2,48,768]{4,3,0,1,2:T(8,128)(2,1)S(1)}, u32[]{:S(2)}, u32[]{:S(2)}) collective-permute-start(bf16[2,2,2,48,768]{4,3,0,1,2:T(8,128)(2,1)S(1)} %pad_maximum_fusion.14), channel_id=1, source_target_pairs={{0,4},{2,6},{4,0},{6,2},{8,12},{10,14},{12,8},{14,10},{16,20},{18,... | collective-permute-start | bytes 1769480 | tf_op jit(solution)/shard_map/ppermute | solution.py:53
  390.0 42.3 %collective-permute-start.19 = (bf16[2,2,2,48,768]{4,3,0,1,2:T(8,128)(2,1)S(1)}, bf16[2,2,2,48,768]{4,3,0,1,2:T(8,128)(2,1)S(1)}, u32[]{:S(2)}, u32[]{:S(2)}) collective-permute-start(bf16[2,2,2,48,768]{4,3,0,1,2:T(8,128)(2,1)S(1)} %pad_maximum_fusion.13), channel_id=1, source_target_pairs={{0,2},{2,0},{4,6},{6,4},{8,10},{10,8},{12,14},{14,12},{16,18},{18,... | collective-permute-start | bytes 1769480 | tf_op jit(solution)/shard_map/ppermute | solution.py:53
  396.3 43.9 %collective-permute-start.40 = (bf16[2,2,2,48,768]{4,3,0,1,2:T(8,128)(2,1)}, bf16[2,2,2,48,768]{4,3,0,1,2:T(8,128)(2,1)}, u32[]{:S(2)}, u32[]{:S(2)}) collective-permute-start(bf16[2,2,2,48,768]{4,3,0,1,2:T(8,128)(2,1)} %pad_maximum_fusion.16), channel_id=1, source_target_pairs={{0,4},{2,6},{4,0},{6,2},{8,12},{10,14},{12,8},{14,10},{16,20},{18,... | collective-permute-start | bytes 1769480 | tf_op jit(solution)/shard_map/ppermute | solution.py:53
  404.3 38.3 %collective-permute-start.57 = (bf16[2,2,2,48,768]{4,3,0,1,2:T(8,128)(2,1)}, bf16[2,2,2,48,768]{4,3,0,1,2:T(8,128)(2,1)}, u32[]{:S(2)}, u32[]{:S(2)}) collective-permute-start(bf16[2,2,2,48,768]{4,3,0,1,2:T(8,128)(2,1)} %pad_maximum_fusion.18), channel_id=1, source_target_pairs={{0,4},{2,6},{4,0},{6,2},{8,12},{10,14},{12,8},{14,10},{16,20},{18,... | collective-permute-start | bytes 1769480 | tf_op jit(solution)/shard_map/ppermute | solution.py:53
  (133 other events, 1204.4 us)

commit v2 on v1

v2 whole, which is shorter than its diff:
```python
from functools import partial

import jax
import jax.numpy as jnp
from jax import lax
from jax.experimental import pallas as pl
from jax.experimental.pallas import tpu as pltpu
from jax.sharding import PartitionSpec as P

HEAD_DIM = 64
STEP = 7


MASK_FILL = -1e30
NORM_EPSILON = 1e-05
FIRST_DECAY = 0.5
SECOND_DECAY = 0.5
LEARN_RATE = 0.1
WEIGHT_DECAY = 0.01
EPSILON = 1e-08
LOW = jnp.bfloat16
WIDE = jnp.float32


def adamw_step(master, first_moment, second_moment, gradient, decay_rate):
    first_new = FIRST_DECAY * first_moment + (1.0 - FIRST_DECAY) * gradient
    second_new = SECOND_DECAY * second_moment + (1.0 - SECOND_DECAY) * gradient * gradient
    first_fixed = first_new / (1.0 - FIRST_DECAY**STEP)
    second_fixed = second_new / (1.0 - SECOND_DECAY**STEP)
    direction = first_fixed / (jnp.sqrt(second_fixed) + EPSILON)
    master_new = master - LEARN_RATE * (direction + decay_rate * master)
    return (master_new, first_new, second_new)


BLOCK_FF = 512
VMEM = pltpu.CompilerParams(vmem_limit_bytes=58 * 2**20)
ROOT_HALF = 0.7071067811865476
BELL_TOP = 0.3989422804014327


def dot(left, right):
    return jnp.dot(left, right, preferred_element_type=WIDE)


def dot_nt(left, right):
    return lax.dot_general(left, right, (((1,), (1,)), ((), ())), preferred_element_type=WIDE)


def dot_tn(left, right):
    return lax.dot_general(left, right, (((0,), (0,)), ((), ())), preferred_element_type=WIDE)


def gelu_pair(x):
    cdf = 0.5 * lax.erf(x * ROOT_HALF) + 0.5
    return x * cdf, cdf + x * (jnp.exp(x * x * -0.5) * BELL_TOP)


def mean_rows(value):
    return jnp.mean(value, axis=-1, keepdims=True)


def norm_parts(pre):
    centred = pre - mean_rows(pre)
    inverse = lax.rsqrt(mean_rows(centred * centred) + NORM_EPSILON)
    return centred * inverse, inverse


def norm_grad(upstream, normed, inverse, gain):
    scaled = upstream * gain
    return inverse * (scaled - mean_rows(scaled) - normed * mean_rows(scaled * normed))


def col_sum(value):
    return jnp.sum(value, axis=0, keepdims=True)


def fold_rows(value):
    return jnp.sum(value.reshape(-1, 8, value.shape[1]), axis=0)


def by_rows(count, body, start, unroll=1):
    at = lambda r: pl.ds(pl.multiple_of(r * TILE, TILE), TILE)
    return lax.fori_loop(0, count // TILE, lambda r, c: body(at(r), c), start, unroll=unroll)


def lane_half(shape, e):
    lane = lax.broadcasted_iota(jnp.int32, shape, 1)
    return (lane < HEAD_DIM) if e == 0 else (lane >= HEAD_DIM)


TILE = 256


def attend_kernel(
    place, lengths, x_ref, mask_ref, w0_ref, w1_ref, o0_ref, o1_ref, p0_ref, p1_ref, nv_ref,
    qkv_ref, probs_ref, ctx_ref, pre_ref, score_s,
):
    x = x_ref[...]
    row = place[0] * pl.num_programs(0) + pl.program_id(0)
    slot = lax.broadcasted_iota(jnp.int32, (1, x.shape[0]), 1)
    present = (mask_ref[pl.ds(row, 1)] == 1) | (slot == 0)
    valid = jnp.where((slot < lengths[row]) & present, 1.0, 0.0)
    valid = jnp.broadcast_to(valid, (16, x.shape[0])).astype(LOW)
    bias = (1.0 - dot_tn(valid, jnp.full((16, 128), 0.0625, LOW))) * MASK_FILL
    width = w0_ref.shape[2]
    pairs = width // 128
    scale = jnp.asarray(HEAD_DIM ** (-0.5), LOW)
    for half, (w_ref, p_ref) in enumerate(((w0_ref, p0_ref), (w1_ref, p1_ref))):
        base = 3 * width * half
        q = dot(x, w_ref[0]) + p_ref[0:1]
        qkv_ref[:, base : base + width] = q.astype(LOW)
        qkv_ref[:, base + width : base + 2 * width] = dot(x, w_ref[1]).astype(LOW)
        v = dot(x, w_ref[2]) + p_ref[1:2]
        qkv_ref[:, base + 2 * width : base + 3 * width] = v.astype(LOW)
    for half in range(2):
        base = 3 * width * half
        for pair in range(pairs):
            at = base + 128 * pair
            kp = qkv_ref[:, at + width : at + width + 128] * scale
            for e in range(2):
                ke = jnp.where(lane_half(kp.shape, e), kp, jnp.zeros_like(kp))
                score_s[2 * pair + e] = dot_nt(ke, qkv_ref[:, at : at + 128])
        for head in range(2 * pairs):
            for left in range(0, x.shape[0], 128):
                masked = score_s[head, :, left : left + 128] + bias
                top = jnp.max(masked, axis=0, keepdims=True)
                ex = jnp.exp(masked - top)
                total = jnp.sum(ex, axis=0, keepdims=True)
                low = (ex * (1.0 / total)).astype(LOW)
                probs_ref[0, half * 2 * pairs + head, :, left : left + 128] = low
        vt = qkv_ref[:, base + 2 * width : base + 3 * width].T
        for pair in range(pairs):
            outs = []
            for e in range(2):
                low = 128 * pair + HEAD_DIM * e
                outs.append(
                    dot(vt[low : low + HEAD_DIM], probs_ref[0, half * 2 * pairs + 2 * pair + e])
                )
            ctx = jnp.concatenate(outs, axis=0).T.astype(LOW)
            ctx_ref[:, half * width + 128 * pair : half * width + 128 * pair + 128] = ctx
    attn = dot(ctx_ref[:, :width], o0_ref[...]) + dot(ctx_ref[:, width:], o1_ref[...])
    pre_ref[...] = x.astype(WIDE) + nv_ref[0:1] + attn


def attend(place, lengths, hidden_in, key_mask, w0, w1, o0, o1, p0, p1, nv):
    seqs, seq_len = key_mask.shape[0] // 2, key_mask.shape[1]
    d = hidden_in.shape[1]
    width = w0.shape[2]
    heads = 2 * width // HEAD_DIM
    tokens = seqs * seq_len
    full = lambda a: pl.BlockSpec(a.shape, lambda s, c, n: (0,) * a.ndim)
    rows = lambda cols: pl.BlockSpec((seq_len, cols), lambda s, c, n: (s, 0))
    return pl.pallas_call(
        attend_kernel,
        out_shape=(
            jax.ShapeDtypeStruct((tokens, 6 * width), LOW),
            jax.ShapeDtypeStruct((seqs, heads, seq_len, seq_len), LOW),
            jax.ShapeDtypeStruct((tokens, 2 * width), LOW),
            jax.ShapeDtypeStruct((tokens, d), WIDE),
        ),
        grid_spec=pltpu.PrefetchScalarGridSpec(
            num_scalar_prefetch=2,
            grid=(seqs,),
            in_specs=[
                pl.BlockSpec((seq_len, d), lambda s, c, n: (c[0] * seqs + s, 0)),
                *(full(a) for a in (key_mask, w0, w1, o0, o1, p0, p1, nv)),
            ],
            out_specs=[
                rows(6 * width),
                pl.BlockSpec((1, heads, seq_len, seq_len), lambda s, c, n: (s, 0, 0, 0)),
                rows(2 * width),
                rows(d),
            ],
            scratch_shapes=[pltpu.VMEM((heads // 2, seq_len, seq_len), WIDE)],
        ),
        compiler_params=VMEM,
        name="attend",
        cost_estimate=pl.CostEstimate(flops=8 * 10**9, bytes_accessed=25 * 10**6, transcendentals=3 * 10**6),
    )(place, lengths, hidden_in, key_mask, w0, w1, o0, o1, p0, p1, nv)


ROWS = 512


def ffn_fwd_kernel(
    core, pre_ref, up_ref, e0_ref, e1_ref, c0_ref, c1_ref, b0_ref, b1_ref, nv_ref,
    act_ref, slope_ref, out_ref, grad_ref, low_ref, hl_ref, sums_ref, whole_ref,
    acc_s, wide_s,
):
    j = pl.program_id(0)
    last = pl.num_programs(0) - 1
    tokens = pre_ref.shape[0]

    @pl.when(j == 0)
    def _():
        def one(rows, _):
            normed, _ = norm_parts(pre_ref[rows])
            hidden_one = normed * nv_ref[2:3] + nv_ref[3:4]
            hl_ref[rows] = hidden_one.astype(LOW)
            acc_s[rows] = hidden_one + nv_ref[1:2]
            return 0

        by_rows(tokens, one, 0)

    def step(e_ref, c_ref, b_ref):
        for top in range(0, tokens, ROWS):
            wide_s[top : top + ROWS] = dot(hl_ref[top : top + ROWS], e_ref[...])
        for top in range(0, tokens, ROWS):
            for at in range(top, top + ROWS, 16):
                rows = slice(at, at + 16)
                act, slope = gelu_pair(wide_s[rows] + b_ref[...])
                act_ref[rows] = act.astype(LOW)
                slope_ref[rows] = slope.astype(LOW)
            acc_s[top : top + ROWS] += dot(act_ref[top : top + ROWS], c_ref[...])

    @pl.when(j < (last + 1) // 2)
    def _():
        step(e0_ref, c0_ref, b0_ref)

    @pl.when(j >= (last + 1) // 2)
    def _():
        step(e1_ref, c1_ref, b1_ref)

    @pl.when(j == last)
    def _():
        def one(rows, sums):
            normed, inverse = norm_parts(acc_s[rows])
            out = (normed * nv_ref[4:5] + nv_ref[5:6]).astype(LOW)
            out_ref[rows] = out
            whole_ref[rows] = out
            up = up_ref[rows].astype(WIDE)
            grad = norm_grad(up, normed, inverse, nv_ref[4:5])
            grad_ref[rows] = grad
            low_ref[rows] = grad.astype(LOW)
            new = (fold_rows(grad), fold_rows(up * normed), fold_rows(up))
            return tuple(a + b for a, b in zip(sums, new))

        zero = jnp.zeros((8, pre_ref.shape[1]), WIDE)
        sums = by_rows(tokens, one, (zero,) * 3, unroll=1)
        for i in range(3):
            sums_ref[i : i + 1] = col_sum(sums[i])
        sums_ref[3:8] = jnp.zeros((5, sums_ref.shape[1]), WIDE)


def ffn_fwd(core, pre, grad_out, e0, e1, c0, c1, b0, b1, nv):
    tokens, d = pre.shape
    width = e0.shape[1]
    steps = width // BLOCK_FF
    full = lambda shape: pl.BlockSpec(shape, lambda j, c: (0,) * len(shape))
    lower = lambda j: jnp.minimum(j, steps - 1)
    upper = lambda j: jnp.maximum(j - steps, 0)
    return pl.pallas_call(
        ffn_fwd_kernel,
        out_shape=(
            jax.ShapeDtypeStruct((tokens, 2 * width), LOW),
            jax.ShapeDtypeStruct((tokens, 2 * width), LOW),
            jax.ShapeDtypeStruct((tokens, d), LOW),
            jax.ShapeDtypeStruct((tokens, d), WIDE),
            jax.ShapeDtypeStruct((tokens, d), LOW),
            jax.ShapeDtypeStruct((tokens, d), LOW),
            jax.ShapeDtypeStruct((8, d), WIDE),
            jax.ShapeDtypeStruct((2 * tokens, d), LOW),
        ),
        grid_spec=pltpu.PrefetchScalarGridSpec(
            num_scalar_prefetch=1,
            grid=(2 * steps,),
            in_specs=[
                full((tokens, d)),
                pl.BlockSpec((tokens, d), lambda j, c: (c[0], 0)),
                pl.BlockSpec((d, BLOCK_FF), lambda j, c: (0, lower(j))),
                pl.BlockSpec((d, BLOCK_FF), lambda j, c: (0, upper(j))),
                pl.BlockSpec((BLOCK_FF, d), lambda j, c: (lower(j), 0)),
                pl.BlockSpec((BLOCK_FF, d), lambda j, c: (upper(j), 0)),
                pl.BlockSpec((1, BLOCK_FF), lambda j, c: (0, lower(j))),
                pl.BlockSpec((1, BLOCK_FF), lambda j, c: (0, upper(j))),
                full(nv.shape),
            ],
            out_specs=[
                pl.BlockSpec((tokens, BLOCK_FF), lambda j, c: (0, j)),
                pl.BlockSpec((tokens, BLOCK_FF), lambda j, c: (0, j)),
                full((tokens, d)),
                full((tokens, d)),
                full((tokens, d)),
                full((tokens, d)),
                full((8, d)),
                pl.BlockSpec((tokens, d), lambda j, c: (c[0], 0)),
            ],
            scratch_shapes=[pltpu.VMEM((tokens, d), WIDE), pltpu.VMEM((tokens, BLOCK_FF), WIDE)],
        ),
        compiler_params=VMEM,
        name="ffn_fwd",
        cost_estimate=pl.CostEstimate(flops=11 * 10**9, bytes_accessed=40 * 10**6, transcendentals=4 * 10**6),
    )(core, pre, grad_out, e0, e1, c0, c1, b0, b1, nv)


def place_rows(out_ref, value, rank, count, left=0):
    rows = value.shape[0] // count
    cols = slice(left, left + value.shape[1])
    if rows % 16:
        out_ref[:, cols] = value
        return
    for i in range(count):
        apart = jnp.bitwise_xor(rank, i)
        at = (apart & 3) * (count // 4) + (apart >> 2)
        there = pl.ds(pl.multiple_of(at * rows, 16), rows)
        out_ref[there, cols] = value[i * rows : (i + 1) * rows]


def placed(grad, rank, count):
    rows = grad.shape[0] // count
    if rows % 16 == 0:
        return grad
    at = jnp.arange(count)
    apart = (at // (count // 4)) | ((at % (count // 4)) << 2)
    return grad.reshape(count, rows, -1)[apart ^ rank].reshape(grad.shape)


ANY = pl.BlockSpec(memory_space=pl.ANY)


def with_deps(body, lead, inputs, deps):
    def kernel(*refs):
        body(*refs[: lead + inputs], *refs[lead + inputs + len(deps) :])

    return kernel


def weight_kernel(count, place, left_ref, right_ref, out_ref):
    place_rows(out_ref, dot_tn(left_ref[...], right_ref[...]).astype(LOW), place[1], count)


def weight_grad(place, n_dp, left, right, first, count, block, deps=()):
    tokens = right.shape[0]
    d = left.shape[1]
    halves = left.shape[0] // tokens
    out = pl.pallas_call(
        with_deps(partial(weight_kernel, n_dp), 1, 2, deps),
        out_shape=jax.ShapeDtypeStruct((d, count * block), LOW),
        grid_spec=pltpu.PrefetchScalarGridSpec(
            num_scalar_prefetch=1,
            grid=(count,),
            in_specs=[
                pl.BlockSpec((tokens, d), lambda j, c: (c[0] if halves == 2 else 0, 0)),
                pl.BlockSpec((tokens, block), lambda j, c: (0, first + j)),
            ]
            + [ANY] * len(deps),
            out_specs=pl.BlockSpec((d, block), lambda j, c: (0, j)),
        ),
        compiler_params=VMEM,
        name="weight_grad",
        cost_estimate=pl.CostEstimate(
            flops=2 * d * tokens * count * block, bytes_accessed=6 * 10**6, transcendentals=0
        ),
    )(place, left, right, *deps)
    return placed(out, place[1], n_dp)


def ffn_bwd_kernel(
    final, n_dp, place, low_ref, slope_ref, e_ref, c_ref, sofar_ref, pre_ref, hl_ref, ctx_ref, nv_ref,
    we_ref, bias_ref, one_ref, *rest,
):
    if final:
        ag_ref, sums_ref, wo_ref, acc_s, wg_s, wide_s = rest
    else:
        acc_s, wg_s, wide_s = rest
    j = pl.program_id(0)
    last = pl.num_programs(0) - 1
    tokens = low_ref.shape[0]

    @pl.when(j == 0)
    def _():
        acc_s[...] = sofar_ref[...]

    for top in range(0, tokens, ROWS):
        wide_s[top : top + ROWS] = dot_nt(low_ref[top : top + ROWS], c_ref[...])
    bias = jnp.zeros((8, BLOCK_FF), WIDE)
    for top in range(0, tokens, ROWS):
        for at in range(top, top + ROWS, 16):
            rows = slice(at, at + 16)
            wg = (wide_s[rows] * slope_ref[rows].astype(WIDE)).astype(LOW)
            wg_s[rows] = wg
            bias = bias + fold_rows(wg.astype(WIDE))
        acc_s[top : top + ROWS] += dot_nt(wg_s[top : top + ROWS], e_ref[...])
    bias_ref[...] = col_sum(bias)
    grad = dot_tn(hl_ref[...], wg_s[...]).astype(LOW)
    if final:
        for i in range(we_ref.shape[1] // BLOCK_FF):

            @pl.when(j == i)
            def _():
                place_rows(we_ref, grad, place[1], n_dp, i * BLOCK_FF)
    else:
        place_rows(we_ref, grad, place[1], n_dp)

    @pl.when(j == last)
    def _():
        if not final:
            one_ref[...] = acc_s[...]
            return

        def one(rows, sums):
            normed, inverse = norm_parts(pre_ref[rows])
            up = acc_s[rows]
            grad = norm_grad(up, normed, inverse, nv_ref[2:3])
            one_ref[rows] = grad
            ag_ref[rows] = grad.astype(LOW)
            new = (fold_rows(grad), fold_rows(up * normed), fold_rows(up))
            return tuple(a + b for a, b in zip(sums, new))

        zero = jnp.zeros((8, pre_ref.shape[1]), WIDE)
        sums = by_rows(tokens, one, (zero,) * 3, unroll=1)
        for i in range(3):
            sums_ref[i : i + 1] = col_sum(sums[i])
        sums_ref[3:8] = jnp.zeros((5, sums_ref.shape[1]), WIDE)
        half = wo_ref.shape[1]
        grad = dot_tn(ag_ref[...], ctx_ref[:, :half]).astype(LOW)
        place_rows(we_ref, grad, place[1], n_dp, we_ref.shape[1] - half)
        place_rows(wo_ref, dot_tn(ag_ref[...], ctx_ref[:, half:]).astype(LOW), place[1], n_dp)


def ffn_bwd(place, n_dp, final, low, slope, e, c, sofar, pre, hl, ctx, nv, deps=()):
    tokens, d = low.shape
    width = e.shape[1]
    steps = width // BLOCK_FF
    first = 0 if final else steps
    full = lambda shape: pl.BlockSpec(shape, lambda j, c: (0,) * len(shape))
    half = ctx.shape[1] // 2
    if final:
        both = (d, width + half)
        outs = [(jax.ShapeDtypeStruct(both, LOW), full(both))]
    else:
        outs = [
            (jax.ShapeDtypeStruct((d, width), LOW), pl.BlockSpec((d, BLOCK_FF), lambda j, c: (0, j)))
        ]
    outs += [
        (jax.ShapeDtypeStruct((1, width), WIDE), pl.BlockSpec((1, BLOCK_FF), lambda j, c: (0, j))),
        (jax.ShapeDtypeStruct((tokens, d), WIDE), full((tokens, d))),
    ]
    if final:
        outs += [
            (jax.ShapeDtypeStruct((tokens, d), LOW), full((tokens, d))),
            (jax.ShapeDtypeStruct((8, d), WIDE), full((8, d))),
            (jax.ShapeDtypeStruct((d, half), LOW), full((d, half))),
        ]
    out = pl.pallas_call(
        with_deps(partial(ffn_bwd_kernel, final, n_dp), 1, 9, deps),
        out_shape=tuple(o[0] for o in outs),
        grid_spec=pltpu.PrefetchScalarGridSpec(
            num_scalar_prefetch=1,
            grid=(steps,),
            in_specs=[
                full((tokens, d)),
                pl.BlockSpec((tokens, BLOCK_FF), lambda j, c: (0, first + j)),
                pl.BlockSpec((d, BLOCK_FF), lambda j, c: (0, j)),
                pl.BlockSpec((BLOCK_FF, d), lambda j, c: (j, 0)),
                full((tokens, d)),
                full((tokens, d)) if final else ANY,
                full((tokens, d)),
                full(ctx.shape) if final else ANY,
                full(nv.shape),
            ]
            + [ANY] * len(deps),
            out_specs=[o[1] for o in outs],
            scratch_shapes=[
                pltpu.VMEM((tokens, d), WIDE),
                pltpu.VMEM((tokens, BLOCK_FF), LOW),
                pltpu.VMEM((tokens, BLOCK_FF), WIDE),
            ],
        ),
        compiler_params=VMEM,
        name="ffn_bwd",
        cost_estimate=pl.CostEstimate(flops=8 * 10**9, bytes_accessed=20 * 10**6, transcendentals=0),
    )(place, low, slope, e, c, sofar, pre, hl, ctx, nv, *deps)
    out = list(out)
    for i in (0, 5) if final else (0,):
        out[i] = placed(out[i], place[1], n_dp)
    return out


def attend_back_kernel(
    ag_ref, probs_ref, qkv_ref, o0_ref, o1_ref, grad_ref, sums_ref, dp_s, ds_s, cg_s
):
    width = o0_ref.shape[0]
    pairs = width // 128
    scale = jnp.asarray(HEAD_DIM ** (-0.5), LOW)
    keep = [lane_half((ag_ref.shape[0], 128), e) for e in range(2)]
    side = lambda value, e: jnp.where(keep[e], value, jnp.zeros_like(value))
    for half, o_ref in enumerate((o0_ref, o1_ref)):
        cg_s[...] = dot_nt(ag_ref[...], o_ref[...]).astype(LOW)
        first = half * 2 * pairs
        for pair in range(pairs):
            at = 3 * width * half + 128 * pair
            do = cg_s[:, 128 * pair : 128 * pair + 128]
            vp = qkv_ref[:, at + 2 * width : at + 2 * width + 128]
            for e in range(2):
                dp_s[2 * pair + e] = dot_nt(side(vp, e), do)
            dv = dot(probs_ref[0, first + 2 * pair], side(do, 0))
            dv = (dv + dot(probs_ref[0, first + 2 * pair + 1], side(do, 1))).astype(LOW)
            grad_ref[:, at + 2 * width : at + 2 * width + 128] = dv
            to = half * width + 128 * pair
            sums_ref[0, 1:2, to : to + 128] = col_sum(dv.astype(WIDE))
        for head in range(2 * pairs):
            for left in range(0, ag_ref.shape[0], 128):
                cols = slice(left, left + 128)
                dp = dp_s[head, :, cols]
                probs = probs_ref[0, first + head, :, cols].astype(WIDE)
                inner = jnp.sum(dp * probs, axis=0, keepdims=True)
                ds_s[head, :, cols] = (probs * (dp - inner)).astype(LOW)
        for pair in range(pairs):
            at = 3 * width * half + 128 * pair
            qp = qkv_ref[:, at : at + 128] * scale
            kp = qkv_ref[:, at + width : at + width + 128] * scale
            dk = dot(ds_s[2 * pair], side(qp, 0)) + dot(ds_s[2 * pair + 1], side(qp, 1))
            dq = dot_tn(ds_s[2 * pair], side(kp, 0)) + dot_tn(ds_s[2 * pair + 1], side(kp, 1))
            dq = dq.astype(LOW)
            grad_ref[:, at : at + 128] = dq
            grad_ref[:, at + width : at + width + 128] = dk.astype(LOW)
            to = half * width + 128 * pair
            sums_ref[0, 0:1, to : to + 128] = col_sum(dq.astype(WIDE))


def attend_back(ag, probs, qkv, o0, o1, first, count, before=None, deps=()):
    seqs, heads, seq_len, _ = probs.shape
    tokens, d = ag.shape
    width = o0.shape[0]
    full = lambda a: pl.BlockSpec(a.shape, lambda s: (0,) * a.ndim)
    rows = lambda cols: pl.BlockSpec((seq_len, cols), lambda s: (first + s, 0))
    if before is not None:
        deps = tuple(before) + tuple(deps)
    return pl.pallas_call(
        with_deps(attend_back_kernel, 0, 5, deps),
        out_shape=(
            jax.ShapeDtypeStruct((tokens, 6 * width), LOW),
            jax.ShapeDtypeStruct((seqs, 8, 2 * width), WIDE),
        ),
        grid=(count,),
        in_specs=[
            rows(d),
            pl.BlockSpec((1, heads, seq_len, seq_len), lambda s: (first + s, 0, 0, 0)),
            rows(6 * width),
            full(o0),
            full(o1),
        ]
        + [ANY] * len(deps),
        out_specs=[
            rows(6 * width),
            pl.BlockSpec((1, 8, 2 * width), lambda s: (first + s, 0, 0)),
        ],
        input_output_aliases={} if before is None else {5: 0, 6: 1},
        scratch_shapes=[
            pltpu.VMEM((heads // 2, seq_len, seq_len), WIDE),
            pltpu.VMEM((heads // 2, seq_len, seq_len), LOW),
            pltpu.VMEM((seq_len, width), LOW),
        ],
        compiler_params=VMEM,
        name="attend_back",
        cost_estimate=pl.CostEstimate(
            flops=3 * count * 10**9, bytes_accessed=5 * count * 10**6, transcendentals=0
        ),
    )(ag, probs, qkv, o0, o1, *deps)


def input_kernel(place, grad_ref, w0_ref, w1_ref, one_ref, out_ref, whole_ref):
    width = w0_ref.shape[2]
    total = one_ref[...]
    for i in range(6):
        w = (w0_ref, w1_ref)[i // 3][i % 3]
        total = total + dot_nt(grad_ref[:, i * width : (i + 1) * width], w)
    out_ref[...] = total.astype(LOW)
    whole_ref[...] = total.astype(LOW).astype(WIDE)


def input_side(place, grad, w0, w1, one, deps=()):
    tokens, d = one.shape
    block = min(ROWS, tokens)
    full = lambda a: pl.BlockSpec(a.shape, lambda s, c: (0,) * a.ndim)
    rows = lambda cols: pl.BlockSpec((block, cols), lambda s, c: (s, 0))
    return pl.pallas_call(
        with_deps(input_kernel, 1, 4, deps),
        out_shape=(
            jax.ShapeDtypeStruct((tokens, d), LOW),
            jax.ShapeDtypeStruct((2 * tokens, d), WIDE),
        ),
        grid_spec=pltpu.PrefetchScalarGridSpec(
            num_scalar_prefetch=1,
            grid=(tokens // block,),
            in_specs=[rows(grad.shape[1]), full(w0), full(w1), rows(d)] + [ANY] * len(deps),
            out_specs=[
                rows(d),
                pl.BlockSpec((block, d), lambda s, c: (c[0] * (tokens // block) + s, 0)),
            ],
        ),
        compiler_params=VMEM,
        name="input_side",
        cost_estimate=pl.CostEstimate(flops=4 * 10**9, bytes_accessed=14 * 10**6, transcendentals=0),
    )(place, grad, w0, w1, one, *deps)


def put_kernel(place, other_ref, whole_ref, out_ref):
    out_ref[...] = other_ref[...].astype(out_ref.dtype)


def put_other(place, other, whole, deps=()):
    tokens, d = other.shape
    block = tokens // 4
    return pl.pallas_call(
        with_deps(put_kernel, 1, 2, deps),
        out_shape=jax.ShapeDtypeStruct(whole.shape, whole.dtype),
        grid_spec=pltpu.PrefetchScalarGridSpec(
            num_scalar_prefetch=1,
            grid=(4,),
            in_specs=[pl.BlockSpec((block, d), lambda s, c: (s, 0)), ANY] + [ANY] * len(deps),
            out_specs=pl.BlockSpec((block, d), lambda s, c: ((1 - c[0]) * 4 + s, 0)),
        ),
        input_output_aliases={2: 0},
        compiler_params=VMEM,
        name="put_other",
        cost_estimate=pl.CostEstimate(flops=0, bytes_accessed=4 * tokens * d, transcendentals=0),
    )(place, other, whole, *deps)


def gather_kernel(count, layout, wide, place, z_ref, x_ref, y_ref, da_ref, db_ref, *refs):
    outs, held = refs[: len(layout)], refs[len(layout)]
    block = z_ref.shape[0] // (count // 4)
    step = pl.program_id(0)

    def blocks():
        for apart in range(count):
            first = (apart >> 2) * block
            ref = (z_ref, x_ref, y_ref, da_ref)[apart & 3]
            if apart & 3 == 3 and first >= da_ref.shape[0]:
                ref, first = db_ref, first - da_ref.shape[0]
            yield jnp.bitwise_xor(place[1], apart), ref[first : first + block]

    for (kind, first, end), out in zip(layout, outs):

        @pl.when((step >= first) & (step < end))
        def _():
            for at, value in blocks():
                if kind == "deep":
                    rows = block // out.shape[0]
                    there = pl.ds(pl.multiple_of(at * rows, 16), rows)
                    for i in range(out.shape[0]):
                        out[i, there] = value[i * rows : i * rows + rows]
                else:
                    to = held if kind == "flip" else out
                    to[pl.ds(pl.multiple_of(at * block, 16), block)] = value
            if kind == "flip":
                out[...] = held[...].T


def gather_place(place, n_dp, layout, z, x, y, da, db, deps=()):
    rows, cols = z.shape[0] * 4, z.shape[1]
    block = rows // n_dp
    deep = layout[0][0] == "deep"
    wide = 128 if deep else 384
    shapes, specs, steps = [], [], []
    for kind, left, right in layout:
        full = right - left
        if deep:
            left, right = 0, cols
            shapes.append((full // cols, rows * cols // full, cols))
        else:
            shapes.append((full, rows) if kind == "flip" else (rows, full))
        first, end = left // wide, right // wide
        steps.append((kind, first, end))
        at = lambda j, first=first, end=end: jnp.clip(j - first, 0, end - first - 1)
        if deep:
            specs.append(pl.BlockSpec(shapes[-1][:2] + (wide,), lambda j, c, at=at: (0, 0, at(j))))
        elif kind == "flip":
            specs.append(pl.BlockSpec((wide, rows), lambda j, c, at=at: (at(j), 0)))
        else:
            specs.append(pl.BlockSpec((rows, wide), lambda j, c, at=at: (0, at(j))))
    if (block // (shapes[0][0] if deep else 1)) % 16:
        plane = jnp.stack([z, x, y, jnp.concatenate([da, db])])
        blocks = plane.reshape(4, n_dp // 4, block, cols).transpose(1, 0, 2, 3)
        blocks = blocks.reshape(n_dp, block, cols)[jnp.arange(n_dp) ^ place[1]]
        outs = []
        for (kind, left, right), shape in zip(layout, shapes):
            if deep:
                outs.append(
                    blocks.reshape(n_dp, shape[0], -1, cols).transpose(1, 0, 2, 3).reshape(shape)
                )
            else:
                whole = blocks.reshape(rows, cols)[:, left:right]
                outs.append(whole.T if kind == "flip" else whole)
        return outs
    spec = lambda a: pl.BlockSpec((a.shape[0], wide), lambda j, c: (0, j))
    return pl.pallas_call(
        with_deps(partial(gather_kernel, n_dp, steps, wide), 1, 5, deps),
        out_shape=[jax.ShapeDtypeStruct(shape, LOW) for shape in shapes],
        grid_spec=pltpu.PrefetchScalarGridSpec(
            num_scalar_prefetch=1,
            grid=(cols // wide,),
            in_specs=[spec(a) for a in (z, x, y, da, db)] + [ANY] * len(deps),
            out_specs=specs,
            scratch_shapes=[pltpu.VMEM((rows, wide), LOW)],
        ),
        compiler_params=VMEM,
        name="gather_place",
        cost_estimate=pl.CostEstimate(flops=0, bytes_accessed=4 * rows * cols, transcendentals=0),
    )(place, z, x, y, da, db, *deps)


def swap(value):
    return lax.ppermute(value, "tensor", [(0, 1), (1, 0)])


def across(value, apart, count):
    return lax.ppermute(value, "dp", [(i, i ^ apart) for i in range(count)])


def far_groups(count):
    groups, weight = [], 4
    while weight < count:
        members = min(4, count // weight)
        groups.append((weight, members))
        weight *= members
    return groups


def scatter_flow(mine, came, count):
    rows, width = mine.shape
    shape = lambda a: a.reshape(2, 2, 2, rows // 8, a.shape[1])
    mine, came = shape(mine), [shape(c) for c in came]

    def part(*at):
        other = [c[at].astype(WIDE) for c in came]
        return mine[at].astype(WIDE) + (jnp.concatenate(other, axis=-1) if other[1:] else other[0])

    every = slice(None)
    to_x, to_y = part(every, 1, 0).astype(LOW), part(1, every, 1).astype(LOW)
    from_x, from_y = yield [to_x, to_y], lambda v: [across(v[0], 1, count), across(v[1], 2, count)]
    to_y = (part(1, 0, 0) + from_x[1].astype(WIDE)).astype(LOW)
    to_x = (part(0, 1, 1) + from_y[1].astype(WIDE)).astype(LOW)
    last_x, last_y = yield [to_x, to_y], lambda v: [across(v[0], 1, count), across(v[1], 2, count)]
    upper = part(0, 0, 0) + from_x[0].astype(WIDE) + last_y.astype(WIDE)
    lower = part(0, 0, 1) + from_y[0].astype(WIDE) + last_x.astype(WIDE)
    held = jnp.concatenate([upper, lower], axis=0)
    for weight, members in reversed(far_groups(count)):
        pieces = held.reshape(members, -1, width)
        sends = [pieces[m].astype(LOW) for m in range(1, members)]
        came = yield (
            sends,
            lambda v, w=weight: [across(p, (m + 1) * w, count) for m, p in enumerate(v)],
        )
        held = pieces[0]
        for piece in came:
            held = held + piece.astype(WIDE)
    return held


def gather_flow(shard, count):
    held = shard
    for weight, members in far_groups(count):
        came = yield (
            [held],
            lambda v, w=weight, n=members: [across(v[0], m * w, count) for m in range(1, n)],
        )
        held = jnp.concatenate([held] + list(came), axis=0)
    half = held.shape[0] // 2
    x, y = yield [held], lambda v: [across(v[0], 1, count), across(v[0], 2, count)]
    upper, lower = x[:half], y[half:]
    both = yield [upper, lower], lambda v: [across(v[0], 2, count), across(v[1], 1, count)]
    return held, x, y, both[0], both[1]


def total_flow(mine, others, count):
    (came,) = yield [others], lambda v: [swap(v[0])]
    total = mine + came
    apart = 1
    while apart < count:
        (came,) = yield [total], lambda v, apart=apart: [across(v[0], apart, count)]
        total = total + came
        apart *= 2
    return total


def behind(value, after):
    return lax.optimization_barrier((value, after))[0]


class Flow:
    def __init__(self, steps, then=None):
        self.steps, self.then = steps, then
        self.came, self.result, self.done = None, None, False
        self.sends = ()

    def advance(self, after=None):
        if after is not None and self.came is not None:
            self.came = behind(list(self.came), after)
        while not self.done:
            try:
                sends, send = self.steps.send(self.came)
            except StopIteration as stop:
                if self.then is None:
                    self.result, self.done = stop.value, True
                    return []
                self.steps, self.then = self.then(stop.value)
                self.came = None
                continue
            self.came, self.sends = send(sends), list(sends)
            return self.sends
        return []

    def finish(self):
        while not self.done:
            self.advance()
        return self.result


def local(
    n_dp,
    hidden_in,
    grad_out,
    lengths,
    key_mask,
    triple_weight,
    outward_weight,
    expand_weight,
    contract_weight,
    triple_master,
    triple_first,
    triple_second,
    outward_master,
    outward_first,
    outward_second,
    expand_master,
    expand_first,
    expand_second,
    contract_master,
    contract_first,
    contract_second,
    pair_bias,
    pair_first,
    pair_second,
    expand_bias,
    expand_bias_first,
    expand_bias_second,
    norm_vectors,
    vectors_first,
    vectors_second,
):
    core = lax.axis_index("tensor")
    rank = lax.axis_index("dp")

    own = pair_bias.shape[1]
    n_bias = expand_bias.shape[0]
    place = jnp.stack([core, rank]).astype(jnp.int32)
    bias_row = expand_bias[None]
    triple_other = swap(triple_weight)
    pair_other = swap(pair_bias)
    outward_other = swap(outward_weight)
    expand_here, contract_here, bias_here = behind(
        [expand_weight, contract_weight, bias_row], [triple_other, pair_other, outward_other]
    )
    bias_other = swap(bias_here)
    expand_other = swap(expand_here)
    contract_other = swap(contract_here)
    updates = {}

    def contract_then(share):
        new = adamw_step(
            contract_master.T, contract_first.T, contract_second.T, share, WEIGHT_DECAY
        )
        updates["contract"] = new
        return gather_flow(new[0].astype(LOW), n_dp), None

    def expand_then(share):
        new = adamw_step(
            expand_master, expand_first, expand_second, share[:, :n_bias], WEIGHT_DECAY
        )
        out = adamw_step(
            outward_master.T, outward_first.T, outward_second.T, share[:, n_bias:], WEIGHT_DECAY
        )
        updates["expand"], updates["outward"] = new, out
        return gather_flow(jnp.concatenate([new[0], out[0]], axis=1).astype(LOW), n_dp), None

    def triple_then(share):
        share = jnp.stack([share[:, j * own : (j + 1) * own] for j in range(3)])
        new = adamw_step(triple_master, triple_first, triple_second, share, WEIGHT_DECAY)
        updates["triple"] = new
        return gather_flow(new[0].astype(LOW).reshape(-1, own), n_dp), None

    qkv, probs, context, pre_one = attend(
        place, lengths, hidden_in, key_mask, triple_weight, triple_other, outward_weight,
        outward_other, pair_bias, pair_other, norm_vectors,
    )
    active, slope, layer_own, pre_two_grad, branch_grad, hidden_low, sums_two, layer_out = ffn_fwd(
        place, pre_one, grad_out, expand_weight, expand_other, contract_weight, contract_other,
        bias_row, bias_other, norm_vectors,
    )
    layer_other = swap(layer_own)

    steps = n_bias // BLOCK_FF
    weight = partial(weight_grad, place, n_dp)
    contract_theirs = weight(branch_grad, active, steps, steps, BLOCK_FF)
    contract_mine = weight(branch_grad, active, 0, steps, BLOCK_FF, deps=(contract_theirs,))
    contract_flow = Flow(scatter_flow(contract_mine, [swap(contract_theirs)], n_dp), contract_then)
    sends = contract_flow.advance()
    expand_theirs, bias_theirs, hidden_sofar = ffn_bwd(
        place, n_dp, False, branch_grad, slope, expand_other, contract_other, pre_two_grad,
        pre_two_grad, hidden_low, context, norm_vectors, deps=sends,
    )
    expand_came = swap(expand_theirs)
    sends = contract_flow.advance(bias_theirs)
    expand_mine, bias_mine, pre_one_grad, attention_grad, sums_one, outward_theirs = ffn_bwd(
        place, n_dp, True, branch_grad, slope, expand_weight, contract_weight, hidden_sofar,
        pre_one, hidden_low, context, norm_vectors, deps=sends,
    )
    expand_flow = Flow(
        scatter_flow(expand_mine, [expand_came, swap(outward_theirs)], n_dp), expand_then
    )
    sends = contract_flow.advance(sums_one) + expand_flow.advance()
    projected_grad, sums_pair = attend_back(
        attention_grad, probs, qkv, outward_weight, outward_other, 0, lengths.shape[0] // 2,
        deps=sends,
    )
    sends = contract_flow.advance(sums_pair) + expand_flow.advance(sums_pair)
    triple_theirs = weight(hidden_in, projected_grad, 1, 1, 3 * own, deps=sends)
    triple_mine = weight(hidden_in, projected_grad, 0, 1, 3 * own, deps=(triple_theirs,))
    triple_flow = Flow(scatter_flow(triple_mine, [swap(triple_theirs)], n_dp), triple_then)
    sends = triple_flow.advance() + expand_flow.advance(triple_mine)
    input_own, input_grad = input_side(
        place, projected_grad, triple_weight, triple_other, pre_one_grad, deps=sends
    )

    triple_flow.advance(input_own)
    contract_flow.advance(triple_flow.sends)
    expand_flow.advance(triple_flow.sends)
    layer_out = put_other(place, layer_other, layer_out, deps=triple_flow.sends)

    d = norm_vectors.shape[1]
    sums_pair, bias_mine, bias_theirs = behind([sums_pair, bias_mine, bias_theirs], layer_out)
    pair_grad = jnp.sum(sums_pair, axis=0)[:2]
    spare = jnp.zeros((8 - (2 * own + n_bias) // d, d), WIDE)
    bundle = lambda left, right, bias: jnp.concatenate(
        [
            sums_one,
            sums_two,
            pair_grad[:, left:right].reshape(-1, d),
            bias.reshape(-1, d),
            spare,
        ]
    )
    vector_flow = Flow(
        total_flow(bundle(0, own, bias_mine), bundle(own, 2 * own, bias_theirs), n_dp)
    )
    vector_flow.advance()
    triple_flow.advance(layer_out)
    contract_flow.advance(triple_flow.sends)
    input_grad = put_other(place, swap(input_own), input_grad, deps=triple_flow.sends)
    vector_flow.advance(input_grad)
    expand_flow.advance(input_grad)
    triple_flow.advance(input_grad)
    gather = partial(gather_place, place, n_dp)
    contract_flow.finish()
    (contract_copy,) = gather(
        (("flip", 0, n_bias),), *contract_flow.result, deps=triple_flow.sends
    )
    vector_flow.advance(contract_copy)
    expand_flow.advance(contract_copy)
    triple_flow.advance(contract_copy)
    vector_flow.advance(triple_flow.sends)
    expand_flow.finish()
    expand_copy, outward_copy = gather(
        (("plain", 0, n_bias), ("flip", n_bias, n_bias + own)),
        *expand_flow.result,
        deps=triple_flow.sends,
    )
    triple_flow.advance(expand_copy)
    vector_sum = vector_flow.finish()
    triple_flow.finish()
    (triple_copy,) = gather((("deep", 0, 3 * own),), *triple_flow.result)
    vector_total = jnp.stack([vector_sum[i] for i in (0, 8, 1, 2, 9, 10)])
    pair_total = vector_sum[16 : 16 + 2 * own // d].reshape(2, own)
    widen_total = vector_sum[16 + 2 * own // d :].reshape(-1)[:n_bias]
    contract_new, expand_new = updates["contract"], updates["expand"]
    outward_new, triple_new = updates["outward"], updates["triple"]
    pair_new = adamw_step(pair_bias, pair_first, pair_second, pair_total, 0.0)
    widen_new = adamw_step(expand_bias, expand_bias_first, expand_bias_second, widen_total, 0.0)
    vectors_new = adamw_step(norm_vectors, vectors_first, vectors_second, vector_total, 0.0)
    return (
        layer_out,
        input_grad,
        triple_new[0],
        triple_new[1],
        triple_new[2],
        triple_copy,
        outward_new[0].T,
        outward_new[1].T,
        outward_new[2].T,
        outward_copy,
        expand_new[0],
        expand_new[1],
        expand_new[2],
        expand_copy,
        contract_new[0].T,
        contract_new[1].T,
        contract_new[2].T,
        contract_copy,
        pair_new[0],
        pair_new[1],
        pair_new[2],
        widen_new[0],
        widen_new[1],
        widen_new[2],
        vectors_new[0],
        vectors_new[1],
        vectors_new[2],
    )


def solution(mesh):
    matrix_specs = (
        P(None, "dp", "tensor"),
        P("tensor", "dp"),
        P("dp", "tensor"),
        P("tensor", "dp"),
    )
    copy_specs = (P(None, None, "tensor"), P("tensor", None), P(None, "tensor"), P("tensor", None))
    vector_specs = (P(None, "tensor"),) * 3 + (P("tensor"),) * 3 + (P(),) * 3
    in_specs = (
        (P("dp", None), P("dp", None), P("dp"), P("dp", None))
        + copy_specs
        + tuple(spec for spec in matrix_specs for _ in range(3))
        + vector_specs
    )
    out_specs = (P("dp", None), P("dp", None))
    for spec, copied in zip(matrix_specs, copy_specs):
        out_specs += (spec,) * 3 + (copied,)
    out_specs += vector_specs
    return jax.shard_map(
        partial(local, mesh.shape["dp"]),
        mesh=mesh,
        in_specs=in_specs,
        out_specs=out_specs,
        check_vma=False,
    )
```

time: 457 us -> 321 us (0.70); the launches traced: 450 us -> 319 us
  Pallas kernels: 0 us -> 159 us
  matrix products: 143 us -> 0 us
  local copies, waits for them, and re-layouts: 78.6 us -> 21.1 us
  waiting for transfers between devices: 97 us -> 49.4 us
  other arithmetic: 65.3 us -> 29.5 us
    pallas_call x0 -> x15, Pallas kernels: none -> 159 us  [the longest x2 37.1 us: ffn_bwd(): pl.pallas_call(with_deps(partial(ffn_bwd_kernel, final, n_dp), 1, 9, deps...]
    dot_general x22 -> x0, matrix products: 143 us -> none  [the longest x1 35.3 us: local(): jnp.dot(hidden_low, expand_all, preferred_element_type=WIDE)]
    ppermute x52 -> x46, waiting for transfers between devices: 97 us -> 46.1 us  [across(): return lax.ppermute(value, 'dp', [(i, i ^ apart) for i in range(count)])]
    unnamed x190 -> x133, local copies, waits for them, and re-layouts: 25.4 us -> 4.61 us
    convert_element_type x32 -> x10, other arithmetic: 30.7 us -> 12 us  [the longest x5 6.46 us: scatter_flow(): to_x, to_y = (part(every, 1, 0).astype(LOW), part(1, every, 1).astype(LOW))]
    another operation x22 -> x1, local copies, waits for them, and re-layouts: 9.8 us -> 0.02 us  [triple_then(): share = jnp.stack([share[:, j * own:(j + 1) * own] for j in range(3)])]
    slice x31 -> x15, local copies, waits for them, and re-layouts: 15.1 us -> 5.89 us  [the longest x2 2.56 us: local(): vector_total = jnp.stack([vector_sum[i] for i in (0, 8, 1, 2, 9, 10)])]
    reduce_sum x6 -> x1, other arithmetic: 10.6 us -> 1.51 us  [local(): pair_grad = jnp.sum(sums_pair, axis=0)[:2]]
  transfers between devices with their start and end apart: 63 -> 59, of which waited for: 29 -> 16; matrix products, arithmetic and copies ran while one was open for 37% -> 13% of each run, Pallas kernels for 0% -> 37%
where the time goes in v2:
time: 321 us; the launch traced here: 319 us
  Pallas kernels  159 us (50%)
  starting transfers between devices  58.7 us (18%)
  waiting for transfers between devices  49.4 us (15%)
  other arithmetic  29.5 us (9%)
  local copies, waits for them, and re-layouts  21.1 us (7%)
    ppermute x46, starting transfers between devices, across(): return lax.ppermute(value, 'dp', [(i, i ^ apart) for i in range(count)])  56.3 us
    ppermute x46, waiting for transfers between devices, across(): return lax.ppermute(value, 'dp', [(i, i ^ apart) for i in range(count)])  46.1 us
    pallas_call x2, Pallas kernels, ffn_bwd(): pl.pallas_call(with_deps(partial(ffn_bwd_kernel, final, n_dp), 1, 9, deps...  37.1 us
    pallas_call x4, Pallas kernels, weight_grad(): pl.pallas_call(with_deps(partial(weight_kernel, n_dp), 1, 2, deps), out_s...  26.3 us
    pallas_call x1, Pallas kernels, ffn_fwd(): pl.pallas_call(ffn_fwd_kernel, out_shape=(jax.ShapeDtypeStruct((tokens, 2...  24.7 us
    pallas_call x1, Pallas kernels, attend(): pl.pallas_call(attend_kernel, out_shape=(jax.ShapeDtypeStruct((tokens, 6...  18.8 us
    pallas_call x1, Pallas kernels, attend_back(): pl.pallas_call(with_deps(attend_back_kernel, 0, 5, deps), out_shape=(jax....  16.6 us
    pallas_call x3, Pallas kernels, gather_place(): pl.pallas_call(with_deps(partial(gather_kernel, n_dp, steps, wide), 1, 5,...  15.5 us
  transfers between devices with their start and end apart: 59, of which 16 were waited for; matrix products, arithmetic and copies ran while one was open for 13% of the time, Pallas kernels for 37%

profile of v2, /device:TPU:0, one launch (start us, length us, event | category | flops | bytes accessed | tf_op | source)
XLA Modules:
  0.0 319.1 jit_solution(16275952233613288781)
XLA Ops:
  2.4 3.1 collective-permute-done.2.p1_ref
  7.2 18.8 %attend.1 = (bf16[1024,2304]{1,0:T(8,128)(2,1)}, bf16[4,12,256,256]{3,2,1,0:T(8,128)(2,1)}, bf16[1024,768]{1,0:T(8,128)(2,1)}, f32[1024,768]{1,0:T(8,128)}) custom-call(s32[2]{0:T(128)} %pad_add_fusion.place.core.refs_0_, s32[8]{0:T(128)} %lengths.1, bf16[2048,768]{1,0:T(8,128)(2,1)} %refs_1_.3, s32[8,256]{1,0:T(8,128)} %mask_ref.1, ...), custom_call_target="tpu_custom_call" | custom-call | flops 8000000000 | bytes 25000000 | tf_op jit(solution)/shard_map/attend/pallas_call | solution.py:153
  27.5 24.7 %ffn_fwd.1 = (bf16[1024,3072]{1,0:T(8,128)(2,1)}, bf16[1024,3072]{1,0:T(8,128)(2,1)}, bf16[1024,768]{1,0:T(8,128)(2,1)}, f32[1024,768]{1,0:T(8,128)}, bf16[1024,...) custom-call(s32[2]{0:T(128)} %pad_add_fusion.place.core.refs_0_, ...), custom_call_target="tpu_custom_call" | custom-call | flops 11000000512 | bytes 40000000 | tf_op jit(solution)/shard_map/ffn_fwd/pallas_call | solution.py:252
  52.2 6.8 %weight_grad.4.refs_3_ = bf16[768,1536]{1,0:T(8,128)(2,1)} custom-call(s32[2]{0:T(128)} %pad_add_fusion.place.core.refs_0_, bf16[1024,768]{1,0:T(8,128)(2,1)} %get-tuple-element.105.refs_1_, bf16[1024,3072]{1,0:T(8,128)(2,1)} %get-tuple-element.110.refs_2_), custom_call_target="tpu_custom_call" | custom-call | flops 2415919104 | bytes 6000000 | tf_op jit(solution)/shard_map/weight_grad/pallas_call | solution.py:336
  59.2 6.9 %weight_grad.5 = bf16[768,1536]{1,0:T(8,128)(2,1)} custom-call(s32[2]{0:T(128)} %pad_add_fusion.place.core.refs_0_, bf16[1024,768]{1,0:T(8,128)(2,1)} %get-tuple-element.105.refs_1_, bf16[1024,3072]{1,0:T(8,128)(2,1)} %get-tuple-element.110.refs_2_, bf16[768,1536]{1,0:T(8,128)(2,1)} %weight_grad.4.refs_3_), custom_call_target="tpu_custom_call" | custom-call | flops 2415919104 | bytes 6000000 | tf_op jit(solution)/shard_map/weight_grad/pallas_call | solution.py:336
  70.2 2.9 collective-permute-start.9
  74.6 15.3 %ffn_bwd.2 = (bf16[768,1536]{1,0:T(8,128)(2,1)}, f32[1,1536]{1,0:T(1,128)}, f32[1024,768]{1,0:T(8,128)}) custom-call(s32[2]{0:T(128)} %pad_add_fusion.place.core.refs_0_, bf16[1024,768]{1,0:T(8,128)(2,1)} %get-tuple-element.105.refs_1_, bf16[1024,3072]{1,0:T(8,128)(2,1)} %get-tuple-element.106.refs_2_, bf16[768,1536]{1,0:T(8,128)(2,1)} %copy-done.61, ...), custom_call_target="tpu_custom_call" | custom-call | flops 8000000000 | bytes 20000000 | tf_op jit(solution)/shard_map/ffn_bwd/pallas_call | solution.py:445
  91.6 21.8 %ffn_bwd.3 = (bf16[768,1920]{1,0:T(8,128)(2,1)}, f32[1,1536]{1,0:T(1,128)}, f32[1024,768]{1,0:T(8,128)}, bf16[1024,768]{1,0:T(8,128)(2,1)}, f32[8,768]{1,0:T(8,128)}, /*index=5*/bf16[768,384]{1,0:T(8,128)(2,1)}) custom-call(s32[2]{0:T(128)} %pad_add_fusion.place.core.refs_0_, bf16[1024,768]{1,0:T(8,128)(2,1)} %get-tuple-element.105.refs_1_, ...), custom_call_target="tpu_custom_call" | custom-call | flops 8000000000 | bytes 20000000 | tf_op jit(solution)/shard_map/ffn_bwd/pallas_call | solution.py:445
  115.2 3.0 collective-permute-start.15
  126.5 16.6 %attend_back.1 = (bf16[1024,2304]{1,0:T(8,128)(2,1)}, f32[4,8,768]{2,1,0:T(8,128)}) custom-call(bf16[1024,768]{1,0:T(8,128)(2,1)} %get-tuple-element.115.refs_0_, bf16[4,12,256,256]{3,2,1,0:T(8,128)(2,1)} %get-tuple-element.116.refs_1_, bf16[1024,2304]{1,0:T(8,128)(2,1)} %get-tuple-element.117.refs_2_, bf16[384,768]{1,0:T(8,128)(2,1)} %refs_3_.3, ...), custom_call_target="tpu_custom_call" | custom-call | flops 12000000000 | bytes 20000000 | tf_op jit(solution)/shard_map/attend_back/pallas_call | solution.py:530
  148.7 6.4 %weight_grad.6.refs_3_ = bf16[768,1152]{1,0:T(8,128)(2,1)} custom-call(s32[2]{0:T(128)} %pad_add_fusion.place.core.refs_0_, bf16[2048,768]{1,0:T(8,128)(2,1)} %refs_1_.3, bf16[1024,2304]{1,0:T(8,128)(2,1)} %get-tuple-element.124.refs_2_.refs_1_, bf16[48,1536]{1,0:T(8,128)(2,1)} %get-tuple-element.192.refs_3_, bf16[96,1920]{1,0:T(8,128)(2,1)} %get-tuple-element.205.refs_4_, ...), custom_call_target="tpu_custom_call" | custom-call | flops 1811939328 | bytes 6000000 | tf_op jit(solution)/shard_map/weight_grad/pallas_call | solution.py:336
  157.9 6.2 %weight_grad.7 = bf16[768,1152]{1,0:T(8,128)(2,1)} custom-call(s32[2]{0:T(128)} %pad_add_fusion.place.core.refs_0_, bf16[2048,768]{1,0:T(8,128)(2,1)} %refs_1_.3, bf16[1024,2304]{1,0:T(8,128)(2,1)} %get-tuple-element.124.refs_2_.refs_1_, bf16[768,1152]{1,0:T(8,128)(2,1)} %weight_grad.6.refs_3_), custom_call_target="tpu_custom_call" | custom-call | flops 1811939328 | bytes 6000000 | tf_op jit(solution)/shard_map/weight_grad/pallas_call | solution.py:336
  174.5 10.7 %input_side.1 = (bf16[1024,768]{1,0:T(8,128)(2,1)}, f32[2048,768]{1,0:T(8,128)}) custom-call(s32[2]{0:T(128)} %pad_add_fusion.place.core.refs_0_, bf16[1024,2304]{1,0:T(8,128)(2,1)} %get-tuple-element.124.refs_2_.refs_1_, bf16[3,768,384]{2,1,0:T(8,128)(2,1)} %refs_2_.1, bf16[3,768,384]{2,1,0:T(8,128)(2,1)} %collective-permute-done.w1_ref.refs_3_, ...), custom_call_target="tpu_custom_call" | custom-call | flops 4000000000 | bytes 14000000 | tf_op jit(solution)/shard_map/input_side/pallas_call | solution.py:578
  190.5 3.5 %collective-permute-done.35 = bf16[48,1536]{1,0:T(8,128)(2,1)S(1)} collective-permute-done((bf16[48,1536]{1,0:T(8,128)(2,1)S(1)}, bf16[48,1536]{1,0:T(8,128)(2,1)S(1)}, u32[]{:S(2)}, u32[]{:S(2)}) %collective-permute-start.35) | collective-permute-done | bytes 147488 | tf_op jit(solution)/shard_map/ppermute | solution.py:710
  195.1 11.6 %collective-permute-done.43 = bf16[48,1920]{1,0:T(8,128)(2,1)S(1)} collective-permute-done((bf16[48,1920]{1,0:T(8,128)(2,1)S(1)}, bf16[48,1920]{1,0:T(8,128)(2,1)S(1)}, u32[]{:S(2)}, u32[]{:S(2)}) %collective-permute-start.43) | collective-permute-done | bytes 184352 | tf_op jit(solution)/shard_map/ppermute | solution.py:710
  212.8 4.2 %put_other.2 = bf16[2048,768]{1,0:T(8,128)(2,1)} custom-call(s32[2]{0:T(128)} %pad_add_fusion.place.core.refs_0_, bf16[1024,768]{1,0:T(8,128)(2,1)} %collective-permute-done.6.refs_1_, bf16[2048,768]{1,0:T(8,128)(2,1)} %get-tuple-element.104.refs_2_, bf16[96,1152]{1,0:T(8,128)(2,1)} %copy-done.18, ...), custom_call_target="tpu_custom_call", output_to_operand_aliasing={{}: (2, {})} | custom-call | bytes 3145728 | tf_op jit(solution)/shard_map/put_other/pallas_call | solution.py:606
  227.6 3.3 %concatenate.75 = f32[24,768]{1,0:T(8,128)} concatenate(f32[8,768]{1,0:T(8,128)} %get-tuple-element.118, f32[8,768]{1,0:T(8,128)} %get-tuple-element.163, f32[1,768]{1,0:T(1,128)S(1)} %bitcast.247, f32[2,768]{1,0:T(2,128)S(1)} %reshape.233, f32[5,768]{1,0:T(8,128)S(1)} %broadcast_in_dim.7), dimensions={0} | concatenate | bytes 147456 | tf_op jit(solution)/shard_map/concatenate | solution.py:937
  235.6 4.7 %put_other.3 = f32[2048,768]{1,0:T(8,128)} custom-call(s32[2]{0:T(128)} %pad_add_fusion.place.core.refs_0_, bf16[1024,768]{1,0:T(8,128)(2,1)} %collective-permute-done.24.refs_1_, f32[2048,768]{1,0:T(8,128)} %get-tuple-element.137.refs_2_, bf16[48,1152]{1,0:T(8,128)(2,1)} %copy-done.23, bf16[48,1152]{1,0:T(8,128)(2,1)} %copy-done.22, ...), custom_call_target="tpu_custom_call", output_to_operand_aliasing={{}: (2, {})} | custom-call | bytes 3145728 | tf_op jit(solution)/shard_map/put_other/pallas_call | solution.py:606
  258.8 5.1 %gather_place.3 = bf16[1536,768]{1,0:T(8,128)(2,1)} custom-call(s32[2]{0:T(128)} %pad_add_fusion.place.core.refs_0_, bf16[192,1536]{1,0:T(8,128)(2,1)} %copy-done.5, bf16[192,1536]{1,0:T(8,128)(2,1)} %copy-done.11, bf16[192,1536]{1,0:T(8,128)(2,1)} %collective-permute-done.37.refs_3_, bf16[96,1536]{1,0:T(8,128)(2,1)} %copy-done.33, ...), custom_call_target="tpu_custom_call" | custom-call | bytes 4718592 | tf_op jit(solution)/shard_map/gather_place/pallas_call | solution.py:689
  265.0 10.1 %collective-permute-done.56 = f32[24,768]{1,0:T(8,128)S(1)} collective-permute-done((f32[24,768]{1,0:T(8,128)S(1)}, f32[24,768]{1,0:T(8,128)S(1)}, u32[]{:S(2)}, u32[]{:S(2)}) %collective-permute-start.56) | collective-permute-done | bytes 73760 | tf_op jit(solution)/shard_map/ppermute | solution.py:710
  276.5 3.2 collective-permute-done.57
  301.2 6.1 %gather_place.4 = (bf16[768,1536]{1,0:T(8,128)(2,1)}, bf16[384,768]{1,0:T(8,128)(2,1)}) custom-call(s32[2]{0:T(128)} %pad_add_fusion.place.core.refs_0_, bf16[192,1920]{1,0:T(8,128)(2,1)} %copy-done.4, bf16[192,1920]{1,0:T(8,128)(2,1)} %copy-done.7, bf16[192,1920]{1,0:T(8,128)(2,1)} %copy-done.8, bf16[96,1920]{1,0:T(8,128)(2,1)} %copy-done.27, ...), custom_call_target="tpu_custom_call" | custom-call | bytes 5898240 | tf_op jit(solution)/shard_map/gather_place/pallas_call | solution.py:689
  310.0 3.4 %collective-permute-done.52.refs_4_ = bf16[288,384]{1,0:T(8,128)(2,1)S(1)} collective-permute-done((bf16[288,384]{1,0:T(8,128)(2,1)S(1)}, bf16[288,384]{1,0:T(8,128)(2,1)S(1)}, u32[]{:S(2)}, u32[]{:S(2)}) %collective-permute-start.52) | collective-permute-done | bytes 221216 | tf_op jit(solution)/shard_map/ppermute | solution.py:710
  314.8 4.3 %gather_place.5 = bf16[3,768,384]{2,1,0:T(8,128)(2,1)} custom-call(s32[2]{0:T(128)} %pad_add_fusion.place.core.refs_0_, bf16[576,384]{1,0:T(8,128)(2,1)} %copy-done.2, bf16[576,384]{1,0:T(8,128)(2,1)} %copy-done.15, bf16[576,384]{1,0:T(8,128)(2,1)} %copy-done.16, bf16[288,384]{1,0:T(8,128)(2,1)} %copy-done.40, bf16[288,384]{1,0:T(8,128)(2,1)} %copy-done.41), custom_call_target="tpu_custom_call" | custom-call | bytes 3538944 | tf_op jit(solution)/shard_map/gather_place/pallas_call | solution.py:689
  (305 shorter events, 114.5 us)
Async XLA Ops:
  5.7 20.4 %collective-permute-start.3 = (bf16[768,1536]{1,0:T(8,128)(2,1)}, bf16[768,1536]{1,0:T(8,128)(2,1)S(1)}, u32[]{:S(2)}, u32[]{:S(2)}) collective-permute-start(bf16[768,1536]{1,0:T(8,128)(2,1)} %refs_3_.2), channel_id=1, source_target_pairs={{0,1},{1,0},{2,3},{3,2},{4,5},{5,4},{6,7},{7,6},{8,9},{9,8},{10,11... | collective-permute-start | bytes 7077896 | tf_op jit(solution)/shard_map/ppermute | solution.py:706
  6.1 20.0 %collective-permute-start.4 = (bf16[1536,768]{1,0:T(8,128)(2,1)}, bf16[1536,768]{1,0:T(8,128)(2,1)}, u32[]{:S(2)}, u32[]{:S(2)}) collective-permute-start(bf16[1536,768]{1,0:T(8,128)(2,1)} %refs_4_.1), channel_id=1, source_target_pairs={{0,1},{1,0},{2,3},{3,2},{4,5},{5,4},{6,7},{7,6},{8,9},{9,8},{10,11... | collective-permute-start | bytes 7077896 | tf_op jit(solution)/shard_map/ppermute | solution.py:706
  6.8 19.2 %collective-permute-start.5 = (f32[1,1536]{1,0:T(1,128)S(1)}, f32[1,1536]{1,0:T(1,128)S(1)}, u32[]{:S(2)}, u32[]{:S(2)}) collective-permute-start(f32[1,1536]{1,0:T(1,128)S(1)} %broadcast_in_dim.6.b0_ref), channel_id=1, source_target_pairs={{0,1},{1,0},{2,3},{3,2},{4,5},{5,4},{6,7},{7,6},{8,9},{9,8},{10,11... | collective-permute-start | bytes 18440 | tf_op jit(solution)/shard_map/ppermute | solution.py:706
  70.2 19.8 %collective-permute-start.9 = (bf16[2,96,1536]{2,1,0:T(8,128)(2,1)}, bf16[2,96,1536]{2,1,0:T(8,128)(2,1)S(1)}, u32[]{:S(2)}, u32[]{:S(2)}) collective-permute-start(bf16[2,96,1536]{2,1,0:T(8,128)(2,1)} %fusion.8.refs_11_), channel_id=1, source_target_pairs={{0,4},{2,6},{4,0},{6,2},{8,12},{10,14},{12,8},{14,10},{16,20},{18,... | collective-permute-start | bytes 1769480 | tf_op jit(solution)/shard_map/ppermute | solution.py:710
  89.9 29.9 %collective-permute-start.12 = (bf16[768,1536]{1,0:T(8,128)(2,1)}, bf16[768,1536]{1,0:T(8,128)(2,1)}, u32[]{:S(2)}, u32[]{:S(2)}) collective-permute-start(bf16[768,1536]{1,0:T(8,128)(2,1)} %get-tuple-element.122), channel_id=1, source_target_pairs={{0,1},{1,0},{2,3},{3,2},{4,5},{5,4},{6,7},{7,6},{8,9},{9,8},{10,11... | collective-permute-start | bytes 7077896 | tf_op jit(solution)/shard_map/ppermute | solution.py:706
  91.1 22.7 %collective-permute-start.10 = (bf16[96,1536]{1,0:T(8,128)(2,1)}, bf16[96,1536]{1,0:T(8,128)(2,1)S(1)}, u32[]{:S(2)}, u32[]{:S(2)}) collective-permute-start(bf16[96,1536]{1,0:T(8,128)(2,1)} %get-tuple-element.197.refs_10_), channel_id=1, source_target_pairs={{0,2},{2,0},{4,6},{6,4},{8,10},{10,8},{12,14},{14,12},{16,18},{18,... | collective-permute-start | bytes 884744 | tf_op jit(solution)/shard_map/ppermute | solution.py:710
  91.6 22.1 %collective-permute-start.11 = (bf16[96,1536]{1,0:T(8,128)(2,1)}, bf16[96,1536]{1,0:T(8,128)(2,1)}, u32[]{:S(2)}, u32[]{:S(2)}) collective-permute-start(bf16[96,1536]{1,0:T(8,128)(2,1)} %get-tuple-element.196.refs_11_), channel_id=1, source_target_pairs={{0,4},{2,6},{4,0},{6,2},{8,12},{10,14},{12,8},{14,10},{16,20},{18,... | collective-permute-start | bytes 884744 | tf_op jit(solution)/shard_map/ppermute | solution.py:710
  115.2 28.0 %collective-permute-start.15 = (bf16[48,1536]{1,0:T(8,128)(2,1)S(1)}, bf16[48,1536]{1,0:T(8,128)(2,1)S(1)}, u32[]{:S(2)}, u32[]{:S(2)}) collective-permute-start(bf16[48,1536]{1,0:T(8,128)(2,1)S(1)} %get-tuple-element.222.refs_6_), channel_id=1, source_target_pairs={{0,16},{2,18},{4,20},{6,22},{8,24},{10,26},{12,28},{14,30},{16,0},... | collective-permute-start | bytes 442376 | tf_op jit(solution)/shard_map/ppermute | solution.py:710
  118.2 25.0 %collective-permute-start.16 = (bf16[48,1536]{1,0:T(8,128)(2,1)S(1)}, bf16[48,1536]{1,0:T(8,128)(2,1)S(1)}, u32[]{:S(2)}, u32[]{:S(2)}) collective-permute-start(bf16[48,1536]{1,0:T(8,128)(2,1)S(1)} %get-tuple-element.221.refs_7_), channel_id=1, source_target_pairs={{0,24},{2,26},{4,28},{6,30},{8,16},{10,18},{12,20},{14,22},{16,8},... | collective-permute-start | bytes 442376 | tf_op jit(solution)/shard_map/ppermute | solution.py:710
  119.5 23.7 %collective-permute-start.14 = (bf16[48,1536]{1,0:T(8,128)(2,1)S(1)}, bf16[48,1536]{1,0:T(8,128)(2,1)S(1)}, u32[]{:S(2)}, u32[]{:S(2)}) collective-permute-start(bf16[48,1536]{1,0:T(8,128)(2,1)S(1)} %slice.564.refs_5_), channel_id=1, source_target_pairs={{0,8},{2,10},{4,12},{6,14},{8,0},{10,2},{12,4},{14,6},{16,24},{18,... | collective-permute-start | bytes 442376 | tf_op jit(solution)/shard_map/ppermute | solution.py:710
  123.5 22.9 %collective-permute-start.17 = (bf16[2,96,1920]{2,1,0:T(8,128)(2,1)}, bf16[2,96,1920]{2,1,0:T(8,128)(2,1)}, u32[]{:S(2)}, u32[]{:S(2)}) collective-permute-start(bf16[2,96,1920]{2,1,0:T(8,128)(2,1)} %get-tuple-element.207.refs_8_), channel_id=1, source_target_pairs={{0,2},{2,0},{4,6},{6,4},{8,10},{10,8},{12,14},{14,12},{16,18},{18,... | collective-permute-start | bytes 2211848 | tf_op jit(solution)/shard_map/ppermute | solution.py:710
  125.0 21.5 %collective-permute-start.18 = (bf16[2,96,1920]{2,1,0:T(8,128)(2,1)S(1)}, bf16[2,96,1920]{2,1,0:T(8,128)(2,1)}, u32[]{:S(2)}, u32[]{:S(2)}) collective-permute-start(bf16[2,96,1920]{2,1,0:T(8,128)(2,1)S(1)} %get-tuple-element.206.refs_9_), channel_id=1, source_target_pairs={{0,4},{2,6},{4,0},{6,2},{8,12},{10,14},{12,8},{14,10},{16,20},{18,... | collective-permute-start | bytes 2211848 | tf_op jit(solution)/shard_map/ppermute | solution.py:710
  156.1 56.1 %collective-permute-start.6 = (bf16[1024,768]{1,0:T(8,128)(2,1)}, bf16[1024,768]{1,0:T(8,128)(2,1)}, u32[]{:S(2)}, u32[]{:S(2)}) collective-permute-start(bf16[1024,768]{1,0:T(8,128)(2,1)} %get-tuple-element.103), channel_id=1, source_target_pairs={{0,1},{1,0},{2,3},{3,2},{4,5},{5,4},{6,7},{7,6},{8,9},{9,8},{10,11... | collective-permute-start | bytes 4718600 | tf_op jit(solution)/shard_map/ppermute | solution.py:706
  156.1 31.6 %collective-permute-start.33 = (bf16[48,1536]{1,0:T(8,128)(2,1)S(1)}, bf16[48,1536]{1,0:T(8,128)(2,1)}, u32[]{:S(2)}, u32[]{:S(2)}) collective-permute-start(bf16[48,1536]{1,0:T(8,128)(2,1)S(1)} %copy-done.12), channel_id=1, source_target_pairs={{0,8},{2,10},{4,12},{6,14},{8,0},{10,2},{12,4},{14,6},{16,24},{18,... | collective-permute-start | bytes 442376 | tf_op jit(solution)/shard_map/ppermute | solution.py:710
  166.1 23.7 %collective-permute-start.34 = (bf16[48,1536]{1,0:T(8,128)(2,1)S(1)}, bf16[48,1536]{1,0:T(8,128)(2,1)}, u32[]{:S(2)}, u32[]{:S(2)}) collective-permute-start(bf16[48,1536]{1,0:T(8,128)(2,1)S(1)} %copy-done.12), channel_id=1, source_target_pairs={{0,16},{2,18},{4,20},{6,22},{8,24},{10,26},{12,28},{14,30},{16,0},... | collective-permute-start | bytes 442376 | tf_op jit(solution)/shard_map/ppermute | solution.py:710
  186.7 20.1 %collective-permute-start.43 = (bf16[48,1920]{1,0:T(8,128)(2,1)S(1)}, bf16[48,1920]{1,0:T(8,128)(2,1)S(1)}, u32[]{:S(2)}, u32[]{:S(2)}) collective-permute-start(bf16[48,1920]{1,0:T(8,128)(2,1)S(1)} %copy-done.44), channel_id=1, source_target_pairs={{0,16},{2,18},{4,20},{6,22},{8,24},{10,26},{12,28},{14,30},{16,0},... | collective-permute-start | bytes 552968 | tf_op jit(solution)/shard_map/ppermute | solution.py:710
  187.7 20.5 %collective-permute-start.44 = (bf16[48,1920]{1,0:T(8,128)(2,1)S(1)}, bf16[48,1920]{1,0:T(8,128)(2,1)S(1)}, u32[]{:S(2)}, u32[]{:S(2)}) collective-permute-start(bf16[48,1920]{1,0:T(8,128)(2,1)S(1)} %copy-done.43), channel_id=1, source_target_pairs={{0,24},{2,26},{4,28},{6,30},{8,16},{10,18},{12,20},{14,22},{16,8},... | collective-permute-start | bytes 552968 | tf_op jit(solution)/shard_map/ppermute | solution.py:710
  189.8 20.0 %collective-permute-start.42 = (bf16[48,1920]{1,0:T(8,128)(2,1)S(1)}, bf16[48,1920]{1,0:T(8,128)(2,1)S(1)}, u32[]{:S(2)}, u32[]{:S(2)}) collective-permute-start(bf16[48,1920]{1,0:T(8,128)(2,1)S(1)} %copy-done.42), channel_id=1, source_target_pairs={{0,8},{2,10},{4,12},{6,14},{8,0},{10,2},{12,4},{14,6},{16,24},{18,... | collective-permute-start | bytes 552968 | tf_op jit(solution)/shard_map/ppermute | solution.py:710
  194.0 41.4 %collective-permute-start.24 = (bf16[1024,768]{1,0:T(8,128)(2,1)}, bf16[1024,768]{1,0:T(8,128)(2,1)}, u32[]{:S(2)}, u32[]{:S(2)}) collective-permute-start(bf16[1024,768]{1,0:T(8,128)(2,1)} %get-tuple-element.134), channel_id=1, source_target_pairs={{0,1},{1,0},{2,3},{3,2},{4,5},{5,4},{6,7},{7,6},{8,9},{9,8},{10,11... | collective-permute-start | bytes 4718600 | tf_op jit(solution)/shard_map/ppermute | solution.py:706
  212.3 20.1 %collective-permute-start.37 = (bf16[192,1536]{1,0:T(8,128)(2,1)S(1)}, bf16[192,1536]{1,0:T(8,128)(2,1)}, u32[]{:S(2)}, u32[]{:S(2)}) collective-permute-start(bf16[192,1536]{1,0:T(8,128)(2,1)S(1)} %pad_maximum_fusion.1.refs_1_), channel_id=1, source_target_pairs={{0,4},{2,6},{4,0},{6,2},{8,12},{10,14},{12,8},{14,10},{16,20},{18,... | collective-permute-start | bytes 1769480 | tf_op jit(solution)/shard_map/ppermute | solution.py:710
  254.5 35.7 %collective-permute-start.48 = (bf16[192,1920]{1,0:T(8,128)(2,1)S(1)}, bf16[192,1920]{1,0:T(8,128)(2,1)S(1)}, u32[]{:S(2)}, u32[]{:S(2)}) collective-permute-start(bf16[192,1920]{1,0:T(8,128)(2,1)S(1)} %pad_maximum_fusion.refs_1_), channel_id=1, source_target_pairs={{0,2},{2,0},{4,6},{6,4},{8,10},{10,8},{12,14},{14,12},{16,18},{18,... | collective-permute-start | bytes 2211848 | tf_op jit(solution)/shard_map/ppermute | solution.py:710
  256.7 33.5 %collective-permute-start.49 = (bf16[192,1920]{1,0:T(8,128)(2,1)S(1)}, bf16[192,1920]{1,0:T(8,128)(2,1)S(1)}, u32[]{:S(2)}, u32[]{:S(2)}) collective-permute-start(bf16[192,1920]{1,0:T(8,128)(2,1)S(1)} %pad_maximum_fusion.refs_1_), channel_id=1, source_target_pairs={{0,4},{2,6},{4,0},{6,2},{8,12},{10,14},{12,8},{14,10},{16,20},{18,... | collective-permute-start | bytes 2211848 | tf_op jit(solution)/shard_map/ppermute | solution.py:710
  281.7 25.6 %collective-permute-start.40 = (bf16[576,384]{1,0:T(8,128)(2,1)S(1)}, bf16[576,384]{1,0:T(8,128)(2,1)S(1)}, u32[]{:S(2)}, u32[]{:S(2)}) collective-permute-start(bf16[576,384]{1,0:T(8,128)(2,1)S(1)} %pad_maximum_fusion.2.refs_6_.refs_1_), channel_id=1, source_target_pairs={{0,2},{2,0},{4,6},{6,4},{8,10},{10,8},{12,14},{14,12},{16,18},{18,... | collective-permute-start | bytes 1327112 | tf_op jit(solution)/shard_map/ppermute | solution.py:710
  281.9 25.4 %collective-permute-start.41 = (bf16[576,384]{1,0:T(8,128)(2,1)S(1)}, bf16[576,384]{1,0:T(8,128)(2,1)S(1)}, u32[]{:S(2)}, u32[]{:S(2)}) collective-permute-start(bf16[576,384]{1,0:T(8,128)(2,1)S(1)} %pad_maximum_fusion.2.refs_6_.refs_1_), channel_id=1, source_target_pairs={{0,4},{2,6},{4,0},{6,2},{8,12},{10,14},{12,8},{14,10},{16,20},{18,... | collective-permute-start | bytes 1327112 | tf_op jit(solution)/shard_map/ppermute | solution.py:710
  (100 other events, 1080.0 us)

commit v3 on v2

--- a/solution.py
+++ b/solution.py
@@ -22,18 +22,10 @@
 WIDE = jnp.float32
 
 
-def adamw_step(master, first_moment, second_moment, gradient, decay_rate):
-    first_new = FIRST_DECAY * first_moment + (1.0 - FIRST_DECAY) * gradient
-    second_new = SECOND_DECAY * second_moment + (1.0 - SECOND_DECAY) * gradient * gradient
-    first_fixed = first_new / (1.0 - FIRST_DECAY**STEP)
-    second_fixed = second_new / (1.0 - SECOND_DECAY**STEP)
-    direction = first_fixed / (jnp.sqrt(second_fixed) + EPSILON)
-    master_new = master - LEARN_RATE * (direction + decay_rate * master)
-    return (master_new, first_new, second_new)
-
-
 BLOCK_FF = 512
-VMEM = pltpu.CompilerParams(vmem_limit_bytes=58 * 2**20)
+NO_COST = pl.CostEstimate(flops=0, bytes_accessed=0, transcendentals=0)
+LONG = pl.CostEstimate(flops=5 * 10**10, bytes_accessed=10**8, transcendentals=0)
+VMEM = pltpu.CompilerParams(vmem_limit_bytes=64 * 2**20)
 ROOT_HALF = 0.7071067811865476
 BELL_TOP = 0.3989422804014327
 
@@ -175,7 +167,7 @@
         ),
         compiler_params=VMEM,
         name="attend",
-        cost_estimate=pl.CostEstimate(flops=8 * 10**9, bytes_accessed=25 * 10**6, transcendentals=3 * 10**6),
+        cost_estimate=LONG,
     )(place, lengths, hidden_in, key_mask, w0, w1, o0, o1, p0, p1, nv)
 
 
@@ -289,8 +281,19 @@
         ),
         compiler_params=VMEM,
         name="ffn_fwd",
-        cost_estimate=pl.CostEstimate(flops=11 * 10**9, bytes_accessed=40 * 10**6, transcendentals=4 * 10**6),
+        cost_estimate=LONG,
     )(core, pre, grad_out, e0, e1, c0, c1, b0, b1, nv)
+
+
+def reverse(value, count):
+    out = value & 0
+    for bit in range(count.bit_length() - 1):
+        out = out * 2 + ((value >> bit) & 1)
+    return out
+
+
+def spot(apart, count):
+    return (apart & 3) * (count // 4) + reverse(apart >> 2, count // 4)
 
 
 def place_rows(out_ref, value, rank, count, left=0):
@@ -300,8 +303,7 @@
         out_ref[:, cols] = value
         return
     for i in range(count):
-        apart = jnp.bitwise_xor(rank, i)
-        at = (apart & 3) * (count // 4) + (apart >> 2)
+        at = spot(jnp.bitwise_xor(rank, i), count)
         there = pl.ds(pl.multiple_of(at * rows, 16), rows)
         out_ref[there, cols] = value[i * rows : (i + 1) * rows]
 
@@ -310,9 +312,9 @@
     rows = grad.shape[0] // count
     if rows % 16 == 0:
         return grad
-    at = jnp.arange(count)
-    apart = (at // (count // 4)) | ((at % (count // 4)) << 2)
-    return grad.reshape(count, rows, -1)[apart ^ rank].reshape(grad.shape)
+    blocks = grad.reshape(count, rows, -1)
+    apart = jnp.arange(count)
+    return jnp.zeros_like(blocks).at[spot(apart ^ rank, count)].set(blocks).reshape(grad.shape)
 
 
 ANY = pl.BlockSpec(memory_space=pl.ANY)
@@ -348,9 +350,7 @@
         ),
         compiler_params=VMEM,
         name="weight_grad",
-        cost_estimate=pl.CostEstimate(
-            flops=2 * d * tokens * count * block, bytes_accessed=6 * 10**6, transcendentals=0
-        ),
+        cost_estimate=LONG,
     )(place, left, right, *deps)
     return placed(out, place[1], n_dp)
 
@@ -469,7 +469,7 @@
         ),
         compiler_params=VMEM,
         name="ffn_bwd",
-        cost_estimate=pl.CostEstimate(flops=8 * 10**9, bytes_accessed=20 * 10**6, transcendentals=0),
+        cost_estimate=LONG,
     )(place, low, slope, e, c, sofar, pre, hl, ctx, nv, *deps)
     out = list(out)
     for i in (0, 5) if final else (0,):
@@ -478,8 +478,13 @@
 
 
 def attend_back_kernel(
-    ag_ref, probs_ref, qkv_ref, o0_ref, o1_ref, grad_ref, sums_ref, dp_s, ds_s, cg_s
+    start, ag_ref, probs_ref, qkv_ref, o0_ref, o1_ref, sofar_ref, grad_ref, sums_ref,
+    dp_s, ds_s, cg_s,
 ):
+    @pl.when(pl.program_id(0) == 0)
+    def _():
+        sums_ref[...] = jnp.zeros_like(sums_ref) if start else sofar_ref[...]
+
     width = o0_ref.shape[0]
     pairs = width // 128
     scale = jnp.asarray(HEAD_DIM ** (-0.5), LOW)
@@ -498,7 +503,7 @@
             dv = (dv + dot(probs_ref[0, first + 2 * pair + 1], side(do, 1))).astype(LOW)
             grad_ref[:, at + 2 * width : at + 2 * width + 128] = dv
             to = half * width + 128 * pair
-            sums_ref[0, 1:2, to : to + 128] = col_sum(dv.astype(WIDE))
+            sums_ref[1:2, to : to + 128] += col_sum(dv.astype(WIDE))
         for head in range(2 * pairs):
             for left in range(0, ag_ref.shape[0], 128):
                 cols = slice(left, left + 128)
@@ -516,37 +521,37 @@
             grad_ref[:, at : at + 128] = dq
             grad_ref[:, at + width : at + width + 128] = dk.astype(LOW)
             to = half * width + 128 * pair
-            sums_ref[0, 0:1, to : to + 128] = col_sum(dq.astype(WIDE))
+            sums_ref[0:1, to : to + 128] += col_sum(dq.astype(WIDE))
 
 
 def attend_back(ag, probs, qkv, o0, o1, first, count, before=None, deps=()):
     seqs, heads, seq_len, _ = probs.shape
     tokens, d = ag.shape
     width = o0.shape[0]
-    full = lambda a: pl.BlockSpec(a.shape, lambda s: (0,) * a.ndim)
+    full = lambda shape: pl.BlockSpec(shape, lambda s: (0,) * len(shape))
     rows = lambda cols: pl.BlockSpec((seq_len, cols), lambda s: (first + s, 0))
-    if before is not None:
-        deps = tuple(before) + tuple(deps)
+    sums = (8, 2 * width)
+    start = before is None
+    if not start:
+        deps = (before[0],) + tuple(deps)
     return pl.pallas_call(
-        with_deps(attend_back_kernel, 0, 5, deps),
+        with_deps(partial(attend_back_kernel, start), 0, 6, deps),
         out_shape=(
             jax.ShapeDtypeStruct((tokens, 6 * width), LOW),
-            jax.ShapeDtypeStruct((seqs, 8, 2 * width), WIDE),
+            jax.ShapeDtypeStruct(sums, WIDE),
         ),
         grid=(count,),
         in_specs=[
             rows(d),
             pl.BlockSpec((1, heads, seq_len, seq_len), lambda s: (first + s, 0, 0, 0)),
             rows(6 * width),
-            full(o0),
-            full(o1),
+            full(o0.shape),
+            full(o1.shape),
+            ANY if start else full(sums),
         ]
         + [ANY] * len(deps),
-        out_specs=[
-            rows(6 * width),
-            pl.BlockSpec((1, 8, 2 * width), lambda s: (first + s, 0, 0)),
-        ],
-        input_output_aliases={} if before is None else {5: 0, 6: 1},
+        out_specs=[rows(6 * width), full(sums)],
+        input_output_aliases={} if start else {6: 0},
         scratch_shapes=[
             pltpu.VMEM((heads // 2, seq_len, seq_len), WIDE),
             pltpu.VMEM((heads // 2, seq_len, seq_len), LOW),
@@ -554,10 +559,8 @@
         ],
         compiler_params=VMEM,
         name="attend_back",
-        cost_estimate=pl.CostEstimate(
-            flops=3 * count * 10**9, bytes_accessed=5 * count * 10**6, transcendentals=0
-        ),
-    )(ag, probs, qkv, o0, o1, *deps)
+        cost_estimate=LONG,
+    )(ag, probs, qkv, o0, o1, ag if start else before[1], *deps)
 
 
 def input_kernel(place, grad_ref, w0_ref, w1_ref, one_ref, out_ref, whole_ref):
@@ -592,8 +595,229 @@
         ),
         compiler_params=VMEM,
         name="input_side",
-        cost_estimate=pl.CostEstimate(flops=4 * 10**9, bytes_accessed=14 * 10**6, transcendentals=0),
+        cost_estimate=LONG,
     )(place, grad, w0, w1, one, *deps)
+
+
+def bundle_kernel(one_ref, two_ref, pair_ref, b0_ref, b1_ref, mine_ref, theirs_ref):
+    half = pair_ref.shape[1] // 2
+    d = one_ref.shape[1]
+    for i, (ref, b_ref) in enumerate(((mine_ref, b0_ref), (theirs_ref, b1_ref))):
+        ref[...] = jnp.zeros_like(ref)
+        ref[0:8] = one_ref[...]
+        ref[8:16] = two_ref[...]
+        for j in range(2):
+            ref[16:17, j * half : (j + 1) * half] = pair_ref[j : j + 1, i * half : (i + 1) * half]
+        for j in range(b_ref.shape[1] // d):
+            ref[17 + j : 18 + j] = b_ref[:, j * d : (j + 1) * d]
+
+
+def bundle(one, two, pair, mine, theirs, deps=()):
+    out = jax.ShapeDtypeStruct((24, one.shape[1]), WIDE)
+    spec = lambda a: pl.BlockSpec(a.shape, lambda: (0, 0))
+    return pl.pallas_call(
+        with_deps(bundle_kernel, 0, 5, deps),
+        out_shape=(out, out),
+        in_specs=[spec(a) for a in (one, two, pair, mine, theirs)] + [ANY] * len(deps),
+        out_specs=(spec(out), spec(out)),
+        name="bundle",
+    )(one, two, pair, mine, theirs, *deps)
+
+
+def gather_kernel(count, layout, place, z_ref, x_ref, y_ref, da_ref, db_ref, *refs):
+    outs, scratch = refs[: len(layout)], list(refs[len(layout) :])
+    tos = [scratch.pop(0) if kind == "flip" else out for (kind, _, _), out in zip(layout, outs)]
+    block = z_ref.shape[0] // (count // 4)
+    for apart in range(count):
+        at = jnp.bitwise_xor(place[1], apart)
+        first = reverse(apart >> 2, count // 4) * block
+        ref = (z_ref, x_ref, y_ref, da_ref)[apart & 3]
+        if apart & 3 == 3 and first >= da_ref.shape[0]:
+            ref, first = db_ref, first - da_ref.shape[0]
+        for (kind, left, right), to in zip(layout, tos):
+            if kind == "deep":
+                rows = block // to.shape[0]
+                for i in range(to.shape[0]):
+                    here = slice(first + i * rows, first + i * rows + rows)
+                    to[i, pl.ds(pl.multiple_of(at * rows, 16), rows)] = ref[here]
+            else:
+                there = pl.ds(pl.multiple_of(at * block, 16), block)
+                to[there] = ref[first : first + block, left:right]
+    for (kind, _, _), out, to in zip(layout, outs, tos):
+        if kind == "flip":
+            out[...] = to[...].T
+
+
+def gather_place(place, n_dp, layout, z, x, y, da, db, deps=()):
+    rows, cols = z.shape[0] * 4, z.shape[1]
+    block = rows // n_dp
+    deep = [right - left for kind, left, right in layout if kind == "deep"]
+    shapes = []
+    for kind, left, right in layout:
+        wide = right - left
+        if kind == "deep":
+            shapes.append((wide // cols, rows * cols // wide, cols))
+        else:
+            shapes.append((wide, rows) if kind == "flip" else (rows, wide))
+    if (block // (shapes[0][0] if deep else 1)) % 16:
+        plane = jnp.stack([z, x, y, jnp.concatenate([da, db])])
+        blocks = plane.reshape(n_dp, block, cols)[spot(jnp.arange(n_dp) ^ place[1], n_dp)]
+        outs = []
+        for (kind, left, right), shape in zip(layout, shapes):
+            if kind == "deep":
+                outs.append(blocks.reshape(n_dp, shape[0], -1, cols).transpose(1, 0, 2, 3).reshape(shape))
+            else:
+                whole = blocks.reshape(rows, cols)[:, left:right]
+                outs.append(whole.T if kind == "flip" else whole)
+        return outs
+    spec = lambda a: pl.BlockSpec(a.shape, lambda s, c: (0, 0))
+    return pl.pallas_call(
+        with_deps(partial(gather_kernel, n_dp, layout), 1, 5, deps),
+        out_shape=[jax.ShapeDtypeStruct(shape, LOW) for shape in shapes],
+        grid_spec=pltpu.PrefetchScalarGridSpec(
+            num_scalar_prefetch=1,
+            grid=(1,),
+            in_specs=[spec(a) for a in (z, x, y, da, db)] + [ANY] * len(deps),
+            out_specs=[pl.BlockSpec(s, lambda i, c, n=len(s): (0,) * n) for s in shapes],
+            scratch_shapes=[
+                pltpu.VMEM(shape[::-1], LOW)
+                for (kind, _, _), shape in zip(layout, shapes)
+                if kind == "flip"
+            ],
+        ),
+        compiler_params=VMEM,
+        name="gather_place",
+        cost_estimate=LONG,
+    )(place, z, x, y, da, db, *deps)
+
+
+def combine_kernel(plan, *refs):
+    outs = refs[len(refs) - len(plan) :]
+    for parts, out in zip(plan, outs):
+        rows = out.shape[0] // len(parts)
+        for i, terms in enumerate(parts):
+            sides = []
+            for inputs in terms:
+                pieces = [refs[r][...].astype(WIDE) for r in inputs]
+                sides.append(pieces[0] if not pieces[1:] else jnp.concatenate(pieces, axis=1))
+            out[i * rows : (i + 1) * rows] = sum(sides[1:], sides[0]).astype(LOW)
+
+
+def cut(terms, rows):
+    take = lambda a, n: a[n * rows : (n + 1) * rows].astype(WIDE)
+    sides = [jnp.concatenate([take(a, n) for a, n in term], axis=1) for term in terms]
+    return sum(sides[1:], sides[0])
+
+
+class Blocks:
+    def __init__(self, rows):
+        self.rows, self.arrays, self.specs = rows, [], []
+
+    def add(self, terms):
+        plan = []
+        for term in terms:
+            plan.append([])
+            for array, number in term:
+                plan[-1].append(len(self.arrays))
+                self.arrays.append(array)
+                self.specs.append(
+                    pl.BlockSpec((self.rows, array.shape[1]), lambda i, number=number: (number, 0))
+                )
+        return plan
+
+
+def combine(results, rows, deps=()):
+    if rows % 16:
+        return [
+            jnp.concatenate([cut(terms, rows) for terms in parts]).astype(LOW) for parts in results
+        ]
+    blocks = Blocks(rows)
+    plan = [[blocks.add(terms) for terms in parts] for parts in results]
+    shapes = [
+        (rows * len(parts), sum(a.shape[1] for a, _ in parts[0][0])) for parts in results
+    ]
+    return pl.pallas_call(
+        with_deps(partial(combine_kernel, plan), 0, len(blocks.arrays), deps),
+        out_shape=[jax.ShapeDtypeStruct(s, LOW) for s in shapes],
+        grid=(1,),
+        in_specs=blocks.specs + [ANY] * len(deps),
+        out_specs=[pl.BlockSpec(s, lambda i: (0, 0)) for s in shapes],
+        compiler_params=VMEM,
+        name="combine",
+        cost_estimate=NO_COST,
+    )(*blocks.arrays, *deps)
+
+
+def adamw_step(master, first_moment, second_moment, gradient, decay_rate):
+    first_new = FIRST_DECAY * first_moment + (1.0 - FIRST_DECAY) * gradient
+    second_new = SECOND_DECAY * second_moment + (1.0 - SECOND_DECAY) * gradient * gradient
+    first_fixed = first_new / (1.0 - FIRST_DECAY**STEP)
+    second_fixed = second_new / (1.0 - SECOND_DECAY**STEP)
+    direction = first_fixed / (jnp.sqrt(second_fixed) + EPSILON)
+    master_new = master - LEARN_RATE * (direction + decay_rate * master)
+    return (master_new, first_new, second_new)
+
+
+def update_kernel(plan, widths, deep, *refs):
+    inputs, rest = refs[: len(refs) - 6 * len(widths) - 1], refs[len(refs) - 6 * len(widths) - 1 :]
+    states, outs, copy_ref = rest[: 3 * len(widths)], rest[3 * len(widths) : -1], rest[-1]
+    gradient = 0.0
+    for term in plan:
+        pieces = [inputs[r][...].astype(WIDE) for r in term]
+        gradient = gradient + (pieces[0] if not pieces[1:] else jnp.concatenate(pieces, axis=1))
+    rows, at = gradient.shape[0], 0
+    for i, width in enumerate(widths):
+        mine, to = states[3 * i : 3 * i + 3], outs[3 * i : 3 * i + 3]
+        groups = deep or 1
+        for j in range(groups):
+            part = gradient[:, at : at + width // groups]
+            old = [ref[j] if deep else ref[...] for ref in mine]
+            new = adamw_step(*old, part, WEIGHT_DECAY)
+            for ref, value in zip(to, new):
+                if deep:
+                    ref[j] = value
+                else:
+                    ref[...] = value
+            if deep:
+                copy_ref[j * rows : (j + 1) * rows] = new[0].astype(LOW)
+            else:
+                copy_ref[:, at : at + width] = new[0].astype(LOW)
+            at += width // groups
+
+
+def update(terms, rows, states, deep=0):
+    count = lambda s: s[0].shape[0] * s[0].shape[2] if deep else s[0].shape[1]
+    widths = [count(s) for s in states]
+    total = sum(widths)
+    if rows % 16:
+        gradient, at, news = cut(terms, rows), 0, []
+        for state, width in zip(states, widths):
+            part = gradient[:, at : at + width]
+            if deep:
+                part = jnp.stack(jnp.split(part, deep, axis=1))
+            news.append(adamw_step(*state, part, WEIGHT_DECAY))
+            at += width
+        copies = [n[0].astype(LOW) for n in news]
+        if deep:
+            return news, copies[0].reshape(-1, copies[0].shape[2])
+        return news, jnp.concatenate(copies, axis=1)
+    blocks = Blocks(rows)
+    plan = blocks.add(terms)
+    spec = lambda a: pl.BlockSpec(a.shape, lambda i: (0,) * a.ndim)
+    flat = [a for state in states for a in state]
+    copy = jax.ShapeDtypeStruct((rows * deep, total // deep) if deep else (rows, total), LOW)
+    outs = [jax.ShapeDtypeStruct(a.shape, WIDE) for a in flat] + [copy]
+    out = pl.pallas_call(
+        partial(update_kernel, plan, widths, deep),
+        out_shape=outs,
+        grid=(1,),
+        in_specs=blocks.specs + [spec(a) for a in flat],
+        out_specs=[spec(a) for a in outs],
+        compiler_params=VMEM,
+        name="update",
+        cost_estimate=NO_COST,
+    )(*blocks.arrays, *flat)
+    return [out[3 * i : 3 * i + 3] for i in range(len(states))], out[-1]
 
 
 def put_kernel(place, other_ref, whole_ref, out_ref):
@@ -602,104 +826,20 @@
 
 def put_other(place, other, whole, deps=()):
     tokens, d = other.shape
-    block = tokens // 4
     return pl.pallas_call(
         with_deps(put_kernel, 1, 2, deps),
         out_shape=jax.ShapeDtypeStruct(whole.shape, whole.dtype),
         grid_spec=pltpu.PrefetchScalarGridSpec(
             num_scalar_prefetch=1,
-            grid=(4,),
-            in_specs=[pl.BlockSpec((block, d), lambda s, c: (s, 0)), ANY] + [ANY] * len(deps),
-            out_specs=pl.BlockSpec((block, d), lambda s, c: ((1 - c[0]) * 4 + s, 0)),
+            grid=(1,),
+            in_specs=[pl.BlockSpec((tokens, d), lambda s, c: (0, 0)), ANY] + [ANY] * len(deps),
+            out_specs=pl.BlockSpec((tokens, d), lambda s, c: (1 - c[0], 0)),
         ),
         input_output_aliases={2: 0},
         compiler_params=VMEM,
         name="put_other",
-        cost_estimate=pl.CostEstimate(flops=0, bytes_accessed=4 * tokens * d, transcendentals=0),
+        cost_estimate=LONG,
     )(place, other, whole, *deps)
-
-
-def gather_kernel(count, layout, wide, place, z_ref, x_ref, y_ref, da_ref, db_ref, *refs):
-    outs, held = refs[: len(layout)], refs[len(layout)]
-    block = z_ref.shape[0] // (count // 4)
-    step = pl.program_id(0)
-
-    def blocks():
-        for apart in range(count):
-            first = (apart >> 2) * block
-            ref = (z_ref, x_ref, y_ref, da_ref)[apart & 3]
-            if apart & 3 == 3 and first >= da_ref.shape[0]:
-                ref, first = db_ref, first - da_ref.shape[0]
-            yield jnp.bitwise_xor(place[1], apart), ref[first : first + block]
-
-    for (kind, first, end), out in zip(layout, outs):
-
-        @pl.when((step >= first) & (step < end))
-        def _():
-            for at, value in blocks():
-                if kind == "deep":
-                    rows = block // out.shape[0]
-                    there = pl.ds(pl.multiple_of(at * rows, 16), rows)
-                    for i in range(out.shape[0]):
-                        out[i, there] = value[i * rows : i * rows + rows]
-                else:
-                    to = held if kind == "flip" else out
-                    to[pl.ds(pl.multiple_of(at * block, 16), block)] = value
-            if kind == "flip":
-                out[...] = held[...].T
-
-
-def gather_place(place, n_dp, layout, z, x, y, da, db, deps=()):
-    rows, cols = z.shape[0] * 4, z.shape[1]
-    block = rows // n_dp
-    deep = layout[0][0] == "deep"
-    wide = 128 if deep else 384
-    shapes, specs, steps = [], [], []
-    for kind, left, right in layout:
-        full = right - left
-        if deep:
-            left, right = 0, cols
-            shapes.append((full // cols, rows * cols // full, cols))
-        else:
-            shapes.append((full, rows) if kind == "flip" else (rows, full))
-        first, end = left // wide, right // wide
-        steps.append((kind, first, end))
-        at = lambda j, first=first, end=end: jnp.clip(j - first, 0, end - first - 1)
-        if deep:
-            specs.append(pl.BlockSpec(shapes[-1][:2] + (wide,), lambda j, c, at=at: (0, 0, at(j))))
-        elif kind == "flip":
-            specs.append(pl.BlockSpec((wide, rows), lambda j, c, at=at: (at(j), 0)))
-        else:
-            specs.append(pl.BlockSpec((rows, wide), lambda j, c, at=at: (0, at(j))))
-    if (block // (shapes[0][0] if deep else 1)) % 16:
-        plane = jnp.stack([z, x, y, jnp.concatenate([da, db])])
-        blocks = plane.reshape(4, n_dp // 4, block, cols).transpose(1, 0, 2, 3)
-        blocks = blocks.reshape(n_dp, block, cols)[jnp.arange(n_dp) ^ place[1]]
-        outs = []
-        for (kind, left, right), shape in zip(layout, shapes):
-            if deep:
-                outs.append(
-                    blocks.reshape(n_dp, shape[0], -1, cols).transpose(1, 0, 2, 3).reshape(shape)
-                )
-            else:
-                whole = blocks.reshape(rows, cols)[:, left:right]
-                outs.append(whole.T if kind == "flip" else whole)
-        return outs
-    spec = lambda a: pl.BlockSpec((a.shape[0], wide), lambda j, c: (0, j))
-    return pl.pallas_call(
-        with_deps(partial(gather_kernel, n_dp, steps, wide), 1, 5, deps),
-        out_shape=[jax.ShapeDtypeStruct(shape, LOW) for shape in shapes],
-        grid_spec=pltpu.PrefetchScalarGridSpec(
-            num_scalar_prefetch=1,
-            grid=(cols // wide,),
-            in_specs=[spec(a) for a in (z, x, y, da, db)] + [ANY] * len(deps),
-            out_specs=specs,
-            scratch_shapes=[pltpu.VMEM((rows, wide), LOW)],
-        ),
-        compiler_params=VMEM,
-        name="gather_place",
-        cost_estimate=pl.CostEstimate(flops=0, bytes_accessed=4 * rows * cols, transcendentals=0),
-    )(place, z, x, y, da, db, *deps)
 
 
 def swap(value):
@@ -710,57 +850,76 @@
     return lax.ppermute(value, "dp", [(i, i ^ apart) for i in range(count)])
 
 
-def far_groups(count):
-    groups, weight = [], 4
-    while weight < count:
-        members = min(4, count // weight)
-        groups.append((weight, members))
-        weight *= members
-    return groups
-
-
-def scatter_flow(mine, came, count):
+def far_digits(count, direct):
+    weights = [1 << bit for bit in range(2, count.bit_length() - 1)]
+    size = 2 if direct else 1
+    return [weights[i : i + size] for i in range(0, len(weights), size)]
+
+
+def distances(digit):
+    out = [0]
+    for weight in digit:
+        out = [d + e for d in out for e in (0, weight)]
+    return out
+
+
+def scatter_flow(mine, came, count, direct=False):
     rows, width = mine.shape
-    shape = lambda a: a.reshape(2, 2, 2, rows // 8, a.shape[1])
-    mine, came = shape(mine), [shape(c) for c in came]
-
-    def part(*at):
-        other = [c[at].astype(WIDE) for c in came]
-        return mine[at].astype(WIDE) + (jnp.concatenate(other, axis=-1) if other[1:] else other[0])
-
-    every = slice(None)
-    to_x, to_y = part(every, 1, 0).astype(LOW), part(1, every, 1).astype(LOW)
-    from_x, from_y = yield [to_x, to_y], lambda v: [across(v[0], 1, count), across(v[1], 2, count)]
-    to_y = (part(1, 0, 0) + from_x[1].astype(WIDE)).astype(LOW)
-    to_x = (part(0, 1, 1) + from_y[1].astype(WIDE)).astype(LOW)
-    last_x, last_y = yield [to_x, to_y], lambda v: [across(v[0], 1, count), across(v[1], 2, count)]
-    upper = part(0, 0, 0) + from_x[0].astype(WIDE) + last_y.astype(WIDE)
-    lower = part(0, 0, 1) + from_y[0].astype(WIDE) + last_x.astype(WIDE)
-    held = jnp.concatenate([upper, lower], axis=0)
-    for weight, members in reversed(far_groups(count)):
-        pieces = held.reshape(members, -1, width)
-        sends = [pieces[m].astype(LOW) for m in range(1, members)]
+    block = rows // 8
+
+    def part(y, x, half):
+        at = (y * 2 + x) * 2 + half
+        return [[(mine, at)], [(c, at) for c in came]]
+
+    to_x, to_y = combine(
+        [[part(0, 1, 0), part(1, 1, 0)], [part(1, 0, 1), part(1, 1, 1)]], block
+    )
+    send_both = lambda v: [across(v[0], 1, count), across(v[1], 2, count)]
+    from_x, from_y = yield [to_x, to_y], send_both
+    to_y, to_x = combine(
+        [[part(1, 0, 0) + [[(from_x, 1)]]], [part(0, 1, 1) + [[(from_y, 1)]]]], block
+    )
+    last_x, last_y = yield [to_x, to_y], send_both
+    upper = part(0, 0, 0) + [[(from_x, 0)], [(last_y, 0)]]
+    lower = part(0, 0, 1) + [[(from_y, 0)], [(last_x, 0)]]
+
+    half = block
+    terms = None
+    for digit in far_digits(count, direct):
+        apart = distances(digit)
+        if terms is None:
+            half = half * 2 // len(apart)
+            pieces = [upper, lower]
+            if len(apart) == 4:
+                pieces = [divide(p, 2, i) for p in pieces for i in range(2)]
+        else:
+            half = half // len(apart)
+            pieces = [divide(terms, len(apart), i) for i in range(len(apart))]
+        sends = combine([[piece] for piece in pieces[1:]], half)
         came = yield (
             sends,
-            lambda v, w=weight: [across(p, (m + 1) * w, count) for m, p in enumerate(v)],
+            lambda v, apart=apart: [across(p, d, count) for p, d in zip(v, apart[1:])],
         )
-        held = pieces[0]
-        for piece in came:
-            held = held + piece.astype(WIDE)
-    return held
-
-
-def gather_flow(shard, count):
+        terms = pieces[0] + [[(c, 0)] for c in came]
+    return terms, half
+
+
+def divide(terms, members, number):
+    return [[(a, n * members + number) for a, n in term] for term in terms]
+
+
+def gather_flow(shard, count, direct=False):
     held = shard
-    for weight, members in far_groups(count):
+    for digit in reversed(far_digits(count, direct)):
+        apart = distances(digit)
         came = yield (
             [held],
-            lambda v, w=weight, n=members: [across(v[0], m * w, count) for m in range(1, n)],
+            lambda v, apart=apart: [across(v[0], d, count) for d in apart[1:]],
         )
-        held = jnp.concatenate([held] + list(came), axis=0)
+        (held,) = combine([[[[(h, 0)]] for h in [held] + list(came)]], held.shape[0])
     half = held.shape[0] // 2
     x, y = yield [held], lambda v: [across(v[0], 1, count), across(v[0], 2, count)]
-    upper, lower = x[:half], y[half:]
+    upper, lower = combine([[[[(x, 0)]]], [[[(y, 1)]]]], half)
     both = yield [upper, lower], lambda v: [across(v[0], 2, count), across(v[1], 1, count)]
     return held, x, y, both[0], both[1]
 
@@ -859,28 +1018,23 @@
     contract_other = swap(contract_here)
     updates = {}
 
-    def contract_then(share):
-        new = adamw_step(
-            contract_master.T, contract_first.T, contract_second.T, share, WEIGHT_DECAY
-        )
-        updates["contract"] = new
-        return gather_flow(new[0].astype(LOW), n_dp), None
-
-    def expand_then(share):
-        new = adamw_step(
-            expand_master, expand_first, expand_second, share[:, :n_bias], WEIGHT_DECAY
-        )
-        out = adamw_step(
-            outward_master.T, outward_first.T, outward_second.T, share[:, n_bias:], WEIGHT_DECAY
-        )
-        updates["expand"], updates["outward"] = new, out
-        return gather_flow(jnp.concatenate([new[0], out[0]], axis=1).astype(LOW), n_dp), None
-
-    def triple_then(share):
-        share = jnp.stack([share[:, j * own : (j + 1) * own] for j in range(3)])
-        new = adamw_step(triple_master, triple_first, triple_second, share, WEIGHT_DECAY)
-        updates["triple"] = new
-        return gather_flow(new[0].astype(LOW).reshape(-1, own), n_dp), None
+    def contract_then(summed):
+        state = (contract_master.T, contract_first.T, contract_second.T)
+        (updates["contract"],), copy = update(*summed, [state])
+        return gather_flow(copy, n_dp), None
+
+    def expand_then(summed):
+        states = [
+            (expand_master, expand_first, expand_second),
+            (outward_master.T, outward_first.T, outward_second.T),
+        ]
+        (updates["expand"], updates["outward"]), copy = update(*summed, states)
+        return gather_flow(copy, n_dp), None
+
+    def triple_then(summed):
+        state = (triple_master, triple_first, triple_second)
+        (updates["triple"],), copy = update(*summed, [state], 3)
+        return gather_flow(copy, n_dp, True), None
 
     qkv, probs, context, pre_one = attend(
         place, lengths, hidden_in, key_mask, triple_weight, triple_other, outward_weight,
@@ -890,91 +1044,79 @@
         place, pre_one, grad_out, expand_weight, expand_other, contract_weight, contract_other,
         bias_row, bias_other, norm_vectors,
     )
-    layer_other = swap(layer_own)
 
     steps = n_bias // BLOCK_FF
     weight = partial(weight_grad, place, n_dp)
     contract_theirs = weight(branch_grad, active, steps, steps, BLOCK_FF)
     contract_mine = weight(branch_grad, active, 0, steps, BLOCK_FF, deps=(contract_theirs,))
-    contract_flow = Flow(scatter_flow(contract_mine, [swap(contract_theirs)], n_dp), contract_then)
+    contract_flow = Flow(scatter_flow(contract_mine, [swap(contract_theirs)], n_dp, True), contract_then)
     sends = contract_flow.advance()
     expand_theirs, bias_theirs, hidden_sofar = ffn_bwd(
         place, n_dp, False, branch_grad, slope, expand_other, contract_other, pre_two_grad,
         pre_two_grad, hidden_low, context, norm_vectors, deps=sends,
     )
-    expand_came = swap(expand_theirs)
     sends = contract_flow.advance(bias_theirs)
+    expand_came = swap(behind(expand_theirs, sends))
     expand_mine, bias_mine, pre_one_grad, attention_grad, sums_one, outward_theirs = ffn_bwd(
         place, n_dp, True, branch_grad, slope, expand_weight, contract_weight, hidden_sofar,
         pre_one, hidden_low, context, norm_vectors, deps=sends,
     )
-    expand_flow = Flow(
-        scatter_flow(expand_mine, [expand_came, swap(outward_theirs)], n_dp), expand_then
-    )
-    sends = contract_flow.advance(sums_one) + expand_flow.advance()
+    sends = contract_flow.advance(sums_one)
+    outward_came = swap(behind(outward_theirs, sends))
+    expand_flow = Flow(scatter_flow(expand_mine, [expand_came, outward_came], n_dp), expand_then)
+    sends = sends + expand_flow.advance()
     projected_grad, sums_pair = attend_back(
         attention_grad, probs, qkv, outward_weight, outward_other, 0, lengths.shape[0] // 2,
         deps=sends,
     )
-    sends = contract_flow.advance(sums_pair) + expand_flow.advance(sums_pair)
+    layer_other = swap(behind(layer_own, sends))
+    sends = contract_flow.advance(sums_pair)
+    sends = sends + expand_flow.advance(sends)
+    vectors = bundle(sums_one, sums_two, sums_pair, bias_mine, bias_theirs)
+    vector_flow = Flow(total_flow(*vectors, n_dp))
+    sends = sends + vector_flow.advance()
     triple_theirs = weight(hidden_in, projected_grad, 1, 1, 3 * own, deps=sends)
-    triple_mine = weight(hidden_in, projected_grad, 0, 1, 3 * own, deps=(triple_theirs,))
-    triple_flow = Flow(scatter_flow(triple_mine, [swap(triple_theirs)], n_dp), triple_then)
-    sends = triple_flow.advance() + expand_flow.advance(triple_mine)
+    sends = expand_flow.advance(triple_theirs) + vector_flow.advance(triple_theirs)
+    sends = sends + contract_flow.advance(triple_theirs)
+    triple_mine = weight(hidden_in, projected_grad, 0, 1, 3 * own, deps=sends)
+    triple_came = swap(behind(triple_theirs, sends))
+    triple_flow = Flow(scatter_flow(triple_mine, [triple_came], n_dp, True), triple_then)
+    sends = triple_flow.advance()
+    sends = sends + expand_flow.advance(triple_mine) + contract_flow.advance(triple_mine)
     input_own, input_grad = input_side(
         place, projected_grad, triple_weight, triple_other, pre_one_grad, deps=sends
     )
-
     triple_flow.advance(input_own)
-    contract_flow.advance(triple_flow.sends)
     expand_flow.advance(triple_flow.sends)
-    layer_out = put_other(place, layer_other, layer_out, deps=triple_flow.sends)
-
-    d = norm_vectors.shape[1]
-    sums_pair, bias_mine, bias_theirs = behind([sums_pair, bias_mine, bias_theirs], layer_out)
-    pair_grad = jnp.sum(sums_pair, axis=0)[:2]
-    spare = jnp.zeros((8 - (2 * own + n_bias) // d, d), WIDE)
-    bundle = lambda left, right, bias: jnp.concatenate(
-        [
-            sums_one,
-            sums_two,
-            pair_grad[:, left:right].reshape(-1, d),
-            bias.reshape(-1, d),
-            spare,
-        ]
-    )
-    vector_flow = Flow(
-        total_flow(bundle(0, own, bias_mine), bundle(own, 2 * own, bias_theirs), n_dp)
-    )
-    vector_flow.advance()
-    triple_flow.advance(layer_out)
-    contract_flow.advance(triple_flow.sends)
-    input_grad = put_other(place, swap(input_own), input_grad, deps=triple_flow.sends)
+    layer_out = put_other(place, layer_other, layer_out, deps=expand_flow.sends)
+    contract_flow.advance(layer_out)
+    triple_flow.advance(contract_flow.sends)
+    expand_flow.advance(triple_flow.sends)
+    vector_flow.advance(expand_flow.sends)
+    input_other = swap(behind(input_own, expand_flow.sends))
+    input_grad = put_other(place, input_other, input_grad, deps=expand_flow.sends)
     vector_flow.advance(input_grad)
-    expand_flow.advance(input_grad)
-    triple_flow.advance(input_grad)
     gather = partial(gather_place, place, n_dp)
     contract_flow.finish()
-    (contract_copy,) = gather(
-        (("flip", 0, n_bias),), *contract_flow.result, deps=triple_flow.sends
-    )
-    vector_flow.advance(contract_copy)
-    expand_flow.advance(contract_copy)
+    (contract_copy,) = gather((("flip", 0, n_bias),), *contract_flow.result, deps=(input_grad,))
     triple_flow.advance(contract_copy)
+    expand_flow.advance(triple_flow.sends)
     vector_flow.advance(triple_flow.sends)
+    triple_flow.advance(expand_flow.sends)
+    expand_flow.advance(triple_flow.sends)
+    vector_sum = vector_flow.finish()
+    triple_flow.advance(expand_flow.sends)
     expand_flow.finish()
     expand_copy, outward_copy = gather(
         (("plain", 0, n_bias), ("flip", n_bias, n_bias + own)),
         *expand_flow.result,
         deps=triple_flow.sends,
     )
-    triple_flow.advance(expand_copy)
-    vector_sum = vector_flow.finish()
     triple_flow.finish()
-    (triple_copy,) = gather((("deep", 0, 3 * own),), *triple_flow.result)
+    (triple_copy,) = gather((("deep", 0, 3 * own),), *triple_flow.result, deps=(expand_copy,))
     vector_total = jnp.stack([vector_sum[i] for i in (0, 8, 1, 2, 9, 10)])
-    pair_total = vector_sum[16 : 16 + 2 * own // d].reshape(2, own)
-    widen_total = vector_sum[16 + 2 * own // d :].reshape(-1)[:n_bias]
+    pair_total = vector_sum[16].reshape(2, own)
+    widen_total = vector_sum[17:].reshape(-1)[:n_bias]
     contract_new, expand_new = updates["contract"], updates["expand"]
     outward_new, triple_new = updates["outward"], updates["triple"]
     pair_new = adamw_step(pair_bias, pair_first, pair_second, pair_total, 0.0)

time: 321 us -> 299 us (0.931)
  Pallas kernels: 159 us -> 203 us
  other arithmetic: 29.5 us -> 10.3 us
  local copies, waits for them, and re-layouts: 21.1 us -> 3.1 us
  waiting for transfers between devices: 49.4 us -> 31.4 us
  starting transfers between devices: 58.7 us -> 49.1 us
    pallas_call x4 -> x26, Pallas kernels: 32.1 us -> 78.1 us  [the longest x18 39.4 us: combine(): pl.pallas_call(with_deps(partial(combine_kernel, plan), 0, len(blocks.arr...]
    ppermute x46 -> x43, waiting for transfers between devices: 46.1 us -> 29.2 us  [across(): return lax.ppermute(value, 'dp', [(i, i ^ apart) for i in range(count)])]
    convert_element_type x10 -> x0, other arithmetic: 12 us -> none  [the longest x5 6.46 us: scatter_flow(): to_x, to_y = (part(every, 1, 0).astype(LOW), part(1, every, 1).astype(LOW))]
    ppermute x46 -> x43, starting transfers between devices: 56.3 us -> 46.3 us  [across(): return lax.ppermute(value, 'dp', [(i, i ^ apart) for i in range(count)])]
    another operation x5 -> x0, other arithmetic: 6.55 us -> none
    concatenate x2 -> x0, local copies, waits for them, and re-layouts: 4.83 us -> none  [local(): jnp.concatenate([sums_one, sums_two, pair_grad[:, left:right].reshape(-1,...]
    unnamed x133 -> x0, local copies, waits for them, and re-layouts: 4.61 us -> none
    add x4, other arithmetic: 0.04 us -> 4.01 us  [total_flow(): total = total + came]
  transfers between devices with their start and end apart: 59 -> 56, of which waited for: 16 -> 14; matrix products, arithmetic and copies ran while one was open for 13% -> 5% of each run, Pallas kernels for 37% -> 54%
where the time goes in v3:
time: 299 us; the launch traced here: 298 us
  Pallas kernels  203 us (68%)
  starting transfers between devices  49.1 us (16%)
  waiting for transfers between devices  31.4 us (11%)
  other arithmetic  10.3 us (3%)
  local copies, waits for them, and re-layouts  3.1 us (1%)
    ppermute x43, starting transfers between devices, across(): return lax.ppermute(value, 'dp', [(i, i ^ apart) for i in range(count)])  46.3 us
    pallas_call x18, Pallas kernels, combine(): pl.pallas_call(with_deps(partial(combine_kernel, plan), 0, len(blocks.arr...  39.4 us
    pallas_call x2, Pallas kernels, ffn_bwd(): pl.pallas_call(with_deps(partial(ffn_bwd_kernel, final, n_dp), 1, 9, deps...  37.2 us
    ppermute x43, waiting for transfers between devices, across(): return lax.ppermute(value, 'dp', [(i, i ^ apart) for i in range(count)])  29.2 us
    pallas_call x4, Pallas kernels, weight_grad(): pl.pallas_call(with_deps(partial(weight_kernel, n_dp), 1, 2, deps), out_s...  26.1 us
    pallas_call x1, Pallas kernels, ffn_fwd(): pl.pallas_call(ffn_fwd_kernel, out_shape=(jax.ShapeDtypeStruct((tokens, 2...  24.7 us
    pallas_call x1, Pallas kernels, attend(): pl.pallas_call(attend_kernel, out_shape=(jax.ShapeDtypeStruct((tokens, 6...  18.8 us
    pallas_call x1, Pallas kernels, attend_back(): pl.pallas_call(with_deps(partial(attend_back_kernel, start), 0, 6, deps),...  16.7 us
  transfers between devices with their start and end apart: 56, of which 14 were waited for; matrix products, arithmetic and copies ran while one was open for 5% of the time, Pallas kernels for 54%

profile of v3, /device:TPU:0, one launch (start us, length us, event | category | flops | bytes accessed | tf_op | source)
XLA Modules:
  0.0 297.5 jit_solution(11253436708410673355)
XLA Ops:
  6.6 18.8 %attend.1 = (bf16[1024,2304]{1,0:T(8,128)(2,1)}, bf16[4,12,256,256]{3,2,1,0:T(8,128)(2,1)}, bf16[1024,768]{1,0:T(8,128)(2,1)}, f32[1024,768]{1,0:T(8,128)}) custom-call(s32[2]{0:T(128)} %pad_add_fusion.place.core.refs_0_, s32[8]{0:T(128)} %lengths.1, bf16[2048,768]{1,0:T(8,128)(2,1)} %refs_1_.3, s32[8,256]{1,0:T(8,128)} %mask_ref.1, ...), custom_call_target="tpu_custom_call" | custom-call | flops 49999998976 | bytes 100000000 | tf_op jit(solution)/shard_map/attend/pallas_call | solution.py:145
  25.4 24.7 %ffn_fwd.1 = (bf16[1024,3072]{1,0:T(8,128)(2,1)}, bf16[1024,3072]{1,0:T(8,128)(2,1)}, bf16[1024,768]{1,0:T(8,128)(2,1)}, f32[1024,768]{1,0:T(8,128)}, bf16[1024,...) custom-call(s32[2]{0:T(128)} %pad_add_fusion.place.core.refs_0_, ...), custom_call_target="tpu_custom_call" | custom-call | flops 49999998976 | bytes 100000000 | tf_op jit(solution)/shard_map/ffn_fwd/pallas_call | solution.py:244
  50.2 6.8 %weight_grad.4.refs_3_ = bf16[768,1536]{1,0:T(8,128)(2,1)} custom-call(s32[2]{0:T(128)} %pad_add_fusion.place.core.refs_0_, bf16[1024,768]{1,0:T(8,128)(2,1)} %get-tuple-element.145.refs_1_, bf16[1024,3072]{1,0:T(8,128)(2,1)} %get-tuple-element.146.refs_2_), custom_call_target="tpu_custom_call" | custom-call | flops 49999998976 | bytes 100000000 | tf_op jit(solution)/shard_map/weight_grad/pallas_call | solution.py:338
  57.2 6.8 %weight_grad.5.refs_0_.refs_2_.refs_4_.refs_6_.refs_3_.refs_8_ = bf16[768,1536]{1,0:T(8,128)(2,1)} custom-call(s32[2]{0:T(128)} %pad_add_fusion.place.core.refs_0_, bf16[1024,768]{1,0:T(8,128)(2,1)} %get-tuple-element.145.refs_1_, bf16[1024,3072]{1,0:T(8,128)(2,1)} %get-tuple-element.146.refs_2_, bf16[768,1536]{1,0:T(8,128)(2,1)} %weight_grad.4.refs_3_), custom_call_target="tpu_custom_call" | custom-call | flops 49999998976 | bytes 100000000 | tf_op jit(solution)/shard_map/weight_grad/pallas_call | solution.py:338
  66.8 2.9 collective-permute-start.7
  71.2 15.2 %ffn_bwd.2 = (bf16[768,1536]{1,0:T(8,128)(2,1)}, f32[1,1536]{1,0:T(1,128)}, f32[1024,768]{1,0:T(8,128)}) custom-call(s32[2]{0:T(128)} %pad_add_fusion.place.core.refs_0_, bf16[1024,768]{1,0:T(8,128)(2,1)} %get-tuple-element.145.refs_1_, bf16[1024,3072]{1,0:T(8,128)(2,1)} %get-tuple-element.149.refs_2_, ...), custom_call_target="tpu_custom_call" | custom-call | flops 49999998976 | bytes 100000000 | tf_op jit(solution)/shard_map/ffn_bwd/pallas_call | solution.py:445
  89.4 22.0 %ffn_bwd.3 = (bf16[768,1920]{1,0:T(8,128)(2,1)}, f32[1,1536]{1,0:T(1,128)}, f32[1024,768]{1,0:T(8,128)}, bf16[1024,768]{1,0:T(8,128)(2,1)}, f32[8,768]{1,0:T(8,128)}, /*index=5*/bf16[768,384]{1,0:T(8,128)(2,1)}) custom-call(s32[2]{0:T(128)} %pad_add_fusion.place.core.refs_0_, bf16[1024,768]{1,0:T(8,128)(2,1)} %get-tuple-element.145.refs_1_, ...), custom_call_target="tpu_custom_call" | custom-call | flops 49999998976 | bytes 100000000 | tf_op jit(solution)/shard_map/ffn_bwd/pallas_call | solution.py:445
  114.3 3.0 collective-permute-start.16
  118.9 3.0 %combine.21 = (bf16[192,1920]{1,0:T(8,128)(2,1)}, bf16[192,1920]{1,0:T(8,128)(2,1)}) custom-call(bf16[768,1920]{1,0:T(8,128)(2,1)} %get-tuple-element.165.refs_0_.refs_3_.refs_6_.refs_9_.refs_4_, bf16[768,1536]{1,0:T(8,128)(2,1)} %collective-permute-done.11.refs_1_.refs_4_.refs_7_.refs_10_.refs_5_, ...), custom_call_target="tpu_custom_call" | custom-call | tf_op jit(solution)/shard_map/combine/pallas_call | solution.py:739
  125.1 16.7 %attend_back.1 = (bf16[1024,2304]{1,0:T(8,128)(2,1)}, f32[8,768]{1,0:T(8,128)}) custom-call(bf16[1024,768]{1,0:T(8,128)(2,1)} %get-tuple-element.174.refs_0_.refs_5_, bf16[4,12,256,256]{3,2,1,0:T(8,128)(2,1)} %get-tuple-element.175.refs_1_, bf16[1024,2304]{1,0:T(8,128)(2,1)} %get-tuple-element.176.refs_2_, bf16[384,768]{1,0:T(8,128)(2,1)} %refs_3_.3, ...), custom_call_target="tpu_custom_call" | custom-call | flops 49999998976 | bytes 100000000 | tf_op jit(solution)/shard_map/attend_back/pallas_call | solution.py:537
  143.3 2.8 update.3
  151.6 6.2 %weight_grad.6 = bf16[768,1152]{1,0:T(8,128)(2,1)} custom-call(s32[2]{0:T(128)} %pad_add_fusion.place.core.refs_0_, bf16[2048,768]{1,0:T(8,128)(2,1)} %refs_1_.3, bf16[1024,2304]{1,0:T(8,128)(2,1)} %get-tuple-element.186.refs_2_.refs_1_, bf16[48,1536]{1,0:T(8,128)(2,1)} %get-tuple-element.181.refs_3_.refs_0_, bf16[96,1920]{1,0:T(8,128)(2,1)} %get-tuple-element.184.refs_4_, ...), custom_call_target="tpu_custom_call" | custom-call | flops 49999998976 | bytes 100000000 | tf_op jit(solution)/shard_map/weight_grad/pallas_call | solution.py:338
  166.6 6.2 %weight_grad.7.refs_0_.refs_2_.refs_4_.refs_6_.refs_3_.refs_8_ = bf16[768,1152]{1,0:T(8,128)(2,1)} custom-call(s32[2]{0:T(128)} %pad_add_fusion.place.core.refs_0_, bf16[2048,768]{1,0:T(8,128)(2,1)} %refs_1_.3, bf16[1024,2304]{1,0:T(8,128)(2,1)} %get-tuple-element.186.refs_2_.refs_1_, bf16[96,1920]{1,0:T(8,128)(2,1)} %combine.23.refs_3_, ...), custom_call_target="tpu_custom_call" | custom-call | flops 49999998976 | bytes 100000000 | tf_op jit(solution)/shard_map/weight_grad/pallas_call | solution.py:338
  185.3 10.6 %input_side.1 = (bf16[1024,768]{1,0:T(8,128)(2,1)}, f32[2048,768]{1,0:T(8,128)}) custom-call(s32[2]{0:T(128)} %pad_add_fusion.place.core.refs_0_, bf16[1024,2304]{1,0:T(8,128)(2,1)} %get-tuple-element.186.refs_2_.refs_1_, bf16[3,768,384]{2,1,0:T(8,128)(2,1)} %refs_2_.1, bf16[3,768,384]{2,1,0:T(8,128)(2,1)} %collective-permute-done.w1_ref.refs_3_, ...), custom_call_target="tpu_custom_call" | custom-call | flops 49999998976 | bytes 100000000 | tf_op jit(solution)/shard_map/input_side/pallas_call | solution.py:581
  196.5 3.8 %collective-permute-done.27.refs_5_.refs_6_.refs_10_ = bf16[192,1152]{1,0:T(8,128)(2,1)} collective-permute-done((bf16[192,1152]{1,0:T(8,128)(2,1)}, bf16[192,1152]{1,0:T(8,128)(2,1)}, u32[]{:S(2)}, u32[]{:S(2)}) %collective-permute-start.27) | collective-permute-done | bytes 442400 | tf_op jit(solution)/shard_map/ppermute | solution.py:850
  204.8 3.0 update.4
  208.6 3.3 %put_other.2 = bf16[2048,768]{1,0:T(8,128)(2,1)} custom-call(s32[2]{0:T(128)} %pad_add_fusion.place.core.refs_0_, bf16[1024,768]{1,0:T(8,128)(2,1)} %collective-permute-done.13.refs_1_, bf16[2048,768]{1,0:T(8,128)(2,1)} %get-tuple-element.173.refs_2_, bf16[48,1920]{1,0:T(8,128)(2,1)} %get-tuple-element.207.refs_3_.refs_0_), custom_call_target="tpu_custom_call", output_to_operand_aliasing={{}: (2, {})} | custom-call | flops 49999998976 | bytes 100000000 | tf_op jit(solution)/shard_map/put_other/pallas_call | solution.py:829
  229.7 3.9 %put_other.3.refs_6_ = f32[2048,768]{1,0:T(8,128)} custom-call(s32[2]{0:T(128)} %pad_add_fusion.place.core.refs_0_, bf16[1024,768]{1,0:T(8,128)(2,1)} %collective-permute-done.34.refs_1_, f32[2048,768]{1,0:T(8,128)} %get-tuple-element.219.refs_2_, bf16[96,1920]{1,0:T(8,128)(2,1)} %combine.31.refs_3_.refs_0_), custom_call_target="tpu_custom_call", output_to_operand_aliasing={{}: (2, {})} | custom-call | flops 49999998976 | bytes 100000000 | tf_op jit(solution)/shard_map/put_other/pallas_call | solution.py:829
  234.5 4.5 %gather_place.3 = bf16[1536,768]{1,0:T(8,128)(2,1)} custom-call(s32[2]{0:T(128)} %pad_add_fusion.place.core.refs_0_, bf16[192,1536]{1,0:T(8,128)(2,1)} %combine.27.refs_8_.refs_1_, bf16[192,1536]{1,0:T(8,128)(2,1)} %collective-permute-done.32.refs_0_.refs_2_, bf16[192,1536]{1,0:T(8,128)(2,1)} %collective-permute-done.33.refs_1_.refs_3_, ...), custom_call_target="tpu_custom_call" | custom-call | flops 49999998976 | bytes 100000000 | tf_op jit(solution)/shard_map/gather_place/pallas_call | solution.py:674
  241.5 2.9 collective-permute-start.42
  247.9 3.5 %collective-permute-done.54 = f32[24,768]{1,0:T(8,128)S(1)} collective-permute-done((f32[24,768]{1,0:T(8,128)S(1)}, f32[24,768]{1,0:T(8,128)S(1)}, u32[]{:S(2)}, u32[]{:S(2)}) %collective-permute-start.54) | collective-permute-done | bytes 73760 | tf_op jit(solution)/shard_map/ppermute | solution.py:850
  264.7 9.7 %collective-permute-done.47.refs_1_.refs_3_ = bf16[192,1920]{1,0:T(8,128)(2,1)} collective-permute-done((bf16[192,1920]{1,0:T(8,128)(2,1)}, bf16[192,1920]{1,0:T(8,128)(2,1)}, u32[]{:S(2)}, u32[]{:S(2)}) %collective-permute-start.47) | collective-permute-done | bytes 737312 | tf_op jit(solution)/shard_map/ppermute | solution.py:850
  289.3 4.3 %gather_place.4 = (bf16[768,1536]{1,0:T(8,128)(2,1)}, bf16[384,768]{1,0:T(8,128)(2,1)}) custom-call(s32[2]{0:T(128)} %pad_add_fusion.place.core.refs_0_, bf16[192,1920]{1,0:T(8,128)(2,1)} %combine.32.refs_1_, bf16[192,1920]{1,0:T(8,128)(2,1)} %collective-permute-done.46.refs_0_.refs_2_, bf16[192,1920]{1,0:T(8,128)(2,1)} %collective-permute-done.47.refs_1_.refs_3_, ...), custom_call_target="tpu_custom_call" | custom-call | flops 49999998976 | bytes 100000000 | tf_op jit(solution)/shard_map/gather_place/pallas_call | solution.py:674
  294.1 3.5 %gather_place.5 = bf16[3,768,384]{2,1,0:T(8,128)(2,1)} custom-call(s32[2]{0:T(128)} %pad_add_fusion.place.core.refs_0_, bf16[576,384]{1,0:T(8,128)(2,1)} %combine.33.refs_1_, bf16[576,384]{1,0:T(8,128)(2,1)} %collective-permute-done.44.refs_0_.refs_2_, bf16[576,384]{1,0:T(8,128)(2,1)} %collective-permute-done.45.refs_1_.refs_3_, ...), custom_call_target="tpu_custom_call" | custom-call | flops 49999998976 | bytes 100000000 | tf_op jit(solution)/shard_map/gather_place/pallas_call | solution.py:674
  (139 shorter events, 108.4 us)
Async XLA Ops:
  5.7 19.7 %collective-permute-start.5 = (f32[1,1536]{1,0:T(1,128)}, f32[1,1536]{1,0:T(1,128)}, u32[]{:S(2)}, u32[]{:S(2)}) collective-permute-start(f32[1,1536]{1,0:T(1,128)} %broadcast_in_dim.3.b0_ref), channel_id=1, source_target_pairs={{0,1},{1,0},{2,3},{3,2},{4,5},{5,4},{6,7},{7,6},{8,9},{9,8},{10,11... | collective-permute-start | bytes 18440 | tf_op jit(solution)/shard_map/ppermute | solution.py:846
  6.1 19.4 %collective-permute-start.3 = (bf16[768,1536]{1,0:T(8,128)(2,1)}, bf16[768,1536]{1,0:T(8,128)(2,1)}, u32[]{:S(2)}, u32[]{:S(2)}) collective-permute-start(bf16[768,1536]{1,0:T(8,128)(2,1)} %refs_3_.2), channel_id=1, source_target_pairs={{0,1},{1,0},{2,3},{3,2},{4,5},{5,4},{6,7},{7,6},{8,9},{9,8},{10,11... | collective-permute-start | bytes 7077896 | tf_op jit(solution)/shard_map/ppermute | solution.py:846
  6.2 19.2 %collective-permute-start.4 = (bf16[1536,768]{1,0:T(8,128)(2,1)}, bf16[1536,768]{1,0:T(8,128)(2,1)}, u32[]{:S(2)}, u32[]{:S(2)}) collective-permute-start(bf16[1536,768]{1,0:T(8,128)(2,1)} %refs_4_.1), channel_id=1, source_target_pairs={{0,1},{1,0},{2,3},{3,2},{4,5},{5,4},{6,7},{7,6},{8,9},{9,8},{10,11... | collective-permute-start | bytes 7077896 | tf_op jit(solution)/shard_map/ppermute | solution.py:846
  66.8 19.6 %collective-permute-start.7 = (bf16[192,1536]{1,0:T(8,128)(2,1)}, bf16[192,1536]{1,0:T(8,128)(2,1)}, u32[]{:S(2)}, u32[]{:S(2)}) collective-permute-start(bf16[192,1536]{1,0:T(8,128)(2,1)} %get-tuple-element.147.refs_10_), channel_id=1, source_target_pairs={{0,2},{2,0},{4,6},{6,4},{8,10},{10,8},{12,14},{14,12},{16,18},{18,... | collective-permute-start | bytes 1769480 | tf_op jit(solution)/shard_map/ppermute | solution.py:850
  69.7 16.7 %collective-permute-start.8 = (bf16[192,1536]{1,0:T(8,128)(2,1)}, bf16[192,1536]{1,0:T(8,128)(2,1)}, u32[]{:S(2)}, u32[]{:S(2)}) collective-permute-start(bf16[192,1536]{1,0:T(8,128)(2,1)} %get-tuple-element.148.refs_11_), channel_id=1, source_target_pairs={{0,4},{2,6},{4,0},{6,2},{8,12},{10,14},{12,8},{14,10},{16,20},{18,... | collective-permute-start | bytes 1769480 | tf_op jit(solution)/shard_map/ppermute | solution.py:850
  88.7 22.7 %collective-permute-start.9 = (bf16[96,1536]{1,0:T(8,128)(2,1)}, bf16[96,1536]{1,0:T(8,128)(2,1)}, u32[]{:S(2)}, u32[]{:S(2)}) collective-permute-start(bf16[96,1536]{1,0:T(8,128)(2,1)} %get-tuple-element.156.refs_10_), channel_id=1, source_target_pairs={{0,2},{2,0},{4,6},{6,4},{8,10},{10,8},{12,14},{14,12},{16,18},{18,... | collective-permute-start | bytes 884744 | tf_op jit(solution)/shard_map/ppermute | solution.py:850
  89.3 22.1 %collective-permute-start.10 = (bf16[96,1536]{1,0:T(8,128)(2,1)}, bf16[96,1536]{1,0:T(8,128)(2,1)}, u32[]{:S(2)}, u32[]{:S(2)}) collective-permute-start(bf16[96,1536]{1,0:T(8,128)(2,1)} %get-tuple-element.157.refs_11_), channel_id=1, source_target_pairs={{0,4},{2,6},{4,0},{6,2},{8,12},{10,14},{12,8},{14,10},{16,20},{18,... | collective-permute-start | bytes 884744 | tf_op jit(solution)/shard_map/ppermute | solution.py:850
  89.4 29.5 %collective-permute-start.11 = (bf16[768,1536]{1,0:T(8,128)(2,1)}, bf16[768,1536]{1,0:T(8,128)(2,1)}, u32[]{:S(2)}, u32[]{:S(2)}) collective-permute-start(bf16[768,1536]{1,0:T(8,128)(2,1)} %get-tuple-element.167), channel_id=1, source_target_pairs={{0,1},{1,0},{2,3},{3,2},{4,5},{5,4},{6,7},{7,6},{8,9},{9,8},{10,11... | collective-permute-start | bytes 7077896 | tf_op jit(solution)/shard_map/ppermute | solution.py:846
  114.3 27.5 %collective-permute-start.16 = (bf16[48,1536]{1,0:T(8,128)(2,1)}, bf16[48,1536]{1,0:T(8,128)(2,1)}, u32[]{:S(2)}, u32[]{:S(2)}) collective-permute-start(bf16[48,1536]{1,0:T(8,128)(2,1)} %get-tuple-element.162.refs_6_), channel_id=1, source_target_pairs={{0,16},{2,18},{4,20},{6,22},{8,24},{10,26},{12,28},{14,30},{16,0},... | collective-permute-start | bytes 442376 | tf_op jit(solution)/shard_map/ppermute | solution.py:850
  117.3 24.5 %collective-permute-start.17 = (bf16[48,1536]{1,0:T(8,128)(2,1)}, bf16[48,1536]{1,0:T(8,128)(2,1)}, u32[]{:S(2)}, u32[]{:S(2)}) collective-permute-start(bf16[48,1536]{1,0:T(8,128)(2,1)} %get-tuple-element.163.refs_7_), channel_id=1, source_target_pairs={{0,8},{2,10},{4,12},{6,14},{8,0},{10,2},{12,4},{14,6},{16,24},{18,... | collective-permute-start | bytes 442376 | tf_op jit(solution)/shard_map/ppermute | solution.py:850
  118.9 22.9 %collective-permute-start.18 = (bf16[48,1536]{1,0:T(8,128)(2,1)}, bf16[48,1536]{1,0:T(8,128)(2,1)}, u32[]{:S(2)}, u32[]{:S(2)}) collective-permute-start(bf16[48,1536]{1,0:T(8,128)(2,1)} %get-tuple-element.164.refs_8_), channel_id=1, source_target_pairs={{0,24},{2,26},{4,28},{6,30},{8,16},{10,18},{12,20},{14,22},{16,8},... | collective-permute-start | bytes 442376 | tf_op jit(solution)/shard_map/ppermute | solution.py:850
  121.9 26.1 %collective-permute-start.14 = (bf16[192,1920]{1,0:T(8,128)(2,1)}, bf16[192,1920]{1,0:T(8,128)(2,1)}, u32[]{:S(2)}, u32[]{:S(2)}) collective-permute-start(bf16[192,1920]{1,0:T(8,128)(2,1)} %get-tuple-element.170.refs_9_), channel_id=1, source_target_pairs={{0,2},{2,0},{4,6},{6,4},{8,10},{10,8},{12,14},{14,12},{16,18},{18,... | collective-permute-start | bytes 2211848 | tf_op jit(solution)/shard_map/ppermute | solution.py:850
  123.6 24.4 %collective-permute-start.15 = (bf16[192,1920]{1,0:T(8,128)(2,1)}, bf16[192,1920]{1,0:T(8,128)(2,1)}, u32[]{:S(2)}, u32[]{:S(2)}) collective-permute-start(bf16[192,1920]{1,0:T(8,128)(2,1)} %get-tuple-element.171.refs_10_), channel_id=1, source_target_pairs={{0,4},{2,6},{4,0},{6,2},{8,12},{10,14},{12,8},{14,10},{16,20},{18,... | collective-permute-start | bytes 2211848 | tf_op jit(solution)/shard_map/ppermute | solution.py:850
  143.3 16.3 %collective-permute-start.22 = (f32[24,768]{1,0:T(8,128)}, f32[24,768]{1,0:T(8,128)}, u32[]{:S(2)}, u32[]{:S(2)}) collective-permute-start(f32[24,768]{1,0:T(8,128)} %get-tuple-element.189.refs_6_), channel_id=1, source_target_pairs={{0,1},{1,0},{2,3},{3,2},{4,5},{5,4},{6,7},{7,6},{8,9},{9,8},{10,11... | collective-permute-start | bytes 221192 | tf_op jit(solution)/shard_map/ppermute | solution.py:846
  147.8 60.0 %collective-permute-start.13 = (bf16[1024,768]{1,0:T(8,128)(2,1)}, bf16[1024,768]{1,0:T(8,128)(2,1)}, u32[]{:S(2)}, u32[]{:S(2)}) collective-permute-start(bf16[1024,768]{1,0:T(8,128)(2,1)} %get-tuple-element.172), channel_id=1, source_target_pairs={{0,1},{1,0},{2,3},{3,2},{4,5},{5,4},{6,7},{7,6},{8,9},{9,8},{10,11... | collective-permute-start | bytes 4718600 | tf_op jit(solution)/shard_map/ppermute | solution.py:846
  174.8 37.1 %collective-permute-start.33 = (bf16[192,1536]{1,0:T(8,128)(2,1)}, bf16[192,1536]{1,0:T(8,128)(2,1)}, u32[]{:S(2)}, u32[]{:S(2)}) collective-permute-start(bf16[192,1536]{1,0:T(8,128)(2,1)} %combine.27.refs_8_.refs_1_), channel_id=1, source_target_pairs={{0,4},{2,6},{4,0},{6,2},{8,12},{10,14},{12,8},{14,10},{16,20},{18,... | collective-permute-start | bytes 1769480 | tf_op jit(solution)/shard_map/ppermute | solution.py:850
  179.2 24.9 %collective-permute-start.24 = (bf16[48,1920]{1,0:T(8,128)(2,1)}, bf16[48,1920]{1,0:T(8,128)(2,1)}, u32[]{:S(2)}, u32[]{:S(2)}) collective-permute-start(bf16[48,1920]{1,0:T(8,128)(2,1)} %combine.25.refs_7_), channel_id=1, source_target_pairs={{0,16},{2,18},{4,20},{6,22},{8,24},{10,26},{12,28},{14,30},{16,0},... | collective-permute-start | bytes 552968 | tf_op jit(solution)/shard_map/ppermute | solution.py:850
  183.8 16.5 %collective-permute-start.27 = (bf16[192,1152]{1,0:T(8,128)(2,1)}, bf16[192,1152]{1,0:T(8,128)(2,1)}, u32[]{:S(2)}, u32[]{:S(2)}) collective-permute-start(bf16[192,1152]{1,0:T(8,128)(2,1)} %get-tuple-element.198.refs_6_), channel_id=1, source_target_pairs={{0,4},{2,6},{4,0},{6,2},{8,12},{10,14},{12,8},{14,10},{16,20},{18,... | collective-permute-start | bytes 1327112 | tf_op jit(solution)/shard_map/ppermute | solution.py:850
  195.8 16.1 %collective-permute-start.32 = (bf16[192,1536]{1,0:T(8,128)(2,1)}, bf16[192,1536]{1,0:T(8,128)(2,1)}, u32[]{:S(2)}, u32[]{:S(2)}) collective-permute-start(bf16[192,1536]{1,0:T(8,128)(2,1)} %combine.27.refs_8_.refs_1_), channel_id=1, source_target_pairs={{0,2},{2,0},{4,6},{6,4},{8,10},{10,8},{12,14},{14,12},{16,18},{18,... | collective-permute-start | bytes 1769480 | tf_op jit(solution)/shard_map/ppermute | solution.py:850
  233.6 19.1 %collective-permute-start.43 = (bf16[96,1920]{1,0:T(8,128)(2,1)}, bf16[96,1920]{1,0:T(8,128)(2,1)}, u32[]{:S(2)}, u32[]{:S(2)}) collective-permute-start(bf16[96,1920]{1,0:T(8,128)(2,1)} %combine.31.refs_3_.refs_0_), channel_id=1, source_target_pairs={{0,8},{2,10},{4,12},{6,14},{8,0},{10,2},{12,4},{14,6},{16,24},{18,... | collective-permute-start | bytes 1105928 | tf_op jit(solution)/shard_map/ppermute | solution.py:850
  254.7 19.7 %collective-permute-start.47 = (bf16[192,1920]{1,0:T(8,128)(2,1)}, bf16[192,1920]{1,0:T(8,128)(2,1)}, u32[]{:S(2)}, u32[]{:S(2)}) collective-permute-start(bf16[192,1920]{1,0:T(8,128)(2,1)} %combine.32.refs_1_), channel_id=1, source_target_pairs={{0,4},{2,6},{4,0},{6,2},{8,12},{10,14},{12,8},{14,10},{16,20},{18,... | collective-permute-start | bytes 2211848 | tf_op jit(solution)/shard_map/ppermute | solution.py:850
  255.8 19.7 %collective-permute-start.46 = (bf16[192,1920]{1,0:T(8,128)(2,1)}, bf16[192,1920]{1,0:T(8,128)(2,1)}, u32[]{:S(2)}, u32[]{:S(2)}) collective-permute-start(bf16[192,1920]{1,0:T(8,128)(2,1)} %combine.32.refs_1_), channel_id=1, source_target_pairs={{0,2},{2,0},{4,6},{6,4},{8,10},{10,8},{12,14},{14,12},{16,18},{18,... | collective-permute-start | bytes 2211848 | tf_op jit(solution)/shard_map/ppermute | solution.py:850
  257.8 26.1 %collective-permute-start.45 = (bf16[576,384]{1,0:T(8,128)(2,1)}, bf16[576,384]{1,0:T(8,128)(2,1)}, u32[]{:S(2)}, u32[]{:S(2)}) collective-permute-start(bf16[576,384]{1,0:T(8,128)(2,1)} %combine.33.refs_1_), channel_id=1, source_target_pairs={{0,4},{2,6},{4,0},{6,2},{8,12},{10,14},{12,8},{14,10},{16,20},{18,... | collective-permute-start | bytes 1327112 | tf_op jit(solution)/shard_map/ppermute | solution.py:850
  259.0 26.0 %collective-permute-start.44 = (bf16[576,384]{1,0:T(8,128)(2,1)}, bf16[576,384]{1,0:T(8,128)(2,1)}, u32[]{:S(2)}, u32[]{:S(2)}) collective-permute-start(bf16[576,384]{1,0:T(8,128)(2,1)} %combine.33.refs_1_), channel_id=1, source_target_pairs={{0,2},{2,0},{4,6},{6,4},{8,10},{10,8},{12,14},{14,12},{16,18},{18,... | collective-permute-start | bytes 1327112 | tf_op jit(solution)/shard_map/ppermute | solution.py:850
  (32 other events, 317.3 us)

commit v4 on v3

--- a/solution.py
+++ b/solution.py
@@ -1034,7 +1034,7 @@
     def triple_then(summed):
         state = (triple_master, triple_first, triple_second)
         (updates["triple"],), copy = update(*summed, [state], 3)
-        return gather_flow(copy, n_dp, True), None
+        return gather_flow(copy, n_dp), None
 
     qkv, probs, context, pre_one = attend(
         place, lengths, hidden_in, key_mask, triple_weight, triple_other, outward_weight,
@@ -1088,30 +1088,38 @@
     )
     triple_flow.advance(input_own)
     expand_flow.advance(triple_flow.sends)
-    layer_out = put_other(place, layer_other, layer_out, deps=expand_flow.sends)
+    vector_flow.advance(triple_flow.sends)
+    layer_out = put_other(place, layer_other, layer_out, deps=expand_flow.sends + vector_flow.sends)
     contract_flow.advance(layer_out)
     triple_flow.advance(contract_flow.sends)
     expand_flow.advance(triple_flow.sends)
     vector_flow.advance(expand_flow.sends)
     input_other = swap(behind(input_own, expand_flow.sends))
-    input_grad = put_other(place, input_other, input_grad, deps=expand_flow.sends)
+    input_grad = put_other(
+        place, input_other, input_grad, deps=expand_flow.sends + vector_flow.sends
+    )
+    gather = partial(gather_place, place, n_dp)
+    triple_flow.advance(input_grad)
+    expand_flow.advance(triple_flow.sends)
     vector_flow.advance(input_grad)
-    gather = partial(gather_place, place, n_dp)
+    triple_flow.advance(expand_flow.sends)
     contract_flow.finish()
-    (contract_copy,) = gather((("flip", 0, n_bias),), *contract_flow.result, deps=(input_grad,))
+    (contract_copy,) = gather(
+        (("flip", 0, n_bias),),
+        *contract_flow.result,
+        deps=triple_flow.sends + expand_flow.sends + vector_flow.sends,
+    )
     triple_flow.advance(contract_copy)
+    vector_flow.advance(contract_copy)
     expand_flow.advance(triple_flow.sends)
-    vector_flow.advance(triple_flow.sends)
-    triple_flow.advance(expand_flow.sends)
-    expand_flow.advance(triple_flow.sends)
-    vector_sum = vector_flow.finish()
     triple_flow.advance(expand_flow.sends)
     expand_flow.finish()
     expand_copy, outward_copy = gather(
         (("plain", 0, n_bias), ("flip", n_bias, n_bias + own)),
         *expand_flow.result,
-        deps=triple_flow.sends,
-    )
+        deps=triple_flow.sends + vector_flow.sends,
+    )
+    vector_sum = vector_flow.finish()
     triple_flow.finish()
     (triple_copy,) = gather((("deep", 0, 3 * own),), *triple_flow.result, deps=(expand_copy,))
     vector_total = jnp.stack([vector_sum[i] for i in (0, 8, 1, 2, 9, 10)])

time: 299 us -> 296 us (0.990)
  waiting for transfers between devices: 31.4 us -> 20 us
  starting transfers between devices: 49.1 us -> 54.5 us
    ppermute x43 -> x42, waiting for transfers between devices: 29.2 us -> 17.9 us  [across(): return lax.ppermute(value, 'dp', [(i, i ^ apart) for i in range(count)])]
    ppermute x43 -> x42, starting transfers between devices: 46.3 us -> 51.7 us  [across(): return lax.ppermute(value, 'dp', [(i, i ^ apart) for i in range(count)])]
    pallas_call x18 -> x19, Pallas kernels: 39.4 us -> 41.1 us  [combine(): pl.pallas_call(with_deps(partial(combine_kernel, plan), 0, len(blocks.arr...]
  transfers between devices with their start and end apart: 56 -> 55, of which waited for: 14 -> 9; matrix products, arithmetic and copies ran while one was open for 5% -> 5% of each run, Pallas kernels for 54% -> 55%
where the time goes in v4:
time: 296 us; the launch traced here: 295 us
  Pallas kernels  204 us (69%)
  starting transfers between devices  54.5 us (18%)
  waiting for transfers between devices  20 us (7%)
  other arithmetic  11.9 us (4%)
  local copies, waits for them, and re-layouts  3.1 us (1%)
    ppermute x42, starting transfers between devices, across(): return lax.ppermute(value, 'dp', [(i, i ^ apart) for i in range(count)])  51.7 us
    pallas_call x19, Pallas kernels, combine(): pl.pallas_call(with_deps(partial(combine_kernel, plan), 0, len(blocks.arr...  41.1 us
    pallas_call x2, Pallas kernels, ffn_bwd(): pl.pallas_call(with_deps(partial(ffn_bwd_kernel, final, n_dp), 1, 9, deps...  37.1 us
    pallas_call x4, Pallas kernels, weight_grad(): pl.pallas_call(with_deps(partial(weight_kernel, n_dp), 1, 2, deps), out_s...  26.1 us
    pallas_call x1, Pallas kernels, ffn_fwd(): pl.pallas_call(ffn_fwd_kernel, out_shape=(jax.ShapeDtypeStruct((tokens, 2...  24.7 us
    pallas_call x1, Pallas kernels, attend(): pl.pallas_call(attend_kernel, out_shape=(jax.ShapeDtypeStruct((tokens, 6...  18.8 us
    ppermute x42, waiting for transfers between devices, across(): return lax.ppermute(value, 'dp', [(i, i ^ apart) for i in range(count)])  17.9 us
    pallas_call x1, Pallas kernels, attend_back(): pl.pallas_call(with_deps(partial(attend_back_kernel, start), 0, 6, deps),...  16.7 us
  transfers between devices with their start and end apart: 55, of which 9 were waited for; matrix products, arithmetic and copies ran while one was open for 5% of the time, Pallas kernels for 55%

profile of v4, /device:TPU:0, one launch (start us, length us, event | category | flops | bytes accessed | tf_op | source)
XLA Modules:
  0.0 294.7 jit_solution(13066898518001417635)
XLA Ops:
  6.6 18.8 %attend.1 = (bf16[1024,2304]{1,0:T(8,128)(2,1)}, bf16[4,12,256,256]{3,2,1,0:T(8,128)(2,1)}, bf16[1024,768]{1,0:T(8,128)(2,1)}, f32[1024,768]{1,0:T(8,128)}) custom-call(s32[2]{0:T(128)} %pad_add_fusion.place.core.refs_0_, s32[8]{0:T(128)} %lengths.1, bf16[2048,768]{1,0:T(8,128)(2,1)} %refs_1_.3, s32[8,256]{1,0:T(8,128)} %mask_ref.1, ...), custom_call_target="tpu_custom_call" | custom-call | flops 49999998976 | bytes 100000000 | tf_op jit(solution)/shard_map/attend/pallas_call | solution.py:145
  25.4 24.7 %ffn_fwd.1 = (bf16[1024,3072]{1,0:T(8,128)(2,1)}, bf16[1024,3072]{1,0:T(8,128)(2,1)}, bf16[1024,768]{1,0:T(8,128)(2,1)}, f32[1024,768]{1,0:T(8,128)}, bf16[1024,...) custom-call(s32[2]{0:T(128)} %pad_add_fusion.place.core.refs_0_, ...), custom_call_target="tpu_custom_call" | custom-call | flops 49999998976 | bytes 100000000 | tf_op jit(solution)/shard_map/ffn_fwd/pallas_call | solution.py:244
  50.2 6.8 %weight_grad.4.refs_3_ = bf16[768,1536]{1,0:T(8,128)(2,1)} custom-call(s32[2]{0:T(128)} %pad_add_fusion.place.core.refs_0_, bf16[1024,768]{1,0:T(8,128)(2,1)} %get-tuple-element.145.refs_1_, bf16[1024,3072]{1,0:T(8,128)(2,1)} %get-tuple-element.146.refs_2_), custom_call_target="tpu_custom_call" | custom-call | flops 49999998976 | bytes 100000000 | tf_op jit(solution)/shard_map/weight_grad/pallas_call | solution.py:338
  57.2 6.8 %weight_grad.5.refs_0_.refs_2_.refs_4_.refs_6_.refs_3_.refs_8_ = bf16[768,1536]{1,0:T(8,128)(2,1)} custom-call(s32[2]{0:T(128)} %pad_add_fusion.place.core.refs_0_, bf16[1024,768]{1,0:T(8,128)(2,1)} %get-tuple-element.145.refs_1_, bf16[1024,3072]{1,0:T(8,128)(2,1)} %get-tuple-element.146.refs_2_, bf16[768,1536]{1,0:T(8,128)(2,1)} %weight_grad.4.refs_3_), custom_call_target="tpu_custom_call" | custom-call | flops 49999998976 | bytes 100000000 | tf_op jit(solution)/shard_map/weight_grad/pallas_call | solution.py:338
  64.0 2.8 combine.19
  66.8 2.9 collective-permute-start.7
  71.1 15.2 %ffn_bwd.2 = (bf16[768,1536]{1,0:T(8,128)(2,1)}, f32[1,1536]{1,0:T(1,128)}, f32[1024,768]{1,0:T(8,128)}) custom-call(s32[2]{0:T(128)} %pad_add_fusion.place.core.refs_0_, bf16[1024,768]{1,0:T(8,128)(2,1)} %get-tuple-element.145.refs_1_, bf16[1024,3072]{1,0:T(8,128)(2,1)} %get-tuple-element.149.refs_2_, ...), custom_call_target="tpu_custom_call" | custom-call | flops 49999998976 | bytes 100000000 | tf_op jit(solution)/shard_map/ffn_bwd/pallas_call | solution.py:445
  89.4 21.9 %ffn_bwd.3 = (bf16[768,1920]{1,0:T(8,128)(2,1)}, f32[1,1536]{1,0:T(1,128)}, f32[1024,768]{1,0:T(8,128)}, bf16[1024,768]{1,0:T(8,128)(2,1)}, f32[8,768]{1,0:T(8,128)}, /*index=5*/bf16[768,384]{1,0:T(8,128)(2,1)}) custom-call(s32[2]{0:T(128)} %pad_add_fusion.place.core.refs_0_, bf16[1024,768]{1,0:T(8,128)(2,1)} %get-tuple-element.145.refs_1_, ...), custom_call_target="tpu_custom_call" | custom-call | flops 49999998976 | bytes 100000000 | tf_op jit(solution)/shard_map/ffn_bwd/pallas_call | solution.py:445
  114.3 2.9 %collective-permute-start.16 = (bf16[48,1536]{1,0:T(8,128)(2,1)}, bf16[48,1536]{1,0:T(8,128)(2,1)}, u32[]{:S(2)}, u32[]{:S(2)}) collective-permute-start(bf16[48,1536]{1,0:T(8,128)(2,1)} %get-tuple-element.162.refs_6_), channel_id=1, source_target_pairs={{0,16},{2,18},{4,20},{6,22},{8,24},{10,26},{12,28},{14,30},{16,0},... | collective-permute-start | bytes 442376 | tf_op jit(solution)/shard_map/ppermute | solution.py:850
  118.8 3.0 %combine.22 = (bf16[192,1920]{1,0:T(8,128)(2,1)}, bf16[192,1920]{1,0:T(8,128)(2,1)}) custom-call(bf16[768,1920]{1,0:T(8,128)(2,1)} %get-tuple-element.165.refs_0_.refs_3_.refs_6_.refs_9_.refs_4_, bf16[768,1536]{1,0:T(8,128)(2,1)} %collective-permute-done.11.refs_1_.refs_4_.refs_7_.refs_10_.refs_5_, ...), custom_call_target="tpu_custom_call" | custom-call | tf_op jit(solution)/shard_map/combine/pallas_call | solution.py:739
  125.1 16.7 %attend_back.1 = (bf16[1024,2304]{1,0:T(8,128)(2,1)}, f32[8,768]{1,0:T(8,128)}) custom-call(bf16[1024,768]{1,0:T(8,128)(2,1)} %get-tuple-element.174.refs_0_.refs_5_, bf16[4,12,256,256]{3,2,1,0:T(8,128)(2,1)} %get-tuple-element.175.refs_1_, bf16[1024,2304]{1,0:T(8,128)(2,1)} %get-tuple-element.176.refs_2_, bf16[384,768]{1,0:T(8,128)(2,1)} %refs_3_.3, ...), custom_call_target="tpu_custom_call" | custom-call | flops 49999998976 | bytes 100000000 | tf_op jit(solution)/shard_map/attend_back/pallas_call | solution.py:537
  143.2 2.8 update.3
  151.5 6.2 %weight_grad.6 = bf16[768,1152]{1,0:T(8,128)(2,1)} custom-call(s32[2]{0:T(128)} %pad_add_fusion.place.core.refs_0_, bf16[2048,768]{1,0:T(8,128)(2,1)} %refs_1_.3, bf16[1024,2304]{1,0:T(8,128)(2,1)} %get-tuple-element.186.refs_2_.refs_1_, bf16[48,1536]{1,0:T(8,128)(2,1)} %get-tuple-element.181.refs_3_.refs_0_, bf16[96,1920]{1,0:T(8,128)(2,1)} %get-tuple-element.184.refs_4_, ...), custom_call_target="tpu_custom_call" | custom-call | flops 49999998976 | bytes 100000000 | tf_op jit(solution)/shard_map/weight_grad/pallas_call | solution.py:338
  167.3 6.2 %weight_grad.7.refs_0_.refs_2_.refs_4_.refs_6_.refs_3_.refs_8_ = bf16[768,1152]{1,0:T(8,128)(2,1)} custom-call(s32[2]{0:T(128)} %pad_add_fusion.place.core.refs_0_, bf16[2048,768]{1,0:T(8,128)(2,1)} %refs_1_.3, bf16[1024,2304]{1,0:T(8,128)(2,1)} %get-tuple-element.186.refs_2_.refs_1_, bf16[96,1920]{1,0:T(8,128)(2,1)} %combine.24.refs_3_, ...), custom_call_target="tpu_custom_call" | custom-call | flops 49999998976 | bytes 100000000 | tf_op jit(solution)/shard_map/weight_grad/pallas_call | solution.py:338
  175.4 4.4 %collective-permute-done.21.refs_5_ = bf16[96,1920]{1,0:T(8,128)(2,1)} collective-permute-done((bf16[96,1920]{1,0:T(8,128)(2,1)}, bf16[96,1920]{1,0:T(8,128)(2,1)}, u32[]{:S(2)}, u32[]{:S(2)}) %collective-permute-start.21) | collective-permute-done | bytes 368672 | tf_op jit(solution)/shard_map/ppermute | solution.py:850
  187.0 10.6 %input_side.1 = (bf16[1024,768]{1,0:T(8,128)(2,1)}, f32[2048,768]{1,0:T(8,128)}) custom-call(s32[2]{0:T(128)} %pad_add_fusion.place.core.refs_0_, bf16[1024,2304]{1,0:T(8,128)(2,1)} %get-tuple-element.186.refs_2_.refs_1_, bf16[3,768,384]{2,1,0:T(8,128)(2,1)} %refs_2_.1, bf16[3,768,384]{2,1,0:T(8,128)(2,1)} %collective-permute-done.w1_ref.refs_3_, ...), custom_call_target="tpu_custom_call" | custom-call | flops 49999998976 | bytes 100000000 | tf_op jit(solution)/shard_map/input_side/pallas_call | solution.py:581
  205.6 3.0 %update.4 = (f32[48,1536]{1,0:T(8,128)}, f32[48,1536]{1,0:T(8,128)}, f32[48,1536]{1,0:T(8,128)}, f32[48,384]{1,0:T(8,128)}, f32[48,384]{1,0:T(8,128)}, /*index=5*/f32[48,384]{1,0:T(8,128)}, bf16[48,1920]{1,0:T(8,128)(2,1)}) custom-call(bf16[768,1920]{1,0:T(8,128)(2,1)} %get-tuple-element.165.refs_0_.refs_3_.refs_6_.refs_9_.refs_4_, ...), custom_call_target="tpu_custom_call" | custom-call | tf_op jit(solution)/shard_map/update/pallas_call | solution.py:810
  211.0 3.3 %put_other.2 = bf16[2048,768]{1,0:T(8,128)(2,1)} custom-call(s32[2]{0:T(128)} %pad_add_fusion.place.core.refs_0_, bf16[1024,768]{1,0:T(8,128)(2,1)} %collective-permute-done.13.refs_1_, bf16[2048,768]{1,0:T(8,128)(2,1)} %get-tuple-element.173.refs_2_, bf16[48,1920]{1,0:T(8,128)(2,1)} %get-tuple-element.207.refs_3_.refs_0_, ...), custom_call_target="tpu_custom_call", output_to_operand_aliasing={{}: (2, {})} | custom-call | flops 49999998976 | bytes 100000000 | tf_op jit(solution)/shard_map/put_other/pallas_call | solution.py:829
  232.6 3.9 %put_other.3 = f32[2048,768]{1,0:T(8,128)} custom-call(s32[2]{0:T(128)} %pad_add_fusion.place.core.refs_0_, bf16[1024,768]{1,0:T(8,128)(2,1)} %collective-permute-done.35.refs_1_, f32[2048,768]{1,0:T(8,128)} %get-tuple-element.220.refs_2_, bf16[96,1920]{1,0:T(8,128)(2,1)} %combine.32.refs_3_.refs_0_, ...), custom_call_target="tpu_custom_call", output_to_operand_aliasing={{}: (2, {})} | custom-call | flops 49999998976 | bytes 100000000 | tf_op jit(solution)/shard_map/put_other/pallas_call | solution.py:829
  243.7 3.1 %collective-permute-done.41.refs_1_ = bf16[96,1920]{1,0:T(8,128)(2,1)} collective-permute-done((bf16[96,1920]{1,0:T(8,128)(2,1)}, bf16[96,1920]{1,0:T(8,128)(2,1)}, u32[]{:S(2)}, u32[]{:S(2)}) %collective-permute-start.41) | collective-permute-done | bytes 368672 | tf_op jit(solution)/shard_map/ppermute | solution.py:850
  257.1 4.5 %gather_place.3 = bf16[1536,768]{1,0:T(8,128)(2,1)} custom-call(s32[2]{0:T(128)} %pad_add_fusion.place.core.refs_0_, bf16[192,1536]{1,0:T(8,128)(2,1)} %combine.28.refs_8_.refs_1_, bf16[192,1536]{1,0:T(8,128)(2,1)} %collective-permute-done.33.refs_0_.refs_2_, bf16[192,1536]{1,0:T(8,128)(2,1)} %collective-permute-done.34.refs_1_.refs_3_, ...), custom_call_target="tpu_custom_call" | custom-call | flops 49999998976 | bytes 100000000 | tf_op jit(solution)/shard_map/gather_place/pallas_call | solution.py:674
  276.4 4.6 %collective-permute-done.47.refs_1_.refs_3_ = bf16[576,384]{1,0:T(8,128)(2,1)} collective-permute-done((bf16[576,384]{1,0:T(8,128)(2,1)}, bf16[576,384]{1,0:T(8,128)(2,1)}, u32[]{:S(2)}, u32[]{:S(2)}) %collective-permute-start.47) | collective-permute-done | bytes 442400 | tf_op jit(solution)/shard_map/ppermute | solution.py:850
  286.9 4.3 %gather_place.4 = (bf16[768,1536]{1,0:T(8,128)(2,1)}, bf16[384,768]{1,0:T(8,128)(2,1)}) custom-call(s32[2]{0:T(128)} %pad_add_fusion.place.core.refs_0_, bf16[192,1920]{1,0:T(8,128)(2,1)} %combine.33.refs_7_.refs_1_, bf16[192,1920]{1,0:T(8,128)(2,1)} %collective-permute-done.48.refs_0_.refs_2_, bf16[192,1920]{1,0:T(8,128)(2,1)} %collective-permute-done.49.refs_1_.refs_3_, ...), custom_call_target="tpu_custom_call" | custom-call | flops 49999998976 | bytes 100000000 | tf_op jit(solution)/shard_map/gather_place/pallas_call | solution.py:674
  291.2 3.5 %gather_place.5 = bf16[3,768,384]{2,1,0:T(8,128)(2,1)} custom-call(s32[2]{0:T(128)} %pad_add_fusion.place.core.refs_0_, bf16[576,384]{1,0:T(8,128)(2,1)} %combine.35.refs_1_, bf16[576,384]{1,0:T(8,128)(2,1)} %collective-permute-done.46.refs_0_.refs_2_, bf16[576,384]{1,0:T(8,128)(2,1)} %collective-permute-done.47.refs_1_.refs_3_, ...), custom_call_target="tpu_custom_call" | custom-call | flops 49999998976 | bytes 100000000 | tf_op jit(solution)/shard_map/gather_place/pallas_call | solution.py:674
  (138 shorter events, 110.8 us)
Async XLA Ops:
  5.7 19.7 %collective-permute-start.5 = (f32[1,1536]{1,0:T(1,128)}, f32[1,1536]{1,0:T(1,128)}, u32[]{:S(2)}, u32[]{:S(2)}) collective-permute-start(f32[1,1536]{1,0:T(1,128)} %broadcast_in_dim.3.b0_ref), channel_id=1, source_target_pairs={{0,1},{1,0},{2,3},{3,2},{4,5},{5,4},{6,7},{7,6},{8,9},{9,8},{10,11... | collective-permute-start | bytes 18440 | tf_op jit(solution)/shard_map/ppermute | solution.py:846
  6.1 19.3 %collective-permute-start.3 = (bf16[768,1536]{1,0:T(8,128)(2,1)}, bf16[768,1536]{1,0:T(8,128)(2,1)}, u32[]{:S(2)}, u32[]{:S(2)}) collective-permute-start(bf16[768,1536]{1,0:T(8,128)(2,1)} %refs_3_.2), channel_id=1, source_target_pairs={{0,1},{1,0},{2,3},{3,2},{4,5},{5,4},{6,7},{7,6},{8,9},{9,8},{10,11... | collective-permute-start | bytes 7077896 | tf_op jit(solution)/shard_map/ppermute | solution.py:846
  6.2 19.2 %collective-permute-start.4 = (bf16[1536,768]{1,0:T(8,128)(2,1)}, bf16[1536,768]{1,0:T(8,128)(2,1)}, u32[]{:S(2)}, u32[]{:S(2)}) collective-permute-start(bf16[1536,768]{1,0:T(8,128)(2,1)} %refs_4_.1), channel_id=1, source_target_pairs={{0,1},{1,0},{2,3},{3,2},{4,5},{5,4},{6,7},{7,6},{8,9},{9,8},{10,11... | collective-permute-start | bytes 7077896 | tf_op jit(solution)/shard_map/ppermute | solution.py:846
  66.8 19.6 %collective-permute-start.7 = (bf16[192,1536]{1,0:T(8,128)(2,1)}, bf16[192,1536]{1,0:T(8,128)(2,1)}, u32[]{:S(2)}, u32[]{:S(2)}) collective-permute-start(bf16[192,1536]{1,0:T(8,128)(2,1)} %get-tuple-element.147.refs_10_), channel_id=1, source_target_pairs={{0,2},{2,0},{4,6},{6,4},{8,10},{10,8},{12,14},{14,12},{16,18},{18,... | collective-permute-start | bytes 1769480 | tf_op jit(solution)/shard_map/ppermute | solution.py:850
  69.6 16.7 %collective-permute-start.8 = (bf16[192,1536]{1,0:T(8,128)(2,1)}, bf16[192,1536]{1,0:T(8,128)(2,1)}, u32[]{:S(2)}, u32[]{:S(2)}) collective-permute-start(bf16[192,1536]{1,0:T(8,128)(2,1)} %get-tuple-element.148.refs_11_), channel_id=1, source_target_pairs={{0,4},{2,6},{4,0},{6,2},{8,12},{10,14},{12,8},{14,10},{16,20},{18,... | collective-permute-start | bytes 1769480 | tf_op jit(solution)/shard_map/ppermute | solution.py:850
  88.7 22.6 %collective-permute-start.9 = (bf16[96,1536]{1,0:T(8,128)(2,1)}, bf16[96,1536]{1,0:T(8,128)(2,1)}, u32[]{:S(2)}, u32[]{:S(2)}) collective-permute-start(bf16[96,1536]{1,0:T(8,128)(2,1)} %get-tuple-element.156.refs_10_), channel_id=1, source_target_pairs={{0,2},{2,0},{4,6},{6,4},{8,10},{10,8},{12,14},{14,12},{16,18},{18,... | collective-permute-start | bytes 884744 | tf_op jit(solution)/shard_map/ppermute | solution.py:850
  89.3 22.1 %collective-permute-start.10 = (bf16[96,1536]{1,0:T(8,128)(2,1)}, bf16[96,1536]{1,0:T(8,128)(2,1)}, u32[]{:S(2)}, u32[]{:S(2)}) collective-permute-start(bf16[96,1536]{1,0:T(8,128)(2,1)} %get-tuple-element.157.refs_11_), channel_id=1, source_target_pairs={{0,4},{2,6},{4,0},{6,2},{8,12},{10,14},{12,8},{14,10},{16,20},{18,... | collective-permute-start | bytes 884744 | tf_op jit(solution)/shard_map/ppermute | solution.py:850
  89.4 29.4 %collective-permute-start.11 = (bf16[768,1536]{1,0:T(8,128)(2,1)}, bf16[768,1536]{1,0:T(8,128)(2,1)}, u32[]{:S(2)}, u32[]{:S(2)}) collective-permute-start(bf16[768,1536]{1,0:T(8,128)(2,1)} %get-tuple-element.167), channel_id=1, source_target_pairs={{0,1},{1,0},{2,3},{3,2},{4,5},{5,4},{6,7},{7,6},{8,9},{9,8},{10,11... | collective-permute-start | bytes 7077896 | tf_op jit(solution)/shard_map/ppermute | solution.py:846
  114.3 27.4 %collective-permute-start.16 = (bf16[48,1536]{1,0:T(8,128)(2,1)}, bf16[48,1536]{1,0:T(8,128)(2,1)}, u32[]{:S(2)}, u32[]{:S(2)}) collective-permute-start(bf16[48,1536]{1,0:T(8,128)(2,1)} %get-tuple-element.162.refs_6_), channel_id=1, source_target_pairs={{0,16},{2,18},{4,20},{6,22},{8,24},{10,26},{12,28},{14,30},{16,0},... | collective-permute-start | bytes 442376 | tf_op jit(solution)/shard_map/ppermute | solution.py:850
  117.2 24.5 %collective-permute-start.17 = (bf16[48,1536]{1,0:T(8,128)(2,1)}, bf16[48,1536]{1,0:T(8,128)(2,1)}, u32[]{:S(2)}, u32[]{:S(2)}) collective-permute-start(bf16[48,1536]{1,0:T(8,128)(2,1)} %get-tuple-element.163.refs_7_), channel_id=1, source_target_pairs={{0,8},{2,10},{4,12},{6,14},{8,0},{10,2},{12,4},{14,6},{16,24},{18,... | collective-permute-start | bytes 442376 | tf_op jit(solution)/shard_map/ppermute | solution.py:850
  118.8 22.9 %collective-permute-start.18 = (bf16[48,1536]{1,0:T(8,128)(2,1)}, bf16[48,1536]{1,0:T(8,128)(2,1)}, u32[]{:S(2)}, u32[]{:S(2)}) collective-permute-start(bf16[48,1536]{1,0:T(8,128)(2,1)} %get-tuple-element.164.refs_8_), channel_id=1, source_target_pairs={{0,24},{2,26},{4,28},{6,30},{8,16},{10,18},{12,20},{14,22},{16,8},... | collective-permute-start | bytes 442376 | tf_op jit(solution)/shard_map/ppermute | solution.py:850
  121.9 26.1 %collective-permute-start.14 = (bf16[192,1920]{1,0:T(8,128)(2,1)}, bf16[192,1920]{1,0:T(8,128)(2,1)}, u32[]{:S(2)}, u32[]{:S(2)}) collective-permute-start(bf16[192,1920]{1,0:T(8,128)(2,1)} %get-tuple-element.170.refs_9_), channel_id=1, source_target_pairs={{0,2},{2,0},{4,6},{6,4},{8,10},{10,8},{12,14},{14,12},{16,18},{18,... | collective-permute-start | bytes 2211848 | tf_op jit(solution)/shard_map/ppermute | solution.py:850
  123.6 24.4 %collective-permute-start.15 = (bf16[192,1920]{1,0:T(8,128)(2,1)}, bf16[192,1920]{1,0:T(8,128)(2,1)}, u32[]{:S(2)}, u32[]{:S(2)}) collective-permute-start(bf16[192,1920]{1,0:T(8,128)(2,1)} %get-tuple-element.171.refs_10_), channel_id=1, source_target_pairs={{0,4},{2,6},{4,0},{6,2},{8,12},{10,14},{12,8},{14,10},{16,20},{18,... | collective-permute-start | bytes 2211848 | tf_op jit(solution)/shard_map/ppermute | solution.py:850
  143.2 16.3 %collective-permute-start.22 = (f32[24,768]{1,0:T(8,128)}, f32[24,768]{1,0:T(8,128)}, u32[]{:S(2)}, u32[]{:S(2)}) collective-permute-start(f32[24,768]{1,0:T(8,128)} %get-tuple-element.189.refs_6_), channel_id=1, source_target_pairs={{0,1},{1,0},{2,3},{3,2},{4,5},{5,4},{6,7},{7,6},{8,9},{9,8},{10,11... | collective-permute-start | bytes 221192 | tf_op jit(solution)/shard_map/ppermute | solution.py:846
  147.7 60.8 %collective-permute-start.13 = (bf16[1024,768]{1,0:T(8,128)(2,1)}, bf16[1024,768]{1,0:T(8,128)(2,1)}, u32[]{:S(2)}, u32[]{:S(2)}) collective-permute-start(bf16[1024,768]{1,0:T(8,128)(2,1)} %get-tuple-element.172), channel_id=1, source_target_pairs={{0,1},{1,0},{2,3},{3,2},{4,5},{5,4},{6,7},{7,6},{8,9},{9,8},{10,11... | collective-permute-start | bytes 4718600 | tf_op jit(solution)/shard_map/ppermute | solution.py:846
  161.1 40.9 %collective-permute-start.29 = (f32[24,768]{1,0:T(8,128)}, f32[24,768]{1,0:T(8,128)}, u32[]{:S(2)}, u32[]{:S(2)}) collective-permute-start(f32[24,768]{1,0:T(8,128)} %add.60.refs_4_), channel_id=1, source_target_pairs={{0,2},{2,0},{4,6},{6,4},{8,10},{10,8},{12,14},{14,12},{16,18},{18,... | collective-permute-start | bytes 221192 | tf_op jit(solution)/shard_map/ppermute | solution.py:850
  167.3 15.1 %collective-permute-start.25 = (bf16[768,1152]{1,0:T(8,128)(2,1)}, bf16[768,1152]{1,0:T(8,128)(2,1)}, u32[]{:S(2)}, u32[]{:S(2)}) collective-permute-start(bf16[768,1152]{1,0:T(8,128)(2,1)} %weight_grad.6), channel_id=1, source_target_pairs={{0,1},{1,0},{2,3},{3,2},{4,5},{5,4},{6,7},{7,6},{8,9},{9,8},{10,11... | collective-permute-start | bytes 5308424 | tf_op jit(solution)/shard_map/ppermute | solution.py:846
  181.9 21.9 %collective-permute-start.24 = (bf16[48,1920]{1,0:T(8,128)(2,1)}, bf16[48,1920]{1,0:T(8,128)(2,1)}, u32[]{:S(2)}, u32[]{:S(2)}) collective-permute-start(bf16[48,1920]{1,0:T(8,128)(2,1)} %combine.26.refs_7_), channel_id=1, source_target_pairs={{0,16},{2,18},{4,20},{6,22},{8,24},{10,26},{12,28},{14,30},{16,0},... | collective-permute-start | bytes 552968 | tf_op jit(solution)/shard_map/ppermute | solution.py:850
  197.6 16.7 %collective-permute-start.34 = (bf16[192,1536]{1,0:T(8,128)(2,1)}, bf16[192,1536]{1,0:T(8,128)(2,1)}, u32[]{:S(2)}, u32[]{:S(2)}) collective-permute-start(bf16[192,1536]{1,0:T(8,128)(2,1)} %combine.28.refs_8_.refs_1_), channel_id=1, source_target_pairs={{0,4},{2,6},{4,0},{6,2},{8,12},{10,14},{12,8},{14,10},{16,20},{18,... | collective-permute-start | bytes 1769480 | tf_op jit(solution)/shard_map/ppermute | solution.py:850
  198.0 16.4 %collective-permute-start.33 = (bf16[192,1536]{1,0:T(8,128)(2,1)}, bf16[192,1536]{1,0:T(8,128)(2,1)}, u32[]{:S(2)}, u32[]{:S(2)}) collective-permute-start(bf16[192,1536]{1,0:T(8,128)(2,1)} %combine.28.refs_8_.refs_1_), channel_id=1, source_target_pairs={{0,2},{2,0},{4,6},{6,4},{8,10},{10,8},{12,14},{14,12},{16,18},{18,... | collective-permute-start | bytes 1769480 | tf_op jit(solution)/shard_map/ppermute | solution.py:850
  224.1 30.7 %collective-permute-start.43 = (bf16[96,1536]{1,0:T(8,128)(2,1)}, bf16[96,1536]{1,0:T(8,128)(2,1)}, u32[]{:S(2)}, u32[]{:S(2)}) collective-permute-start(bf16[96,1536]{1,0:T(8,128)(2,1)} %get-tuple-element.211), channel_id=1, source_target_pairs={{0,4},{2,6},{4,0},{6,2},{8,12},{10,14},{12,8},{14,10},{16,20},{18,... | collective-permute-start | bytes 884744 | tf_op jit(solution)/shard_map/ppermute | solution.py:850
  224.6 32.5 %collective-permute-start.44 = (bf16[96,1536]{1,0:T(8,128)(2,1)}, bf16[96,1536]{1,0:T(8,128)(2,1)}, u32[]{:S(2)}, u32[]{:S(2)}) collective-permute-start(bf16[96,1536]{1,0:T(8,128)(2,1)} %get-tuple-element.212), channel_id=1, source_target_pairs={{0,2},{2,0},{4,6},{6,4},{8,10},{10,8},{12,14},{14,12},{16,18},{18,... | collective-permute-start | bytes 884744 | tf_op jit(solution)/shard_map/ppermute | solution.py:850
  248.9 19.7 %collective-permute-start.49 = (bf16[192,1920]{1,0:T(8,128)(2,1)}, bf16[192,1920]{1,0:T(8,128)(2,1)}, u32[]{:S(2)}, u32[]{:S(2)}) collective-permute-start(bf16[192,1920]{1,0:T(8,128)(2,1)} %combine.33.refs_7_.refs_1_), channel_id=1, source_target_pairs={{0,4},{2,6},{4,0},{6,2},{8,12},{10,14},{12,8},{14,10},{16,20},{18,... | collective-permute-start | bytes 2211848 | tf_op jit(solution)/shard_map/ppermute | solution.py:850
  250.0 18.6 %collective-permute-start.48 = (bf16[192,1920]{1,0:T(8,128)(2,1)}, bf16[192,1920]{1,0:T(8,128)(2,1)}, u32[]{:S(2)}, u32[]{:S(2)}) collective-permute-start(bf16[192,1920]{1,0:T(8,128)(2,1)} %combine.33.refs_7_.refs_1_), channel_id=1, source_target_pairs={{0,2},{2,0},{4,6},{6,4},{8,10},{10,8},{12,14},{14,12},{16,18},{18,... | collective-permute-start | bytes 2211848 | tf_op jit(solution)/shard_map/ppermute | solution.py:850
  (31 other events, 321.7 us)

commit v5 on v4

--- a/solution.py
+++ b/solution.py
@@ -1045,10 +1045,9 @@
         bias_row, bias_other, norm_vectors,
     )
 
-    steps = n_bias // BLOCK_FF
     weight = partial(weight_grad, place, n_dp)
-    contract_theirs = weight(branch_grad, active, steps, steps, BLOCK_FF)
-    contract_mine = weight(branch_grad, active, 0, steps, BLOCK_FF, deps=(contract_theirs,))
+    contract_theirs = weight(branch_grad, active, 2, 2, n_bias // 2)
+    contract_mine = weight(branch_grad, active, 0, 2, n_bias // 2, deps=(contract_theirs,))
     contract_flow = Flow(scatter_flow(contract_mine, [swap(contract_theirs)], n_dp, True), contract_then)
     sends = contract_flow.advance()
     expand_theirs, bias_theirs, hidden_sofar = ffn_bwd(

time: 296 us -> 296 us (level)
  no operation moved by 1% of the time
where the time goes in v5:
time: 296 us; the launch traced here: 294 us
  Pallas kernels  204 us (69%)
  starting transfers between devices  54.5 us (18%)
  waiting for transfers between devices  20 us (7%)
  other arithmetic  11.9 us (4%)
  local copies, waits for them, and re-layouts  3.1 us (1%)
    ppermute x42, starting transfers between devices, across(): return lax.ppermute(value, 'dp', [(i, i ^ apart) for i in range(count)])  51.7 us
    pallas_call x19, Pallas kernels, combine(): pl.pallas_call(with_deps(partial(combine_kernel, plan), 0, len(blocks.arr...  41.1 us
    pallas_call x2, Pallas kernels, ffn_bwd(): pl.pallas_call(with_deps(partial(ffn_bwd_kernel, final, n_dp), 1, 9, deps...  37.1 us
    pallas_call x4, Pallas kernels, weight_grad(): pl.pallas_call(with_deps(partial(weight_kernel, n_dp), 1, 2, deps), out_s...  25.4 us
    pallas_call x1, Pallas kernels, ffn_fwd(): pl.pallas_call(ffn_fwd_kernel, out_shape=(jax.ShapeDtypeStruct((tokens, 2...  24.7 us
    pallas_call x1, Pallas kernels, attend(): pl.pallas_call(attend_kernel, out_shape=(jax.ShapeDtypeStruct((tokens, 6...  18.8 us
    ppermute x42, waiting for transfers between devices, across(): return lax.ppermute(value, 'dp', [(i, i ^ apart) for i in range(count)])  17.9 us
    pallas_call x1, Pallas kernels, attend_back(): pl.pallas_call(with_deps(partial(attend_back_kernel, start), 0, 6, deps),...  16.7 us
  transfers between devices with their start and end apart: 55, of which 9 were waited for; matrix products, arithmetic and copies ran while one was open for 5% of the time, Pallas kernels for 55%

profile of v5, /device:TPU:0, one launch (start us, length us, event | category | flops | bytes accessed | tf_op | source)
XLA Modules:
  0.0 294.0 jit_solution(14844222657401260418)
XLA Ops:
  6.6 18.8 %attend.1 = (bf16[1024,2304]{1,0:T(8,128)(2,1)}, bf16[4,12,256,256]{3,2,1,0:T(8,128)(2,1)}, bf16[1024,768]{1,0:T(8,128)(2,1)}, f32[1024,768]{1,0:T(8,128)}) custom-call(s32[2]{0:T(128)} %pad_add_fusion.place.core.refs_0_, s32[8]{0:T(128)} %lengths.1, bf16[2048,768]{1,0:T(8,128)(2,1)} %refs_1_.3, s32[8,256]{1,0:T(8,128)} %mask_ref.1, ...), custom_call_target="tpu_custom_call" | custom-call | flops 49999998976 | bytes 100000000 | tf_op jit(solution)/shard_map/attend/pallas_call | solution.py:145
  25.4 24.7 %ffn_fwd.1 = (bf16[1024,3072]{1,0:T(8,128)(2,1)}, bf16[1024,3072]{1,0:T(8,128)(2,1)}, bf16[1024,768]{1,0:T(8,128)(2,1)}, f32[1024,768]{1,0:T(8,128)}, bf16[1024,...) custom-call(s32[2]{0:T(128)} %pad_add_fusion.place.core.refs_0_, ...), custom_call_target="tpu_custom_call" | custom-call | flops 49999998976 | bytes 100000000 | tf_op jit(solution)/shard_map/ffn_fwd/pallas_call | solution.py:244
  50.2 6.5 %weight_grad.4.refs_3_ = bf16[768,1536]{1,0:T(8,128)(2,1)} custom-call(s32[2]{0:T(128)} %pad_add_fusion.place.core.refs_0_, bf16[1024,768]{1,0:T(8,128)(2,1)} %get-tuple-element.145.refs_1_, bf16[1024,3072]{1,0:T(8,128)(2,1)} %get-tuple-element.146.refs_2_), custom_call_target="tpu_custom_call" | custom-call | flops 49999998976 | bytes 100000000 | tf_op jit(solution)/shard_map/weight_grad/pallas_call | solution.py:338
  56.8 6.5 %weight_grad.5.refs_0_.refs_2_.refs_4_.refs_6_.refs_3_.refs_8_ = bf16[768,1536]{1,0:T(8,128)(2,1)} custom-call(s32[2]{0:T(128)} %pad_add_fusion.place.core.refs_0_, bf16[1024,768]{1,0:T(8,128)(2,1)} %get-tuple-element.145.refs_1_, bf16[1024,3072]{1,0:T(8,128)(2,1)} %get-tuple-element.146.refs_2_, bf16[768,1536]{1,0:T(8,128)(2,1)} %weight_grad.4.refs_3_), custom_call_target="tpu_custom_call" | custom-call | flops 49999998976 | bytes 100000000 | tf_op jit(solution)/shard_map/weight_grad/pallas_call | solution.py:338
  63.3 2.8 combine.19
  66.0 2.9 collective-permute-start.7
  70.4 15.2 %ffn_bwd.2 = (bf16[768,1536]{1,0:T(8,128)(2,1)}, f32[1,1536]{1,0:T(1,128)}, f32[1024,768]{1,0:T(8,128)}) custom-call(s32[2]{0:T(128)} %pad_add_fusion.place.core.refs_0_, bf16[1024,768]{1,0:T(8,128)(2,1)} %get-tuple-element.145.refs_1_, bf16[1024,3072]{1,0:T(8,128)(2,1)} %get-tuple-element.149.refs_2_, ...), custom_call_target="tpu_custom_call" | custom-call | flops 49999998976 | bytes 100000000 | tf_op jit(solution)/shard_map/ffn_bwd/pallas_call | solution.py:445
  88.7 21.9 %ffn_bwd.3 = (bf16[768,1920]{1,0:T(8,128)(2,1)}, f32[1,1536]{1,0:T(1,128)}, f32[1024,768]{1,0:T(8,128)}, bf16[1024,768]{1,0:T(8,128)(2,1)}, f32[8,768]{1,0:T(8,128)}, /*index=5*/bf16[768,384]{1,0:T(8,128)(2,1)}) custom-call(s32[2]{0:T(128)} %pad_add_fusion.place.core.refs_0_, bf16[1024,768]{1,0:T(8,128)(2,1)} %get-tuple-element.145.refs_1_, ...), custom_call_target="tpu_custom_call" | custom-call | flops 49999998976 | bytes 100000000 | tf_op jit(solution)/shard_map/ffn_bwd/pallas_call | solution.py:445
  113.5 2.9 %collective-permute-start.16 = (bf16[48,1536]{1,0:T(8,128)(2,1)}, bf16[48,1536]{1,0:T(8,128)(2,1)}, u32[]{:S(2)}, u32[]{:S(2)}) collective-permute-start(bf16[48,1536]{1,0:T(8,128)(2,1)} %get-tuple-element.162.refs_6_), channel_id=1, source_target_pairs={{0,16},{2,18},{4,20},{6,22},{8,24},{10,26},{12,28},{14,30},{16,0},... | collective-permute-start | bytes 442376 | tf_op jit(solution)/shard_map/ppermute | solution.py:850
  118.1 3.0 %combine.22 = (bf16[192,1920]{1,0:T(8,128)(2,1)}, bf16[192,1920]{1,0:T(8,128)(2,1)}) custom-call(bf16[768,1920]{1,0:T(8,128)(2,1)} %get-tuple-element.165.refs_0_.refs_3_.refs_6_.refs_9_.refs_4_, bf16[768,1536]{1,0:T(8,128)(2,1)} %collective-permute-done.11.refs_1_.refs_4_.refs_7_.refs_10_.refs_5_, ...), custom_call_target="tpu_custom_call" | custom-call | tf_op jit(solution)/shard_map/combine/pallas_call | solution.py:739
  124.3 16.7 %attend_back.1 = (bf16[1024,2304]{1,0:T(8,128)(2,1)}, f32[8,768]{1,0:T(8,128)}) custom-call(bf16[1024,768]{1,0:T(8,128)(2,1)} %get-tuple-element.174.refs_0_.refs_5_, bf16[4,12,256,256]{3,2,1,0:T(8,128)(2,1)} %get-tuple-element.175.refs_1_, bf16[1024,2304]{1,0:T(8,128)(2,1)} %get-tuple-element.176.refs_2_, bf16[384,768]{1,0:T(8,128)(2,1)} %refs_3_.3, ...), custom_call_target="tpu_custom_call" | custom-call | flops 49999998976 | bytes 100000000 | tf_op jit(solution)/shard_map/attend_back/pallas_call | solution.py:537
  142.5 2.8 update.3
  150.8 6.2 %weight_grad.6 = bf16[768,1152]{1,0:T(8,128)(2,1)} custom-call(s32[2]{0:T(128)} %pad_add_fusion.place.core.refs_0_, bf16[2048,768]{1,0:T(8,128)(2,1)} %refs_1_.3, bf16[1024,2304]{1,0:T(8,128)(2,1)} %get-tuple-element.186.refs_2_.refs_1_, bf16[48,1536]{1,0:T(8,128)(2,1)} %get-tuple-element.181.refs_3_.refs_0_, bf16[96,1920]{1,0:T(8,128)(2,1)} %get-tuple-element.184.refs_4_, ...), custom_call_target="tpu_custom_call" | custom-call | flops 49999998976 | bytes 100000000 | tf_op jit(solution)/shard_map/weight_grad/pallas_call | solution.py:338
  166.5 6.2 %weight_grad.7.refs_0_.refs_2_.refs_4_.refs_6_.refs_3_.refs_8_ = bf16[768,1152]{1,0:T(8,128)(2,1)} custom-call(s32[2]{0:T(128)} %pad_add_fusion.place.core.refs_0_, bf16[2048,768]{1,0:T(8,128)(2,1)} %refs_1_.3, bf16[1024,2304]{1,0:T(8,128)(2,1)} %get-tuple-element.186.refs_2_.refs_1_, bf16[96,1920]{1,0:T(8,128)(2,1)} %combine.24.refs_3_, ...), custom_call_target="tpu_custom_call" | custom-call | flops 49999998976 | bytes 100000000 | tf_op jit(solution)/shard_map/weight_grad/pallas_call | solution.py:338
  174.7 4.4 %collective-permute-done.21.refs_5_ = bf16[96,1920]{1,0:T(8,128)(2,1)} collective-permute-done((bf16[96,1920]{1,0:T(8,128)(2,1)}, bf16[96,1920]{1,0:T(8,128)(2,1)}, u32[]{:S(2)}, u32[]{:S(2)}) %collective-permute-start.21) | collective-permute-done | bytes 368672 | tf_op jit(solution)/shard_map/ppermute | solution.py:850
  186.3 10.6 %input_side.1 = (bf16[1024,768]{1,0:T(8,128)(2,1)}, f32[2048,768]{1,0:T(8,128)}) custom-call(s32[2]{0:T(128)} %pad_add_fusion.place.core.refs_0_, bf16[1024,2304]{1,0:T(8,128)(2,1)} %get-tuple-element.186.refs_2_.refs_1_, bf16[3,768,384]{2,1,0:T(8,128)(2,1)} %refs_2_.1, bf16[3,768,384]{2,1,0:T(8,128)(2,1)} %collective-permute-done.w1_ref.refs_3_, ...), custom_call_target="tpu_custom_call" | custom-call | flops 49999998976 | bytes 100000000 | tf_op jit(solution)/shard_map/input_side/pallas_call | solution.py:581
  204.8 3.0 %update.4 = (f32[48,1536]{1,0:T(8,128)}, f32[48,1536]{1,0:T(8,128)}, f32[48,1536]{1,0:T(8,128)}, f32[48,384]{1,0:T(8,128)}, f32[48,384]{1,0:T(8,128)}, /*index=5*/f32[48,384]{1,0:T(8,128)}, bf16[48,1920]{1,0:T(8,128)(2,1)}) custom-call(bf16[768,1920]{1,0:T(8,128)(2,1)} %get-tuple-element.165.refs_0_.refs_3_.refs_6_.refs_9_.refs_4_, ...), custom_call_target="tpu_custom_call" | custom-call | tf_op jit(solution)/shard_map/update/pallas_call | solution.py:810
  210.3 3.3 %put_other.2 = bf16[2048,768]{1,0:T(8,128)(2,1)} custom-call(s32[2]{0:T(128)} %pad_add_fusion.place.core.refs_0_, bf16[1024,768]{1,0:T(8,128)(2,1)} %collective-permute-done.13.refs_1_, bf16[2048,768]{1,0:T(8,128)(2,1)} %get-tuple-element.173.refs_2_, bf16[48,1920]{1,0:T(8,128)(2,1)} %get-tuple-element.207.refs_3_.refs_0_, ...), custom_call_target="tpu_custom_call", output_to_operand_aliasing={{}: (2, {})} | custom-call | flops 49999998976 | bytes 100000000 | tf_op jit(solution)/shard_map/put_other/pallas_call | solution.py:829
  231.9 3.9 %put_other.3 = f32[2048,768]{1,0:T(8,128)} custom-call(s32[2]{0:T(128)} %pad_add_fusion.place.core.refs_0_, bf16[1024,768]{1,0:T(8,128)(2,1)} %collective-permute-done.35.refs_1_, f32[2048,768]{1,0:T(8,128)} %get-tuple-element.220.refs_2_, bf16[96,1920]{1,0:T(8,128)(2,1)} %combine.32.refs_3_.refs_0_, ...), custom_call_target="tpu_custom_call", output_to_operand_aliasing={{}: (2, {})} | custom-call | flops 49999998976 | bytes 100000000 | tf_op jit(solution)/shard_map/put_other/pallas_call | solution.py:829
  243.0 3.1 %collective-permute-done.41.refs_1_ = bf16[96,1920]{1,0:T(8,128)(2,1)} collective-permute-done((bf16[96,1920]{1,0:T(8,128)(2,1)}, bf16[96,1920]{1,0:T(8,128)(2,1)}, u32[]{:S(2)}, u32[]{:S(2)}) %collective-permute-start.41) | collective-permute-done | bytes 368672 | tf_op jit(solution)/shard_map/ppermute | solution.py:850
  256.4 4.5 %gather_place.3 = bf16[1536,768]{1,0:T(8,128)(2,1)} custom-call(s32[2]{0:T(128)} %pad_add_fusion.place.core.refs_0_, bf16[192,1536]{1,0:T(8,128)(2,1)} %combine.28.refs_8_.refs_1_, bf16[192,1536]{1,0:T(8,128)(2,1)} %collective-permute-done.33.refs_0_.refs_2_, bf16[192,1536]{1,0:T(8,128)(2,1)} %collective-permute-done.34.refs_1_.refs_3_, ...), custom_call_target="tpu_custom_call" | custom-call | flops 49999998976 | bytes 100000000 | tf_op jit(solution)/shard_map/gather_place/pallas_call | solution.py:674
  275.7 4.6 %collective-permute-done.47.refs_1_.refs_3_ = bf16[576,384]{1,0:T(8,128)(2,1)} collective-permute-done((bf16[576,384]{1,0:T(8,128)(2,1)}, bf16[576,384]{1,0:T(8,128)(2,1)}, u32[]{:S(2)}, u32[]{:S(2)}) %collective-permute-start.47) | collective-permute-done | bytes 442400 | tf_op jit(solution)/shard_map/ppermute | solution.py:850
  286.1 4.3 %gather_place.4 = (bf16[768,1536]{1,0:T(8,128)(2,1)}, bf16[384,768]{1,0:T(8,128)(2,1)}) custom-call(s32[2]{0:T(128)} %pad_add_fusion.place.core.refs_0_, bf16[192,1920]{1,0:T(8,128)(2,1)} %combine.33.refs_7_.refs_1_, bf16[192,1920]{1,0:T(8,128)(2,1)} %collective-permute-done.48.refs_0_.refs_2_, bf16[192,1920]{1,0:T(8,128)(2,1)} %collective-permute-done.49.refs_1_.refs_3_, ...), custom_call_target="tpu_custom_call" | custom-call | flops 49999998976 | bytes 100000000 | tf_op jit(solution)/shard_map/gather_place/pallas_call | solution.py:674
  290.5 3.5 %gather_place.5 = bf16[3,768,384]{2,1,0:T(8,128)(2,1)} custom-call(s32[2]{0:T(128)} %pad_add_fusion.place.core.refs_0_, bf16[576,384]{1,0:T(8,128)(2,1)} %combine.35.refs_1_, bf16[576,384]{1,0:T(8,128)(2,1)} %collective-permute-done.46.refs_0_.refs_2_, bf16[576,384]{1,0:T(8,128)(2,1)} %collective-permute-done.47.refs_1_.refs_3_, ...), custom_call_target="tpu_custom_call" | custom-call | flops 49999998976 | bytes 100000000 | tf_op jit(solution)/shard_map/gather_place/pallas_call | solution.py:674
  (138 shorter events, 110.8 us)
Async XLA Ops:
  5.7 19.7 %collective-permute-start.5 = (f32[1,1536]{1,0:T(1,128)}, f32[1,1536]{1,0:T(1,128)}, u32[]{:S(2)}, u32[]{:S(2)}) collective-permute-start(f32[1,1536]{1,0:T(1,128)} %broadcast_in_dim.3.b0_ref), channel_id=1, source_target_pairs={{0,1},{1,0},{2,3},{3,2},{4,5},{5,4},{6,7},{7,6},{8,9},{9,8},{10,11... | collective-permute-start | bytes 18440 | tf_op jit(solution)/shard_map/ppermute | solution.py:846
  6.1 19.3 %collective-permute-start.3 = (bf16[768,1536]{1,0:T(8,128)(2,1)}, bf16[768,1536]{1,0:T(8,128)(2,1)}, u32[]{:S(2)}, u32[]{:S(2)}) collective-permute-start(bf16[768,1536]{1,0:T(8,128)(2,1)} %refs_3_.2), channel_id=1, source_target_pairs={{0,1},{1,0},{2,3},{3,2},{4,5},{5,4},{6,7},{7,6},{8,9},{9,8},{10,11... | collective-permute-start | bytes 7077896 | tf_op jit(solution)/shard_map/ppermute | solution.py:846
  6.2 19.2 %collective-permute-start.4 = (bf16[1536,768]{1,0:T(8,128)(2,1)}, bf16[1536,768]{1,0:T(8,128)(2,1)}, u32[]{:S(2)}, u32[]{:S(2)}) collective-permute-start(bf16[1536,768]{1,0:T(8,128)(2,1)} %refs_4_.1), channel_id=1, source_target_pairs={{0,1},{1,0},{2,3},{3,2},{4,5},{5,4},{6,7},{7,6},{8,9},{9,8},{10,11... | collective-permute-start | bytes 7077896 | tf_op jit(solution)/shard_map/ppermute | solution.py:846
  66.0 19.6 %collective-permute-start.7 = (bf16[192,1536]{1,0:T(8,128)(2,1)}, bf16[192,1536]{1,0:T(8,128)(2,1)}, u32[]{:S(2)}, u32[]{:S(2)}) collective-permute-start(bf16[192,1536]{1,0:T(8,128)(2,1)} %get-tuple-element.147.refs_10_), channel_id=1, source_target_pairs={{0,2},{2,0},{4,6},{6,4},{8,10},{10,8},{12,14},{14,12},{16,18},{18,... | collective-permute-start | bytes 1769480 | tf_op jit(solution)/shard_map/ppermute | solution.py:850
  68.9 16.7 %collective-permute-start.8 = (bf16[192,1536]{1,0:T(8,128)(2,1)}, bf16[192,1536]{1,0:T(8,128)(2,1)}, u32[]{:S(2)}, u32[]{:S(2)}) collective-permute-start(bf16[192,1536]{1,0:T(8,128)(2,1)} %get-tuple-element.148.refs_11_), channel_id=1, source_target_pairs={{0,4},{2,6},{4,0},{6,2},{8,12},{10,14},{12,8},{14,10},{16,20},{18,... | collective-permute-start | bytes 1769480 | tf_op jit(solution)/shard_map/ppermute | solution.py:850
  88.0 22.6 %collective-permute-start.9 = (bf16[96,1536]{1,0:T(8,128)(2,1)}, bf16[96,1536]{1,0:T(8,128)(2,1)}, u32[]{:S(2)}, u32[]{:S(2)}) collective-permute-start(bf16[96,1536]{1,0:T(8,128)(2,1)} %get-tuple-element.156.refs_10_), channel_id=1, source_target_pairs={{0,2},{2,0},{4,6},{6,4},{8,10},{10,8},{12,14},{14,12},{16,18},{18,... | collective-permute-start | bytes 884744 | tf_op jit(solution)/shard_map/ppermute | solution.py:850
  88.5 22.1 %collective-permute-start.10 = (bf16[96,1536]{1,0:T(8,128)(2,1)}, bf16[96,1536]{1,0:T(8,128)(2,1)}, u32[]{:S(2)}, u32[]{:S(2)}) collective-permute-start(bf16[96,1536]{1,0:T(8,128)(2,1)} %get-tuple-element.157.refs_11_), channel_id=1, source_target_pairs={{0,4},{2,6},{4,0},{6,2},{8,12},{10,14},{12,8},{14,10},{16,20},{18,... | collective-permute-start | bytes 884744 | tf_op jit(solution)/shard_map/ppermute | solution.py:850
  88.7 29.4 %collective-permute-start.11 = (bf16[768,1536]{1,0:T(8,128)(2,1)}, bf16[768,1536]{1,0:T(8,128)(2,1)}, u32[]{:S(2)}, u32[]{:S(2)}) collective-permute-start(bf16[768,1536]{1,0:T(8,128)(2,1)} %get-tuple-element.167), channel_id=1, source_target_pairs={{0,1},{1,0},{2,3},{3,2},{4,5},{5,4},{6,7},{7,6},{8,9},{9,8},{10,11... | collective-permute-start | bytes 7077896 | tf_op jit(solution)/shard_map/ppermute | solution.py:846
  113.5 27.5 %collective-permute-start.16 = (bf16[48,1536]{1,0:T(8,128)(2,1)}, bf16[48,1536]{1,0:T(8,128)(2,1)}, u32[]{:S(2)}, u32[]{:S(2)}) collective-permute-start(bf16[48,1536]{1,0:T(8,128)(2,1)} %get-tuple-element.162.refs_6_), channel_id=1, source_target_pairs={{0,16},{2,18},{4,20},{6,22},{8,24},{10,26},{12,28},{14,30},{16,0},... | collective-permute-start | bytes 442376 | tf_op jit(solution)/shard_map/ppermute | solution.py:850
  116.5 24.5 %collective-permute-start.17 = (bf16[48,1536]{1,0:T(8,128)(2,1)}, bf16[48,1536]{1,0:T(8,128)(2,1)}, u32[]{:S(2)}, u32[]{:S(2)}) collective-permute-start(bf16[48,1536]{1,0:T(8,128)(2,1)} %get-tuple-element.163.refs_7_), channel_id=1, source_target_pairs={{0,8},{2,10},{4,12},{6,14},{8,0},{10,2},{12,4},{14,6},{16,24},{18,... | collective-permute-start | bytes 442376 | tf_op jit(solution)/shard_map/ppermute | solution.py:850
  118.1 22.9 %collective-permute-start.18 = (bf16[48,1536]{1,0:T(8,128)(2,1)}, bf16[48,1536]{1,0:T(8,128)(2,1)}, u32[]{:S(2)}, u32[]{:S(2)}) collective-permute-start(bf16[48,1536]{1,0:T(8,128)(2,1)} %get-tuple-element.164.refs_8_), channel_id=1, source_target_pairs={{0,24},{2,26},{4,28},{6,30},{8,16},{10,18},{12,20},{14,22},{16,8},... | collective-permute-start | bytes 442376 | tf_op jit(solution)/shard_map/ppermute | solution.py:850
  121.1 26.1 %collective-permute-start.14 = (bf16[192,1920]{1,0:T(8,128)(2,1)}, bf16[192,1920]{1,0:T(8,128)(2,1)}, u32[]{:S(2)}, u32[]{:S(2)}) collective-permute-start(bf16[192,1920]{1,0:T(8,128)(2,1)} %get-tuple-element.170.refs_9_), channel_id=1, source_target_pairs={{0,2},{2,0},{4,6},{6,4},{8,10},{10,8},{12,14},{14,12},{16,18},{18,... | collective-permute-start | bytes 2211848 | tf_op jit(solution)/shard_map/ppermute | solution.py:850
  122.8 24.4 %collective-permute-start.15 = (bf16[192,1920]{1,0:T(8,128)(2,1)}, bf16[192,1920]{1,0:T(8,128)(2,1)}, u32[]{:S(2)}, u32[]{:S(2)}) collective-permute-start(bf16[192,1920]{1,0:T(8,128)(2,1)} %get-tuple-element.171.refs_10_), channel_id=1, source_target_pairs={{0,4},{2,6},{4,0},{6,2},{8,12},{10,14},{12,8},{14,10},{16,20},{18,... | collective-permute-start | bytes 2211848 | tf_op jit(solution)/shard_map/ppermute | solution.py:850
  142.5 16.3 %collective-permute-start.22 = (f32[24,768]{1,0:T(8,128)}, f32[24,768]{1,0:T(8,128)}, u32[]{:S(2)}, u32[]{:S(2)}) collective-permute-start(f32[24,768]{1,0:T(8,128)} %get-tuple-element.189.refs_6_), channel_id=1, source_target_pairs={{0,1},{1,0},{2,3},{3,2},{4,5},{5,4},{6,7},{7,6},{8,9},{9,8},{10,11... | collective-permute-start | bytes 221192 | tf_op jit(solution)/shard_map/ppermute | solution.py:846
  147.0 60.8 %collective-permute-start.13 = (bf16[1024,768]{1,0:T(8,128)(2,1)}, bf16[1024,768]{1,0:T(8,128)(2,1)}, u32[]{:S(2)}, u32[]{:S(2)}) collective-permute-start(bf16[1024,768]{1,0:T(8,128)(2,1)} %get-tuple-element.172), channel_id=1, source_target_pairs={{0,1},{1,0},{2,3},{3,2},{4,5},{5,4},{6,7},{7,6},{8,9},{9,8},{10,11... | collective-permute-start | bytes 4718600 | tf_op jit(solution)/shard_map/ppermute | solution.py:846
  160.3 40.9 %collective-permute-start.29 = (f32[24,768]{1,0:T(8,128)}, f32[24,768]{1,0:T(8,128)}, u32[]{:S(2)}, u32[]{:S(2)}) collective-permute-start(f32[24,768]{1,0:T(8,128)} %add.60.refs_4_), channel_id=1, source_target_pairs={{0,2},{2,0},{4,6},{6,4},{8,10},{10,8},{12,14},{14,12},{16,18},{18,... | collective-permute-start | bytes 221192 | tf_op jit(solution)/shard_map/ppermute | solution.py:850
  166.5 15.1 %collective-permute-start.25 = (bf16[768,1152]{1,0:T(8,128)(2,1)}, bf16[768,1152]{1,0:T(8,128)(2,1)}, u32[]{:S(2)}, u32[]{:S(2)}) collective-permute-start(bf16[768,1152]{1,0:T(8,128)(2,1)} %weight_grad.6), channel_id=1, source_target_pairs={{0,1},{1,0},{2,3},{3,2},{4,5},{5,4},{6,7},{7,6},{8,9},{9,8},{10,11... | collective-permute-start | bytes 5308424 | tf_op jit(solution)/shard_map/ppermute | solution.py:846
  181.2 21.9 %collective-permute-start.24 = (bf16[48,1920]{1,0:T(8,128)(2,1)}, bf16[48,1920]{1,0:T(8,128)(2,1)}, u32[]{:S(2)}, u32[]{:S(2)}) collective-permute-start(bf16[48,1920]{1,0:T(8,128)(2,1)} %combine.26.refs_7_), channel_id=1, source_target_pairs={{0,16},{2,18},{4,20},{6,22},{8,24},{10,26},{12,28},{14,30},{16,0},... | collective-permute-start | bytes 552968 | tf_op jit(solution)/shard_map/ppermute | solution.py:850
  196.9 16.7 %collective-permute-start.34 = (bf16[192,1536]{1,0:T(8,128)(2,1)}, bf16[192,1536]{1,0:T(8,128)(2,1)}, u32[]{:S(2)}, u32[]{:S(2)}) collective-permute-start(bf16[192,1536]{1,0:T(8,128)(2,1)} %combine.28.refs_8_.refs_1_), channel_id=1, source_target_pairs={{0,4},{2,6},{4,0},{6,2},{8,12},{10,14},{12,8},{14,10},{16,20},{18,... | collective-permute-start | bytes 1769480 | tf_op jit(solution)/shard_map/ppermute | solution.py:850
  197.2 16.4 %collective-permute-start.33 = (bf16[192,1536]{1,0:T(8,128)(2,1)}, bf16[192,1536]{1,0:T(8,128)(2,1)}, u32[]{:S(2)}, u32[]{:S(2)}) collective-permute-start(bf16[192,1536]{1,0:T(8,128)(2,1)} %combine.28.refs_8_.refs_1_), channel_id=1, source_target_pairs={{0,2},{2,0},{4,6},{6,4},{8,10},{10,8},{12,14},{14,12},{16,18},{18,... | collective-permute-start | bytes 1769480 | tf_op jit(solution)/shard_map/ppermute | solution.py:850
  223.4 30.7 %collective-permute-start.43 = (bf16[96,1536]{1,0:T(8,128)(2,1)}, bf16[96,1536]{1,0:T(8,128)(2,1)}, u32[]{:S(2)}, u32[]{:S(2)}) collective-permute-start(bf16[96,1536]{1,0:T(8,128)(2,1)} %get-tuple-element.211), channel_id=1, source_target_pairs={{0,4},{2,6},{4,0},{6,2},{8,12},{10,14},{12,8},{14,10},{16,20},{18,... | collective-permute-start | bytes 884744 | tf_op jit(solution)/shard_map/ppermute | solution.py:850
  223.9 32.5 %collective-permute-start.44 = (bf16[96,1536]{1,0:T(8,128)(2,1)}, bf16[96,1536]{1,0:T(8,128)(2,1)}, u32[]{:S(2)}, u32[]{:S(2)}) collective-permute-start(bf16[96,1536]{1,0:T(8,128)(2,1)} %get-tuple-element.212), channel_id=1, source_target_pairs={{0,2},{2,0},{4,6},{6,4},{8,10},{10,8},{12,14},{14,12},{16,18},{18,... | collective-permute-start | bytes 884744 | tf_op jit(solution)/shard_map/ppermute | solution.py:850
  248.1 19.7 %collective-permute-start.49 = (bf16[192,1920]{1,0:T(8,128)(2,1)}, bf16[192,1920]{1,0:T(8,128)(2,1)}, u32[]{:S(2)}, u32[]{:S(2)}) collective-permute-start(bf16[192,1920]{1,0:T(8,128)(2,1)} %combine.33.refs_7_.refs_1_), channel_id=1, source_target_pairs={{0,4},{2,6},{4,0},{6,2},{8,12},{10,14},{12,8},{14,10},{16,20},{18,... | collective-permute-start | bytes 2211848 | tf_op jit(solution)/shard_map/ppermute | solution.py:850
  249.3 18.6 %collective-permute-start.48 = (bf16[192,1920]{1,0:T(8,128)(2,1)}, bf16[192,1920]{1,0:T(8,128)(2,1)}, u32[]{:S(2)}, u32[]{:S(2)}) collective-permute-start(bf16[192,1920]{1,0:T(8,128)(2,1)} %combine.33.refs_7_.refs_1_), channel_id=1, source_target_pairs={{0,2},{2,0},{4,6},{6,4},{8,10},{10,8},{12,14},{14,12},{16,18},{18,... | collective-permute-start | bytes 2211848 | tf_op jit(solution)/shard_map/ppermute | solution.py:850
  (31 other events, 321.4 us)
